TPU v7x, 256 devices: a whole 4x4x8 slice. The times are simulated.
256 devices in a mesh: seq: 128 (over y_hi, x, z, core), ch: 2 (over y_lo).
Axes of the slice: x: 4, y: 4 (y_hi: 2, y_lo: 2; y = y_hi * 2 + y_lo), z: 8, core: 2. Of those that a mesh axis runs over, the one named last changes fastest.
Arguments:
- gated: bfloat16 [4096, 16384], P('ch', 'seq'), may hold values from -6 to 6
- value: bfloat16 [4096, 16384], P('ch', 'seq'), may hold values from -6 to 6
- upstream: bfloat16 [4096, 16384], P('ch', 'seq'), may hold values from -6 to 6
- residue: float32 [4096, 16], replicated, may hold values from -0.078125 to 0.078125
- rate: float32 [4096, 16], replicated, may hold values from 3.0517578e-06 to 0.0333333333
- skip_weight: float32 [4096], replicated, may hold values from -6 to 6
Outputs:
- grad_gated: bfloat16 [4096, 16384], P('ch', 'seq')
- grad_value: bfloat16 [4096, 16384], P('ch', 'seq')
- grad_residue: float32 [4096, 16], replicated
All inputs are finite; a program needn't handle non-finite values.
Results may differ from a plain program's by a relative error of at most 0.0051.
Values may be sent and summed in bfloat16 or wider, within the bound.
No kernel may reach another device: no remote copies, remote signals or barrier semaphores. Data moves between devices by JAX's collectives and lax.ppermute only.
A program may use at most 128 MiB of HBM per device.

v0:
```python
import math

import jax
import jax.numpy as jnp
from jax import lax
from jax.sharding import PartitionSpec as P


def matmul_high(form, left, right):
    return jnp.einsum(form, left, right, precision=lax.Precision.HIGHEST)


def dft_tables(width_a, count_b):
    total_len = width_a * count_b
    freq_rows = jnp.arange(count_b, dtype=jnp.int32)
    half_rows = jnp.arange(count_b // 2, dtype=jnp.int32)
    phase_idx = freq_rows[:, None] * half_rows[None, :] % count_b
    angle_b = 2.0 * math.pi / count_b * phase_idx.astype(jnp.float32)
    pos_cols = jnp.arange(width_a, dtype=jnp.int32)
    twist_idx = freq_rows[:, None] * pos_cols[None, :] % total_len
    angle_t = 2.0 * math.pi / total_len * twist_idx.astype(jnp.float32)
    inner_idx = pos_cols[:, None] * pos_cols[None, :] % width_a
    angle_a = 2.0 * math.pi / width_a * inner_idx.astype(jnp.float32)
    return (
        jnp.cos(angle_b),
        jnp.sin(angle_b),
        jnp.cos(angle_t),
        jnp.sin(angle_t),
        jnp.cos(angle_a),
        jnp.sin(angle_a),
    )


def forward_dft(signal, tables):
    cos_b, sin_b, cos_t, sin_t, cos_a, sin_a = tables
    channels = signal.shape[0]
    planes = signal.reshape(channels, -1, cos_a.shape[0])
    real_one = matmul_high("cba,kb->cka", planes, cos_b)
    imag_one = -matmul_high("cba,kb->cka", planes, sin_b)
    real_two = real_one * cos_t + imag_one * sin_t
    imag_two = imag_one * cos_t - real_one * sin_t
    real_three = matmul_high("cka,ja->ckj", real_two, cos_a) + matmul_high(
        "cka,ja->ckj", imag_two, sin_a
    )
    imag_three = matmul_high("cka,ja->ckj", imag_two, cos_a) - matmul_high(
        "cka,ja->ckj", real_two, sin_a
    )
    return (real_three, imag_three)


def inverse_dft(real_in, imag_in, tables):
    cos_b, sin_b, cos_t, sin_t, cos_a, sin_a = tables
    channels = real_in.shape[0]
    total_len = cos_t.shape[0] * cos_t.shape[1]
    real_one = matmul_high("ckj,ja->cka", real_in, cos_a) - matmul_high(
        "ckj,ja->cka", imag_in, sin_a
    )
    imag_one = matmul_high("ckj,ja->cka", real_in, sin_a) + matmul_high(
        "ckj,ja->cka", imag_in, cos_a
    )
    real_two = real_one * cos_t - imag_one * sin_t
    imag_two = real_one * sin_t + imag_one * cos_t
    result = matmul_high("cka,kb->cba", real_two, cos_b) - matmul_high(
        "cka,kb->cba", imag_two, sin_b
    )
    return result.reshape(channels, -1) / total_len


def spectral_mul(left_re, left_im, right_re, right_im):
    return (left_re * right_re - left_im * right_im, left_re * right_im + left_im * right_re)


def spectral_conj(left_re, left_im, right_re, right_im):
    return (left_re * right_re + left_im * right_im, left_re * right_im - left_im * right_re)


def filter_core(gated_b, grad_b, res_b, rate_b, skip_b, tables):
    length = gated_b.shape[1]
    positions = jnp.arange(length).astype(jnp.float32)
    basis = jnp.exp(-rate_b[:, :, None] * positions[None, None, :])
    filter_taps = matmul_high("cm,cml->cl", res_b, basis)
    gated_f = gated_b.astype(jnp.float32)
    grad_f = grad_b.astype(jnp.float32)
    gated_re, gated_im = forward_dft(gated_f, tables)
    taps_re, taps_im = forward_dft(filter_taps, tables)
    grad_re, grad_im = forward_dft(grad_f, tables)
    conv = inverse_dft(*spectral_mul(taps_re, taps_im, gated_re, gated_im), tables)
    forward_out = (conv + skip_b[:, None] * gated_f).astype(jnp.bfloat16)
    back = inverse_dft(*spectral_conj(taps_re, taps_im, grad_re, grad_im), tables)
    grad_gated = (back + skip_b[:, None] * grad_f).astype(jnp.bfloat16)
    dfilter = inverse_dft(*spectral_conj(gated_re, gated_im, grad_re, grad_im), tables)
    grad_res = matmul_high("cl,cml->cm", dfilter, basis) / length
    return (forward_out, grad_gated, grad_res)


def apply_blocks(gated_cols, grad_cols, res_local, rate_local, skip_local, tables):
    per_dev = gated_cols.shape[0]
    block_size = math.gcd(per_dev, 4)
    block_count = per_dev // block_size

    def blocked(array):
        return array.reshape((block_count, block_size) + array.shape[1:])

    def step_fn(items):
        return filter_core(items[0], items[1], items[2], items[3], items[4], tables)

    results = lax.map(
        step_fn,
        (
            blocked(gated_cols),
            blocked(grad_cols),
            blocked(res_local),
            blocked(rate_local),
            blocked(skip_local),
        ),
    )
    return tuple((piece.reshape((per_dev,) + piece.shape[2:]) for piece in results))


def local(gated, value, upstream, residue, rate, skip_weight):
    rows_ch, tok_dev = gated.shape
    per_dev = rows_ch // lax.axis_size("seq")
    offset = lax.axis_index("ch") * rows_ch + lax.axis_index("seq") * per_dev
    res_local = lax.dynamic_slice_in_dim(residue, offset, per_dev, 0)
    rate_local = lax.dynamic_slice_in_dim(rate, offset, per_dev, 0)
    skip_local = lax.dynamic_slice_in_dim(skip_weight, offset, per_dev, 0)
    tables = dft_tables(tok_dev, 2 * lax.axis_size("seq"))
    gated_cols, value_cols, upstream_cols = (
        lax.all_to_all(gated, "seq", split_axis=0, concat_axis=1, tiled=True),
        lax.all_to_all(value, "seq", split_axis=0, concat_axis=1, tiled=True),
        lax.all_to_all(upstream, "seq", split_axis=0, concat_axis=1, tiled=True),
    )
    grad_cols = (upstream_cols.astype(jnp.float32) * value_cols.astype(jnp.float32)).astype(
        jnp.bfloat16
    )
    grad_cols = lax.optimization_barrier(grad_cols)
    forward_out, grad_gated, grad_res = apply_blocks(
        gated_cols, grad_cols, res_local, rate_local, skip_local, tables
    )
    forward_f = lax.optimization_barrier(forward_out).astype(jnp.float32)
    value_grad = (upstream_cols.astype(jnp.float32) * forward_f).astype(jnp.bfloat16)
    grad_tok, grad_value = (
        lax.all_to_all(grad_gated, "seq", split_axis=1, concat_axis=0, tiled=True),
        lax.all_to_all(value_grad, "seq", split_axis=1, concat_axis=0, tiled=True),
    )
    gathered = lax.all_gather(grad_res, "seq", axis=0, tiled=True)
    full_res = lax.all_gather(gathered, "ch", axis=0, tiled=True)
    return (grad_tok, grad_value, full_res)


def solution(mesh):
    return jax.shard_map(
        local,
        mesh=mesh,
        in_specs=(P("ch", "seq"), P("ch", "seq"), P("ch", "seq"), P(), P(), P()),
        out_specs=(P("ch", "seq"), P("ch", "seq"), P()),
        check_vma=False,
    )
```

profile of v0, /device:TPU:1, one launch (start us, length us, event | category | flops | bytes accessed | tf_op | source)
XLA Modules:
  0.0 551.8 jit_solution(2886099253650566622)
XLA Ops:
  0.6 36.4 %all_to_all.80 = bf16[128,16,128]{2,1,0:T(8,128)(2,1)S(1)} all-to-all(bf16[128,16,128]{2,1,0:T(8,128)(2,1)} %bitcast.340), channel_id=1, replica_groups=mesh['seq'=128,'ch'=2] {'seq'}, dimensions={0} | all-to-all | bytes 1048576 | tf_op jit(solution)/shard_map/all_to_all | solution.py:131
  37.0 6.8 %all-to-all-start.2 = ((bf16[128,16,128]{2,1,0:T(8,128)(2,1)}), bf16[128,16,128]{2,1,0:T(8,128)(2,1)S(1)}, u32[]{:S(2)}, u32[]{:S(2)}) async-start(bf16[128,16,128]{2,1,0:T(8,128)(2,1)} %bitcast.341), calls=%async_computation.2 | async-start | bytes 1048576 | tf_op jit(solution)/shard_map/all_to_all | solution.py:130
  45.7 18.1 %all-to-all-done.2 = bf16[128,16,128]{2,1,0:T(8,128)(2,1)S(1)} async-done(((bf16[128,16,128]{2,1,0:T(8,128)(2,1)}), bf16[128,16,128]{2,1,0:T(8,128)(2,1)S(1)}, u32[]{:S(2)}, u32[]{:S(2)}) %all-to-all-start.2) | async-done | bytes 524320 | tf_op jit(solution)/shard_map/all_to_all | solution.py:130
  63.8 6.8 %all-to-all-start = ((bf16[128,16,128]{2,1,0:T(8,128)(2,1)}), bf16[128,16,128]{2,1,0:T(8,128)(2,1)S(1)}, u32[]{:S(2)}, u32[]{:S(2)}) async-start(bf16[128,16,128]{2,1,0:T(8,128)(2,1)} %bitcast.2), calls=%async_computation | async-start | bytes 1048576 | tf_op jit(solution)/shard_map/all_to_all | solution.py:129
  71.0 19.6 %all-to-all-done = bf16[128,16,128]{2,1,0:T(8,128)(2,1)S(1)} async-done(((bf16[128,16,128]{2,1,0:T(8,128)(2,1)}), bf16[128,16,128]{2,1,0:T(8,128)(2,1)S(1)}, u32[]{:S(2)}, u32[]{:S(2)}) %all-to-all-start) | async-done | bytes 524320 | tf_op jit(solution)/shard_map/all_to_all | solution.py:129
  91.7 206.3 %while.16 = (s32[]{:T(128)}, bf16[4,4,16384]{2,1,0:T(4,128)(2,1)}, bf16[4,4,16384]{2,1,0:T(4,128)(2,1)}, f32[4,4,16]{2,1,0:T(4,128)S(1)}, f32[4,4,16]{2,1,0:T(4,...) while((s32[]{:T(128)}, bf16[4,4,16384]{2,1,0:T(4,128)(2,1)}, ...), condition=%wide.region_1.2_spmd.clone.clone, body=%wide.region_0.1_spmd.clone.clone.sunk | while | flops 7298826240 | bytes 66263720 | solution.py:107
  92.2 2.6 fusion.499
  115.7 1.6 multiply_subtract_fusion.25
  123.1 4.9 fusion.518
  129.8 1.3 fusion.509
  140.4 1.8 fusion.513
  142.4 2.6 fusion.499
  165.9 1.8 multiply_subtract_fusion.25
  173.5 4.9 fusion.518
  190.5 1.8 fusion.513
  192.5 2.6 fusion.499
  204.7 1.3 fusion.493
  216.2 1.5 multiply_subtract_fusion.25
  223.6 4.9 fusion.518
  240.6 1.8 fusion.513
  242.9 2.6 fusion.499
  266.3 1.6 multiply_subtract_fusion.25
  273.8 4.9 fusion.518
  280.4 1.3 fusion.509
  291.0 1.8 fusion.513
  299.3 2.0 copy_bitcast_fusion.1
  301.3 6.8 %all-to-all-start.4 = ((bf16[16,128,128]{2,0,1:T(8,128)(2,1)}), bf16[16,128,128]{2,0,1:T(8,128)(2,1)S(1)}, u32[]{:S(2)}, u32[]{:S(2)}) async-start(bf16[16,128,128]{2,0,1:T(8,128)(2,1)} %copy_bitcast_fusion.1), calls=%async_computation.4 | async-start | bytes 1048576 | tf_op jit(solution)/shard_map/all_to_all | solution.py:144
  309.8 18.3 %all-to-all-done.4 = bf16[16,128,128]{2,0,1:T(8,128)(2,1)S(1)} async-done(((bf16[16,128,128]{2,0,1:T(8,128)(2,1)}), bf16[16,128,128]{2,0,1:T(8,128)(2,1)S(1)}, u32[]{:S(2)}, u32[]{:S(2)}) %all-to-all-start.4) | async-done | bytes 524320 | tf_op jit(solution)/shard_map/all_to_all | solution.py:144
  328.1 6.8 %all-to-all-start.3 = ((bf16[16,128,128]{2,0,1:T(8,128)(2,1)}), bf16[16,128,128]{2,0,1:T(8,128)(2,1)S(1)}, u32[]{:S(2)}, u32[]{:S(2)}) async-start(bf16[16,128,128]{2,0,1:T(8,128)(2,1)} %copy.199), calls=%async_computation.3 | async-start | bytes 1048576 | tf_op jit(solution)/shard_map/all_to_all | solution.py:143
  334.9 188.5 %all_gather.6 = f32[2048,16]{1,0:T(8,128)S(1)} all-gather(f32[16,16]{1,0:T(8,128)S(1)} %bitcast.346), channel_id=1, replica_groups=mesh['seq'=128,'ch'=2] {'seq'}, dimensions={0}, use_global_device_ids=true | all-gather | bytes 132096 | tf_op jit(solution)/shard_map/all_gather | solution.py:146
  523.4 25.3 %all_gather.7 = f32[4096,16]{1,0:T(8,128)S(1)} all-gather(f32[2048,16]{1,0:T(8,128)S(1)} %all_gather.6), channel_id=1, replica_groups=mesh['seq'=128,'ch'=2] {'ch'}, dimensions={0}, use_global_device_ids=true | all-gather | bytes 393216 | tf_op jit(solution)/shard_map/all_gather | solution.py:147
  548.7 1.3 copy.201
  (211 shorter events, 158.8 us)
Async XLA Ops:
  37.0 33.7 %copy-start = (bf16[128,16,128]{2,1,0:T(8,128)(2,1)}, bf16[128,16,128]{2,1,0:T(8,128)(2,1)S(1)}, u32[]{:S(2)}) copy-start(bf16[128,16,128]{2,1,0:T(8,128)(2,1)S(1)} %all_to_all.80) | copy-start | bytes 1572868
  37.0 26.8 %all-to-all-start.2 = ((bf16[128,16,128]{2,1,0:T(8,128)(2,1)}), bf16[128,16,128]{2,1,0:T(8,128)(2,1)S(1)}, u32[]{:S(2)}, u32[]{:S(2)}) async-start(bf16[128,16,128]{2,1,0:T(8,128)(2,1)} %bitcast.341), calls=%async_computation.2 | async-start | bytes 1048576 | tf_op jit(solution)/shard_map/all_to_all | solution.py:130
  63.8 26.8 %all-to-all-start = ((bf16[128,16,128]{2,1,0:T(8,128)(2,1)}), bf16[128,16,128]{2,1,0:T(8,128)(2,1)S(1)}, u32[]{:S(2)}, u32[]{:S(2)}) async-start(bf16[128,16,128]{2,1,0:T(8,128)(2,1)} %bitcast.2), calls=%async_computation | async-start | bytes 1048576 | tf_op jit(solution)/shard_map/all_to_all | solution.py:129
  298.1 10.1 %copy-start.1 = (bf16[4,4,16384]{2,1,0:T(4,128)(2,1)S(1)}, bf16[4,4,16384]{2,1,0:T(4,128)(2,1)}, u32[]{:S(2)}) copy-start(bf16[4,4,16384]{2,1,0:T(4,128)(2,1)} %get-tuple-element.175) | copy-start | bytes 1572868
  301.3 26.8 %all-to-all-start.4 = ((bf16[16,128,128]{2,0,1:T(8,128)(2,1)}), bf16[16,128,128]{2,0,1:T(8,128)(2,1)S(1)}, u32[]{:S(2)}, u32[]{:S(2)}) async-start(bf16[16,128,128]{2,0,1:T(8,128)(2,1)} %copy_bitcast_fusion.1), calls=%async_computation.4 | async-start | bytes 1048576 | tf_op jit(solution)/shard_map/all_to_all | solution.py:144
  328.1 221.9 %all-to-all-start.3 = ((bf16[16,128,128]{2,0,1:T(8,128)(2,1)}), bf16[16,128,128]{2,0,1:T(8,128)(2,1)S(1)}, u32[]{:S(2)}, u32[]{:S(2)}) async-start(bf16[16,128,128]{2,0,1:T(8,128)(2,1)} %copy.199), calls=%async_computation.3 | async-start | bytes 1048576 | tf_op jit(solution)/shard_map/all_to_all | solution.py:143
where the time goes:
time: 558 us; the launch traced here: 552 us
  blocking collectives  250 us (45%)
  matrix products  182 us (33%)
  waiting for transfers between devices  56.1 us (10%)
  starting transfers between devices  27.3 us (5%)
  local copies, waits for them, and re-layouts  16 us (3%)
  other arithmetic  11.6 us (2%)
  loops' own time  7.84 us (1%)
    all_gather x1, blocking collectives, local(): gathered = lax.all_gather(grad_res, 'seq', axis=0, tiled=True)  189 us
    dot_general x152, matrix products, matmul_high(): return jnp.einsum(form, left, right, precision=lax.Precision.HIGHEST)  182 us
    all_to_all x1, blocking collectives, local(): lax.all_to_all(upstream, 'seq', split_axis=0, concat_axis=1, tiled=True)  36.4 us
    all_gather x1, blocking collectives, local(): full_res = lax.all_gather(gathered, 'ch', axis=0, tiled=True)  25.3 us
    all_to_all x1, waiting for transfers between devices, local(): lax.all_to_all(gated, 'seq', split_axis=0, concat_axis=1, tiled=True)  19.6 us
    all_to_all x1, waiting for transfers between devices, local(): lax.all_to_all(value_grad, 'seq', split_axis=1, concat_axis=0, tiled=True)  18.3 us
    all_to_all x1, waiting for transfers between devices, local(): lax.all_to_all(value, 'seq', split_axis=0, concat_axis=1, tiled=True)  18.1 us
  transfers between devices with their start and end apart: 4, of which 3 were waited for; matrix products, arithmetic and copies ran while one was open for 1% of the time, Pallas kernels for 0%

commit v1 on v0

v1 whole, which is shorter than its diff:
```python
import functools

import jax
import jax.numpy as jnp
from jax import lax
from jax.experimental import pallas as pl
from jax.experimental.pallas import tpu as pltpu
from jax.sharding import PartitionSpec as P

F32 = jnp.float32
BF16 = jnp.bfloat16
LANES = 128
GROUP = 8
PART, UNROLL = 8, 16
LIMIT = 56 * 2**20


def transposed(block):
    return block.astype(F32).T


def spread_modes(src_ref, dst_ref, first, modes, blocks):
    for b in range(blocks):
        start = pl.multiple_of(first + b * LANES, LANES)
        dst_ref[pl.ds(b, modes, stride=blocks), :] = src_ref[:, pl.ds(start, LANES)]


def load_signals(gated_ref, value_ref, upstream_ref, gt, dzt, which, blocks, tokens):
    for b in which:
        rows = pl.ds(b * LANES, LANES)
        dz = upstream_ref[rows, :].astype(F32) * value_ref[rows, :].astype(F32)
        gt[pl.ds(b, tokens, stride=blocks), :] = transposed(gated_ref[rows, :])
        dzt[pl.ds(b, tokens, stride=blocks), :] = transposed(dz.astype(BF16))


def rows_of(ref, index, blocks, g):
    return ref[pl.ds(pl.multiple_of(index * blocks + g * GROUP, GROUP), GROUP), :]


def state_kernel(
    modes, blocks, tokens, gated_hbm, value_hbm, upstream_hbm, rate_hbm, out_ref,
    gated_ref, value_ref, upstream_ref, rate_ref, gt, dzt, lam, pack, sems
):
    half = GROUP * LANES
    groups = blocks // GROUP
    start = pl.multiple_of(lax.axis_index("ch") * (blocks * LANES), LANES)
    rate_copy = pltpu.make_async_copy(
        rate_hbm.at[:, pl.ds(start, blocks * LANES)], rate_ref, sems.at[3 * groups]
    )
    copies = []
    for g in range(groups):
        rows = pl.ds(g * half, half)
        pairs = ((gated_hbm, gated_ref), (upstream_hbm, upstream_ref), (value_hbm, value_ref))
        copies.append(
            [
                pltpu.make_async_copy(src.at[rows, :], dst.at[rows, :], sems.at[3 * g + k])
                for k, (src, dst) in enumerate(pairs)
            ]
        )
    for copy in copies[0] + [rate_copy] + [copy for part in copies[1:] for copy in part]:
        copy.start()
    unroll = UNROLL
    zero = jnp.zeros((GROUP, LANES), F32)
    for g in range(groups):
        for copy in copies[g]:
            copy.wait()
        which = range(g * GROUP, (g + 1) * GROUP)
        load_signals(gated_ref, value_ref, upstream_ref, gt, dzt, which, blocks, tokens)
        if g == 0:
            rate_copy.wait()
            spread_modes(rate_ref, lam, 0, modes, blocks)
        for m0 in range(0, modes, PART):
            decay = [jnp.exp(-rows_of(lam, m, blocks, g)) for m in range(m0, m0 + PART)]

            def body(i, carry, g=g, decay=decay):
                x, y, own = carry
                for u in range(unroll):
                    t = i * unroll + u
                    gv = rows_of(gt, t, blocks, g)
                    dv = rows_of(dzt, t, blocks, g)
                    rv = rows_of(dzt, tokens - 1 - t, blocks, g)
                    x = [a * v + gv for a, v in zip(decay, x)]
                    own = [o + dv * v for o, v in zip(own, x)]
                    y = [a * v + rv for a, v in zip(decay, y)]
                return x, y, own

            zeros = [zero] * PART
            x, y, own = lax.fori_loop(0, tokens // unroll, body, (zeros, zeros, zeros))
            for k in range(PART):
                base = ((m0 + k) * blocks + g * GROUP) * 4
                high = own[k].astype(BF16).astype(F32)
                for kind, rows in enumerate((x[k], y[k], high, own[k] - high)):
                    pack[pl.ds(base + kind, GROUP, stride=4), :] = rows
    out_ref[...] = pack[...].astype(BF16)


def rate_kernel(modes, blocks, rate_ref, lam_ref, lam):
    spread_modes(rate_ref, lam, lax.axis_index("ch") * (blocks * LANES), modes, blocks)
    for h in range(2):
        own = lam[pl.ds(lax.axis_index("seq") * 2 + h, 1), :]
        lam_ref[pl.ds(4 * h, 4), :] = jnp.broadcast_to(own, (4, LANES))


def own_kernel(
    modes, blocks, tokens, gated_ref, value_ref, upstream_ref, rate_ref, res_ref, skip_ref,
    fwd_ref, bwd_ref, dec_ref, gain_ref, gt, dzt
):
    first = lax.axis_index("ch") * (blocks * LANES)
    spread_modes(rate_ref, dec_ref, first, modes, blocks)
    spread_modes(res_ref, gain_ref, first, modes, blocks)
    load_signals(gated_ref, value_ref, upstream_ref, gt, dzt, range(blocks), blocks, tokens)
    dec_ref[...] = jnp.exp(-dec_ref[...])
    part, unroll = PART, UNROLL
    zero = jnp.zeros((GROUP, LANES), F32)
    for g in range(blocks // GROUP):
        skip = jnp.concatenate(
            [
                skip_ref[:, pl.ds(pl.multiple_of(first + (g * GROUP + j) * LANES, LANES), LANES)]
                for j in range(GROUP)
            ],
            axis=0,
        )
        for m0 in range(0, modes, part):
            decay = [rows_of(dec_ref, m, blocks, g) for m in range(m0, m0 + part)]
            gain = [rows_of(gain_ref, m, blocks, g) for m in range(m0, m0 + part)]

            def body(i, carry, g=g, m0=m0, decay=decay, gain=gain, skip=skip):
                x, y = carry
                for u in range(unroll):
                    t = i * unroll + u
                    s = tokens - 1 - t
                    gv = rows_of(gt, t, blocks, g)
                    dv = rows_of(dzt, s, blocks, g)
                    x = [a * v + gv for a, v in zip(decay, x)]
                    y = [a * v + dv for a, v in zip(decay, y)]
                    fwd = rows_of(fwd_ref, t, blocks, g) if m0 else skip * gv
                    bwd = rows_of(bwd_ref, s, blocks, g) if m0 else skip * dv
                    fwd = total([r * v for r, v in zip(gain, x)] + [fwd])
                    bwd = total([r * v for r, v in zip(gain, y)] + [bwd])
                    fwd_ref[pl.ds(pl.multiple_of(t * blocks + g * GROUP, GROUP), GROUP), :] = fwd
                    bwd_ref[pl.ds(pl.multiple_of(s * blocks + g * GROUP, GROUP), GROUP), :] = bwd
                return x, y

            zeros = [zero] * part
            lax.fori_loop(0, tokens // unroll, body, (zeros, zeros))


def total(terms):
    while len(terms) > 1:
        pairs = [a + b for a, b in zip(terms[::2], terms[1::2])]
        terms = pairs + ([terms[-1]] if len(terms) % 2 else [])
    return terms[0]


def scan_kernel(chunks, tokens, in_ref, lam_ref, out_ref, tiles, ahead, behind):
    tiles[...] = in_ref[...].astype(F32)
    lam = lam_ref[...]
    step = jnp.exp(lam * (-1.0 * tokens))
    kind = lax.broadcasted_iota(jnp.int32, (GROUP, LANES), 0) % 4
    unroll = 8
    zero = jnp.zeros((GROUP, LANES), F32)

    def tile_at(d):
        return pl.ds(pl.multiple_of(d * GROUP, GROUP), GROUP)

    def body(i, carry):
        fwd, bwd, own, cross = carry
        for u in range(unroll):
            d = i * unroll + u
            e = chunks - 1 - d
            here, there = tiles[tile_at(d), :], tiles[tile_at(e), :]
            ahead[tile_at(d), :] = fwd
            behind[tile_at(e), :] = bwd
            own = own + here
            cross = cross + here * pltpu.roll(fwd, 1, 0)
            fwd = step * fwd + here
            bwd = step * bwd + there
        return fwd, bwd, own, cross

    _, _, own, cross = lax.fori_loop(0, chunks // unroll, body, (zero, zero, zero, zero))
    cross = cross * jnp.exp(-lam)
    grad = own + pltpu.roll(own, GROUP - 1, 0) + pltpu.roll(cross, 1, 0)
    grad = grad * (1.0 / (chunks * tokens))
    high = grad.astype(BF16).astype(F32)
    tail = jnp.where(kind == 2, high, pltpu.roll(grad - high, 1, 0))

    def finish(i, carry):
        for u in range(unroll // 2):
            two = []
            for h in range(2):
                rows = tile_at((i * (unroll // 2) + u) * 2 + h)
                two.append(
                    jnp.where(kind == 0, ahead[rows, :], jnp.where(kind == 1, behind[rows, :], tail))
                )
            start = pl.multiple_of((i * (unroll // 2) + u) * 2 * GROUP, 2 * GROUP)
            out_ref[pl.ds(start, 2 * GROUP), :] = jnp.concatenate(two, axis=0).astype(BF16)
        return carry

    lax.fori_loop(0, chunks // unroll, finish, 0)


def residue_kernel(modes, blocks, in_ref, out_ref, tiles, flat):
    tiles[...] = in_ref[...].astype(F32)
    for r in range(modes * blocks // GROUP):
        base = r * GROUP * 4
        flat[pl.ds(r * GROUP, GROUP), :] = (
            tiles[pl.ds(base + 2, GROUP, stride=4), :] + tiles[pl.ds(base + 3, GROUP, stride=4), :]
        )
    for b in range(blocks):
        out_ref[:, pl.ds(b * LANES, LANES)] = flat[pl.ds(b, modes, stride=blocks), :]


def final_kernel(
    modes, blocks, tokens, in_ref, fwd_ref, bwd_ref, dec_ref, gain_ref, upstream_ref,
    grad_gated_hbm, grad_value_hbm, tiles, zt, gt, grad_gated_ref, grad_value_ref, sems
):
    tiles[...] = in_ref[...].astype(F32)
    unroll = UNROLL
    copies = []
    for g in range(blocks // GROUP):
        decay = [rows_of(dec_ref, m, blocks, g) for m in range(modes)]
        ahead, behind = [], []
        for m in range(modes):
            base = (m * blocks + g * GROUP) * 4
            scale = rows_of(gain_ref, m, blocks, g) * decay[m]
            ahead.append(tiles[pl.ds(base, GROUP, stride=4), :] * scale)
            behind.append(tiles[pl.ds(base + 1, GROUP, stride=4), :] * scale)

        def body(i, carry, g=g, decay=decay):
            x, y = carry
            for u in range(unroll):
                t = i * unroll + u
                s = tokens - 1 - t
                rows_t = pl.ds(pl.multiple_of(t * blocks + g * GROUP, GROUP), GROUP)
                rows_s = pl.ds(pl.multiple_of(s * blocks + g * GROUP, GROUP), GROUP)
                zt[rows_t, :] = fwd_ref[rows_t, :] + total(list(x))
                gt[rows_s, :] = bwd_ref[rows_s, :] + total(list(y))
                x = [a * v for a, v in zip(decay, x)]
                y = [a * v for a, v in zip(decay, y)]
            return x, y

        lax.fori_loop(0, tokens // unroll, body, (ahead, behind))
        for b in range(g * GROUP, (g + 1) * GROUP):
            rows = pl.ds(b * LANES, LANES)
            z = transposed(zt[pl.ds(b, tokens, stride=blocks), :].astype(BF16))
            grad_value_ref[rows, :] = (upstream_ref[rows, :].astype(F32) * z).astype(BF16)
            back = transposed(gt[pl.ds(b, tokens, stride=blocks), :].astype(BF16))
            grad_gated_ref[rows, :] = back.astype(BF16)
        rows = pl.ds(g * GROUP * LANES, GROUP * LANES)
        pairs = ((grad_gated_ref, grad_gated_hbm), (grad_value_ref, grad_value_hbm))
        for k, (src, dst) in enumerate(pairs):
            copy = pltpu.make_async_copy(src.at[rows, :], dst.at[rows, :], sems.at[2 * g + k])
            copy.start()
            copies.append(copy)
    for copy in copies:
        copy.wait()


def local(gated, value, upstream, residue, rate, skip_weight):
    channels, tokens = gated.shape
    modes = rate.shape[1]
    chunks = lax.axis_size("seq")
    blocks = channels // LANES
    pairs = modes * blocks
    assert tokens == LANES and pairs == 2 * chunks and blocks % GROUP == 0 and modes % 8 == 0
    rate_t, residue_t, skip = rate.T, residue.T, skip_weight[None, :]
    vmem = pl.BlockSpec(memory_space=pltpu.VMEM)
    hbm = pl.BlockSpec(memory_space=pltpu.HBM)
    cells = modes * channels * tokens

    def call(kernel, specs, out_specs, shapes, scratch, sems, flops, size, limit=16 * 2**20):
        return pl.pallas_call(
            kernel,
            in_specs=specs,
            out_specs=out_specs,
            out_shape=[jax.ShapeDtypeStruct(*shape) for shape in shapes],
            scratch_shapes=[pltpu.VMEM(*shape) for shape in scratch]
            + ([pltpu.SemaphoreType.DMA((sems,))] if sems else []),
            compiler_params=pltpu.CompilerParams(vmem_limit_bytes=limit),
            cost_estimate=pl.CostEstimate(flops=flops, bytes_accessed=size, transcendentals=0),
        )

    native = ((channels, tokens), BF16)
    signal = ((tokens * blocks, LANES), F32)
    per_mode = ((pairs, LANES), F32)
    wire = (chunks * GROUP, LANES)
    (states,) = call(
        functools.partial(state_kernel, modes, blocks, tokens),
        [hbm] * 4,
        [vmem],
        [(wire, BF16)],
        [native, native, native, ((modes, channels), F32), signal, signal, per_mode, (wire, F32)],
        3 * (blocks // GROUP) + 1,
        6 * cells,
        6 * channels * tokens,
        LIMIT,
    )(gated, value, upstream, rate_t)

    def exchange(array):
        array = array.reshape(chunks, GROUP, LANES)
        return lax.all_to_all(array, "seq", split_axis=0, concat_axis=0, tiled=True).reshape(wire)

    states, rate_held = lax.optimization_barrier((states, rate_t))
    (lam,) = call(
        functools.partial(rate_kernel, modes, blocks),
        [vmem],
        [vmem],
        [((GROUP, LANES), F32)],
        [per_mode],
        0,
        modes * channels,
        4 * modes * channels,
    )(rate_held)
    (entering,) = call(
        functools.partial(scan_kernel, chunks, tokens),
        [vmem] * 2,
        [vmem],
        [(wire, BF16)],
        [(wire, F32)] * 3,
        0,
        8 * chunks * GROUP * LANES,
        4 * chunks * GROUP * LANES,
    )(exchange(states), lam)
    entering, gated_held = lax.optimization_barrier((entering, gated))
    fwd, bwd, decay, gain = call(
        functools.partial(own_kernel, modes, blocks, tokens),
        [vmem] * 6,
        [vmem] * 4,
        [signal, signal, per_mode, per_mode],
        [signal, signal],
        0,
        8 * cells,
        14 * channels * tokens,
    )(gated_held, value, upstream, rate_t, residue_t, skip)
    returned, fwd, bwd = lax.optimization_barrier((exchange(entering), fwd, bwd))
    (grad_own,) = call(
        functools.partial(residue_kernel, modes, blocks),
        [vmem],
        [vmem],
        [((modes, channels), F32)],
        [(wire, F32), per_mode],
        0,
        modes * channels,
        8 * modes * channels,
    )(returned)
    grad_other = lax.ppermute(grad_own, "ch", [(0, 1), (1, 0)])
    grad_gated, grad_value = call(
        functools.partial(final_kernel, modes, blocks, tokens),
        [vmem] * 6,
        [hbm] * 2,
        [native, native],
        [(wire, F32), signal, signal, native, native],
        2 * (blocks // GROUP),
        4 * cells,
        14 * channels * tokens,
    )(returned, fwd, bwd, decay, gain, upstream)
    low = lax.axis_index("ch") == 0
    grad_res = jnp.concatenate(
        [jnp.where(low, grad_own, grad_other), jnp.where(low, grad_other, grad_own)], axis=1
    )
    return (grad_gated, grad_value, grad_res.T)


def solution(mesh):
    return jax.shard_map(
        local,
        mesh=mesh,
        in_specs=(P("ch", "seq"), P("ch", "seq"), P("ch", "seq"), P(), P(), P()),
        out_specs=(P("ch", "seq"), P("ch", "seq"), P()),
        check_vma=False,
    )
```

time: 558 us -> 68.2 us (0.12); the launches traced: 552 us -> 67.9 us
  blocking collectives: 250 us -> 0 us
  matrix products: 182 us -> 0 us
  waiting for transfers between devices: 56.1 us -> 22.8 us
  Pallas kernels: 0 us -> 17.2 us
  local copies, waits for them, and re-layouts: 16 us -> 3.21 us
  other arithmetic: 11.6 us -> 0.74 us
  loops' own time: 7.84 us -> 0 us
    all_gather x2 -> x0, blocking collectives: 214 us -> none  [the longest x1 189 us: local(): gathered = lax.all_gather(grad_res, 'seq', axis=0, tiled=True)]
    dot_general x152 -> x0, matrix products: 182 us -> none  [matmul_high(): return jnp.einsum(form, left, right, precision=lax.Precision.HIGHEST)]
    all_to_all x1 -> x0, blocking collectives: 36.4 us -> none  [local(): lax.all_to_all(upstream, 'seq', split_axis=0, concat_axis=1, tiled=True)]
    all_to_all x4 -> x2, waiting for transfers between devices: 56.1 us -> 22.8 us  [exchange(): lax.all_to_all(array, 'seq', split_axis=0, concat_axis=0, tiled=True)]
    pallas_call x0 -> x6, Pallas kernels: none -> 17.2 us  [the longest x1 6.32 us: local(): call(functools.partial(state_kernel, modes, blocks, tokens), [hbm] * 4, [...]
    another operation x1 -> x0, loops' own time: 7.84 us -> none  [apply_blocks(): lax.map(step_fn, (blocked(gated_cols), blocked(grad_cols), blocked(res_lo...]
    dynamic_update_slice x8 -> x0, other arithmetic: 7.29 us -> none  [apply_blocks(): lax.map(step_fn, (blocked(gated_cols), blocked(grad_cols), blocked(res_lo...]
    all_to_all x4 -> x2, starting transfers between devices: 27.3 us -> 22.7 us  [exchange(): lax.all_to_all(array, 'seq', split_axis=0, concat_axis=0, tiled=True)]
  transfers between devices with their start and end apart: 4 -> 3, of which waited for: 3 -> 2; matrix products, arithmetic and copies ran while one was open for 1% -> 0% of each run, Pallas kernels for 0% -> 14%
where the time goes in v1:
time: 68.2 us; the launch traced here: 67.9 us
  starting transfers between devices  23.2 us (34%)
  waiting for transfers between devices  22.8 us (33%)
  Pallas kernels  17.2 us (25%)
  local copies, waits for them, and re-layouts  3.21 us (5%)
  between operations  0.79 us (1%)
  other arithmetic  0.74 us (1%)
    all_to_all x2, waiting for transfers between devices, exchange(): lax.all_to_all(array, 'seq', split_axis=0, concat_axis=0, tiled=True)  22.8 us
    all_to_all x2, starting transfers between devices, exchange(): lax.all_to_all(array, 'seq', split_axis=0, concat_axis=0, tiled=True)  22.7 us
    pallas_call x1, Pallas kernels, local(): call(functools.partial(state_kernel, modes, blocks, tokens), [hbm] * 4, [...  6.32 us
    pallas_call x1, Pallas kernels, local(): call(functools.partial(own_kernel, modes, blocks, tokens), [vmem] * 6, [v...  5.46 us
    pallas_call x1, Pallas kernels, local(): call(functools.partial(final_kernel, modes, blocks, tokens), [vmem] * 6,...  3.99 us
    unnamed x20, local copies, waits for them, and re-layouts  3.21 us
  transfers between devices with their start and end apart: 3, of which 2 were waited for; matrix products, arithmetic and copies ran while one was open for 0% of the time, Pallas kernels for 14%

profile of v1, /device:TPU:1, one launch (start us, length us, event | category | flops | bytes accessed | tf_op | source)
XLA Modules:
  0.0 67.9 jit_solution(14853237128370621926)
XLA Ops:
  0.6 0.0 copy-start.6
  0.6 0.0 copy-start.9
  0.7 6.3 %shard_map.85 = bf16[1024,128]{1,0:T(8,128)(2,1)} custom-call(bf16[2048,128]{1,0:T(8,128)(2,1)} %gated_ref, bf16[2048,128]{1,0:T(8,128)(2,1)} %value_ref.1, bf16[2048,128]{1,0:T(8,128)(2,1)} %upstream_ref.3, f32[16,4096]{1,0:T(8,128)} %bitcast.11), custom_call_target="tpu_custom_call" | custom-call | flops 25165824 | bytes 1572864 | tf_op jit(solution)/shard_map/pallas_call | solution.py:287
  7.0 0.0 copy-start.1
  7.0 0.0 copy-start.3
  7.0 16.5 %all-to-all-start = ((bf16[128,8,128]{2,1,0:T(8,128)(2,1)}), bf16[128,8,128]{2,1,0:T(8,128)(2,1)S(1)}, u32[]{:S(2)}, u32[]{:S(2)}) async-start(bf16[128,8,128]{2,1,0:T(8,128)(2,1)} %bitcast.17), calls=%async_computation | async-start | bytes 524288 | tf_op jit(solution)/shard_map/all_to_all | solution.py:301
  23.6 0.0 copy-done.1
  23.6 0.1 shard_map.86.lam_ref
  23.6 14.9 %all-to-all-done = bf16[128,8,128]{2,1,0:T(8,128)(2,1)S(1)} async-done(((bf16[128,8,128]{2,1,0:T(8,128)(2,1)}), bf16[128,8,128]{2,1,0:T(8,128)(2,1)S(1)}, u32[]{:S(2)}, u32[]{:S(2)}) %all-to-all-start) | async-done | bytes 262176 | tf_op jit(solution)/shard_map/all_to_all | solution.py:301
  38.5 0.0 copy-start
  38.5 0.0 copy-start.2
  38.5 1.3 %shard_map.87 = bf16[1024,128]{1,0:T(8,128)(2,1)} custom-call(bf16[1024,128]{1,0:T(8,128)(2,1)S(1)} %bitcast.14, f32[8,128]{1,0:T(8,128)S(1)} %shard_map.86.lam_ref), custom_call_target="tpu_custom_call" | custom-call | flops 1048576 | bytes 524288 | tf_op jit(solution)/shard_map/pallas_call | solution.py:314
  39.8 6.2 %all-to-all-start.1 = ((bf16[128,8,128]{2,1,0:T(8,128)(2,1)}), bf16[128,8,128]{2,1,0:T(8,128)(2,1)S(1)}, u32[]{:S(2)}, u32[]{:S(2)}) async-start(bf16[128,8,128]{2,1,0:T(8,128)(2,1)} %bitcast.3), calls=%async_computation.1 | async-start | bytes 524288 | tf_op jit(solution)/shard_map/all_to_all | solution.py:301
  46.0 0.0 copy-done.6
  46.0 0.0 copy-done.9
  46.1 0.0 copy-done.3
  46.1 0.0 copy-done
  46.1 0.0 copy-done.2
  46.1 5.5 %shard_map.88 = (f32[2048,128]{1,0:T(8,128)S(1)}, f32[2048,128]{1,0:T(8,128)S(1)}, f32[256,128]{1,0:T(8,128)S(1)}, f32[256,128]{1,0:T(8,128)S(1)}) custom-call(bf16[2048,128]{1,0:T(8,128)(2,1)S(1)} %copy-done.2, bf16[2048,128]{1,0:T(8,128)(2,1)S(1)} %copy-done.3, bf16[2048,128]{1,0:T(8,128)(2,1)S(1)} %copy-done, f32[16,4096]{1,0:T(8,128)S(1)} %bitcast.13, ...), custom_call_target="tpu_custom_call" | custom-call | flops 33554432 | bytes 3670016 | tf_op jit(solution)/shard_map/pallas_call | solution.py:325
  51.5 0.0 copy-start.4
  51.6 1.0 %copy-done.4 = f32[2048,128]{1,0:T(8,128)} copy-done((f32[2048,128]{1,0:T(8,128)}, f32[2048,128]{1,0:T(8,128)S(1)}, u32[]{:S(2)}) %copy-start.4) | copy-done | bytes 1048600
  52.5 0.0 copy-start.7
  52.5 0.7 copy-done.7
  53.2 7.8 %all-to-all-done.1 = bf16[128,8,128]{2,1,0:T(8,128)(2,1)S(1)} async-done(((bf16[128,8,128]{2,1,0:T(8,128)(2,1)}), bf16[128,8,128]{2,1,0:T(8,128)(2,1)S(1)}, u32[]{:S(2)}, u32[]{:S(2)}) %all-to-all-start.1) | async-done | bytes 262176 | tf_op jit(solution)/shard_map/all_to_all | solution.py:301
  61.0 0.0 copy-start.8
  61.0 0.1 shard_map.90
  61.1 0.5 collective-permute-start
  61.6 0.3 copy-done.8
  61.9 1.2 %copy-done.5 = f32[2048,128]{1,0:T(8,128)S(1)} copy-done((f32[2048,128]{1,0:T(8,128)S(1)}, f32[2048,128]{1,0:T(8,128)}, u32[]{:S(2)}) %copy-start.5) | copy-done | bytes 1048600
  63.2 4.0 %shard_map.89 = (bf16[2048,128]{1,0:T(8,128)(2,1)}, bf16[2048,128]{1,0:T(8,128)(2,1)}) custom-call(bf16[1024,128]{1,0:T(8,128)(2,1)S(1)} %bitcast.10, f32[2048,128]{1,0:T(8,128)S(1)} %get-tuple-element.23.fwd_ref, f32[2048,128]{1,0:T(8,128)S(1)} %copy-done.5, f32[256,128]{1,0:T(8,128)S(1)} %get-tuple-element.25.dec_ref, f32[256,128]{1,0:T(8,128)S(1)} %copy-done.8, ...), custom_call_target="tpu_custom_call" | custom-call | flops 16777216 | bytes 3670016 | tf_op jit(solution)/shard_map/pallas_call | solution.py:347
  67.2 0.0 collective-permute-done
  67.2 0.7 %maximum_bitcast_fusion = f32[4096,16]{0,1:T(8,128)} fusion(f32[16,2048]{1,0:T(8,128)S(1)} %get-tuple-element.30, f32[16,2048]{1,0:T(8,128)S(1)} %get-tuple-element.29), kind=kLoop, calls=%fused_computation | loop fusion | flops 65536 | bytes 524288 | tf_op jit(solution)/shard_map/transpose | solution.py:361
  (2 shorter events, 0.0 us)
Async XLA Ops:
  0.6 45.4 %copy-start.6 = (f32[4096,16]{0,1:T(8,128)S(1)}, f32[4096,16]{0,1:T(8,128)}, u32[]{:S(2)}) copy-start(f32[4096,16]{0,1:T(8,128)} %param.9) | copy-start | bytes 786436
  0.6 45.4 %copy-start.9 = (f32[4096]{0:T(1024)S(1)}, f32[4096]{0:T(1024)}, u32[]{:S(2)}) copy-start(f32[4096]{0:T(1024)} %param.11) | copy-start | bytes 49156
  7.0 16.6 %copy-start.1 = (f32[4096,16]{0,1:T(8,128)S(1)}, f32[4096,16]{0,1:T(8,128)}, u32[]{:S(2)}) copy-start(f32[4096,16]{0,1:T(8,128)} %param.10) | copy-start | bytes 786436
  7.0 39.1 %copy-start.3 = (bf16[2048,128]{1,0:T(8,128)(2,1)S(1)}, bf16[2048,128]{1,0:T(8,128)(2,1)}, u32[]{:S(2)}) copy-start(bf16[2048,128]{1,0:T(8,128)(2,1)} %value_ref.1) | copy-start | bytes 1572868
  7.0 31.5 %all-to-all-start = ((bf16[128,8,128]{2,1,0:T(8,128)(2,1)}), bf16[128,8,128]{2,1,0:T(8,128)(2,1)S(1)}, u32[]{:S(2)}, u32[]{:S(2)}) async-start(bf16[128,8,128]{2,1,0:T(8,128)(2,1)} %bitcast.17), calls=%async_computation | async-start | bytes 524288 | tf_op jit(solution)/shard_map/all_to_all | solution.py:301
  38.5 7.5 %copy-start = (bf16[2048,128]{1,0:T(8,128)(2,1)S(1)}, bf16[2048,128]{1,0:T(8,128)(2,1)}, u32[]{:S(2)}) copy-start(bf16[2048,128]{1,0:T(8,128)(2,1)} %upstream_ref.3) | copy-start | bytes 1572868
  38.5 7.5 %copy-start.2 = (bf16[2048,128]{1,0:T(8,128)(2,1)S(1)}, bf16[2048,128]{1,0:T(8,128)(2,1)}, u32[]{:S(2)}) copy-start(bf16[2048,128]{1,0:T(8,128)(2,1)} %gated_ref) | copy-start | bytes 1572868
  39.8 21.2 %all-to-all-start.1 = ((bf16[128,8,128]{2,1,0:T(8,128)(2,1)}), bf16[128,8,128]{2,1,0:T(8,128)(2,1)S(1)}, u32[]{:S(2)}, u32[]{:S(2)}) async-start(bf16[128,8,128]{2,1,0:T(8,128)(2,1)} %bitcast.3), calls=%async_computation.1 | async-start | bytes 524288 | tf_op jit(solution)/shard_map/all_to_all | solution.py:301
  51.5 1.0 %copy-start.4 = (f32[2048,128]{1,0:T(8,128)}, f32[2048,128]{1,0:T(8,128)S(1)}, u32[]{:S(2)}) copy-start(f32[2048,128]{1,0:T(8,128)S(1)} %get-tuple-element.24.bwd_ref) | copy-start | bytes 3145732
  52.5 0.7 copy-start.7
  61.0 0.9 %copy-start.8 = (f32[256,128]{1,0:T(8,128)S(1)}, f32[256,128]{1,0:T(8,128)}, u32[]{:S(2)}) copy-start(f32[256,128]{1,0:T(8,128)} %copy-done.7) | copy-start | bytes 393220
  61.1 6.0 %collective-permute-start = (f32[16,2048]{1,0:T(8,128)S(1)}, f32[16,2048]{1,0:T(8,128)S(1)}, u32[]{:S(2)}, u32[]{:S(2)}) collective-permute-start(f32[16,2048]{1,0:T(8,128)S(1)} %shard_map.90), channel_id=1, source_target_pairs={{0,1},{1,0},{2,3},{3,2},{4,5},{5,4},{6,7},{7,6},{8,9},{9,8},{10,11... | collective-permute-start | bytes 393224 | tf_op jit(solution)/shard_map/ppermute | solution.py:346
  61.9 1.2 %copy-start.5 = (f32[2048,128]{1,0:T(8,128)S(1)}, f32[2048,128]{1,0:T(8,128)}, u32[]{:S(2)}) copy-start(f32[2048,128]{1,0:T(8,128)} %copy-done.4) | copy-start | bytes 3145732

commit v2 on v1

v2 whole, which is shorter than its diff:
```python
import functools

import jax
import jax.numpy as jnp
from jax import lax
from jax.experimental import pallas as pl
from jax.experimental.pallas import tpu as pltpu
from jax.sharding import PartitionSpec as P

F32 = jnp.float32
BF16 = jnp.bfloat16
LANES = 128
GROUP = 8
PART, UNROLL = 8, 16
FINAL_UNROLL = 16
STATE_PART, STATE_UNROLL, RUN = 4, 32, 4
LIMIT = 56 * 2**20


def transposed(block):
    return block.astype(F32).T


def spread_modes(src_ref, dst_ref, first, modes, blocks):
    for b in range(blocks):
        start = pl.multiple_of(first + b * LANES, LANES)
        row = b // GROUP * modes * GROUP + b % GROUP
        dst_ref[pl.ds(row, modes, stride=GROUP), :] = src_ref[:, pl.ds(start, LANES)]


def tile(index):
    return pl.ds(pl.multiple_of(index * GROUP, GROUP), GROUP)


def put_signal(signal_ref, gt, b, j, tokens):
    gt[pl.ds(j, tokens, stride=GROUP), :] = transposed(signal_ref[pl.ds(b * LANES, LANES), :])


def put_dz(value_ref, upstream_ref, dz_ref, dzt, b, j, tokens):
    rows = pl.ds(b * LANES, LANES)
    dz = (upstream_ref[rows, :].astype(F32) * value_ref[rows, :].astype(F32)).astype(BF16)
    dz_ref[rows, :] = dz
    dzt[pl.ds(j, tokens, stride=GROUP), :] = transposed(dz)


def total(terms):
    while len(terms) > 1:
        pairs = [a + b for a, b in zip(terms[::2], terms[1::2])]
        terms = pairs + ([terms[-1]] if len(terms) % 2 else [])
    return terms[0]


def power(base, exponent):
    result = base
    for _ in range(exponent - 1):
        result = result * base
    return result


def horner(base, terms):
    result = terms[0]
    for term in terms[1:]:
        result = result * base + term
    return result


def state_kernel(
    modes, blocks, tokens, gated_hbm, value_hbm, upstream_hbm, rate_hbm, out_hbm, dz_hbm,
    gated_ref, value_ref, upstream_ref, dz_ref, rate_ref, gts, dzts, lam, pack, stage, sems, out_sems, dz_sems
):
    half = GROUP * LANES
    groups = blocks // GROUP
    start = pl.multiple_of(lax.axis_index("ch") * (blocks * LANES), LANES)
    rate_copy = pltpu.make_async_copy(
        rate_hbm.at[:, pl.ds(start, blocks * LANES)], rate_ref, sems.at[3 * groups]
    )
    copies = []
    for g in range(groups):
        rows = pl.ds(g * half, half)
        pairs = ((gated_hbm, gated_ref), (upstream_hbm, upstream_ref), (value_hbm, value_ref))
        copies.append(
            [
                pltpu.make_async_copy(src.at[rows, :], dst.at[rows, :], sems.at[3 * g + k])
                for k, (src, dst) in enumerate(pairs)
            ]
        )
    for copy in copies[0] + [rate_copy] + [copy for part in copies[1:] for copy in part]:
        copy.start()
    copies[0][0].wait()
    for j in range(GROUP):
        put_signal(gated_ref, gts[0], j, j, tokens)
    copies[0][1].wait()
    copies[0][2].wait()
    for j in range(GROUP):
        put_dz(value_ref, upstream_ref, dz_ref, dzts[0], j, j, tokens)
    rate_copy.wait()
    spread_modes(rate_ref, lam, 0, modes, blocks)
    zero = jnp.zeros((GROUP, LANES), F32)
    sent, late = [], []
    for g in range(groups):
        gt, dzt = gts[g], dzts[g]
        if g:
            for copy in copies[g]:
                copy.wait()
            for j in range(GROUP):
                put_signal(gated_ref, gt, g * GROUP + j, j, tokens)
                put_dz(value_ref, upstream_ref, dz_ref, dzt, g * GROUP + j, j, tokens)
        rows = pl.ds(g * half, half)
        copy = pltpu.make_async_copy(dz_ref.at[rows, :], dz_hbm.at[rows, :], dz_sems.at[g])
        copy.start()
        late.append(copy)
        lags = None
        for m0 in range(0, modes, STATE_PART):
            some = range(m0, m0 + STATE_PART)
            decay = [jnp.exp(-lam[tile(g * modes + m), :]) for m in some]
            jump = [power(a, RUN) for a in decay]

            def body(i, carry, gt=gt, dzt=dzt, decay=decay, jump=jump, first=m0 == 0):
                x, y, own, reach, lags = carry
                for u in range(STATE_UNROLL // RUN):
                    t = i * STATE_UNROLL + u * RUN
                    gs = [gt[tile(t + k), :] for k in range(RUN)]
                    ds = [dzt[tile(t + k), :] for k in range(RUN)]
                    if first:
                        lags = [
                            c + total([d * v for d, v in zip(ds[k:], gs)])
                            for k, c in enumerate(lags)
                        ]
                    ends = [horner(a, gs) for a in decay]
                    starts = [horner(a, ds[::-1]) for a in decay]
                    own = [o + v * w for o, v, w in zip(own, x, starts)]
                    y = [v + p * w for v, p, w in zip(y, reach, starts)]
                    x = [a * v + w for a, v, w in zip(jump, x, ends)]
                    reach = [a * p for a, p in zip(jump, reach)]
                return x, y, own, reach, lags

            zeros = [zero] * STATE_PART
            ones = [zero + 1.0] * STATE_PART
            carry = (zeros, zeros, zeros, ones, [zero] * RUN if m0 == 0 else [])
            x, y, own, _, found = lax.fori_loop(0, tokens // STATE_UNROLL, body, carry)
            lags = found if m0 == 0 else lags
            for k in range(STATE_PART):
                base = (g * modes + m0 + k) * GROUP * 4
                term = decay[k] * own[k] + horner(decay[k], lags[::-1])
                high = term.astype(BF16).astype(F32)
                for kind, rows in enumerate((x[k], y[k], high, term - high)):
                    pack[pl.ds(base + kind, GROUP, stride=4), :] = rows
            rows = pl.ds((g * modes + m0) * GROUP * 4, STATE_PART * GROUP * 4)
            stage[rows, :] = pack[rows, :].astype(BF16)
            copy = pltpu.make_async_copy(
                stage.at[rows, :], out_hbm.at[rows, :], out_sems.at[len(sent)]
            )
            copy.start()
            sent.append(copy)
    for copy in sent + late:
        copy.wait()


def own_sums(modes, tokens, g, signal, out_ref, dec_ref, gain_ref, skip, order):
    zero = jnp.zeros((GROUP, LANES), F32)
    for m0 in range(0, modes, PART):
        decay = [dec_ref[tile(g * modes + m), :] for m in range(m0, m0 + PART)]
        gain = [gain_ref[tile(g * modes + m), :] for m in range(m0, m0 + PART)]

        def body(i, x, m0=m0, decay=decay, gain=gain):
            for u in range(UNROLL):
                t = order(i * UNROLL + u)
                at = tile(g * tokens + t)
                v = signal[tile(t), :]
                x = [a * w + v for a, w in zip(decay, x)]
                known = out_ref[at, :] if m0 else skip * v
                out_ref[at, :] = total([r * w for r, w in zip(gain, x)] + [known])
            return x

        lax.fori_loop(0, tokens // UNROLL, body, [zero] * PART)


def skip_of(skip_ref, first, g):
    parts = [
        skip_ref[:, pl.ds(pl.multiple_of(first + (g * GROUP + j) * LANES, LANES), LANES)]
        for j in range(GROUP)
    ]
    return jnp.concatenate(parts, axis=0)


def ahead_kernel(
    modes, blocks, tokens, gated_ref, rate_ref, res_ref, skip_ref,
    fwd_ref, dec_ref, gain_ref, lam_ref, gt
):
    first = lax.axis_index("ch") * (blocks * LANES)
    spread_modes(rate_ref, dec_ref, first, modes, blocks)
    spread_modes(res_ref, gain_ref, first, modes, blocks)
    for h in range(2):
        own = dec_ref[pl.ds(lax.axis_index("seq") * 2 + h, 1), :]
        lam_ref[pl.ds(4 * h, 4), :] = jnp.broadcast_to(own, (4, LANES))
    dec_ref[...] = jnp.exp(-dec_ref[...])
    for g in range(blocks // GROUP):
        for j in range(GROUP):
            put_signal(gated_ref, gt, g * GROUP + j, j, tokens)
        skip = skip_of(skip_ref, first, g)
        own_sums(modes, tokens, g, gt, fwd_ref, dec_ref, gain_ref, skip, lambda t: t)


def behind_kernel(modes, blocks, tokens, dz_ref, dec_ref, gain_ref, skip_ref, bwd_ref, dzt):
    first = lax.axis_index("ch") * (blocks * LANES)
    for g in range(blocks // GROUP):
        for j in range(GROUP):
            put_signal(dz_ref, dzt, g * GROUP + j, j, tokens)
        skip = skip_of(skip_ref, first, g)
        order = lambda t: tokens - 1 - t
        own_sums(modes, tokens, g, dzt, bwd_ref, dec_ref, gain_ref, skip, order)


def scan_kernel(chunks, tokens, in_ref, lam_ref, out_hbm, tiles, ahead, behind, stage, sems):
    tiles[...] = in_ref[...].astype(F32)
    lam = lam_ref[...]
    step = jnp.exp(lam * (-1.0 * tokens))
    kind = lax.broadcasted_iota(jnp.int32, (GROUP, LANES), 0) % 4
    unroll = 8
    zero = jnp.zeros((GROUP, LANES), F32)

    def body(i, carry):
        fwd, bwd, own, cross = carry
        for u in range(unroll):
            d = i * unroll + u
            e = chunks - 1 - d
            here, there = tiles[tile(d), :], tiles[tile(e), :]
            ahead[tile(d), :] = fwd
            behind[tile(e), :] = bwd
            own = own + here
            cross = cross + here * pltpu.roll(fwd, 1, 0)
            fwd = step * fwd + here
            bwd = step * bwd + there
        return fwd, bwd, own, cross

    _, _, own, cross = lax.fori_loop(0, chunks // unroll, body, (zero, zero, zero, zero))
    cross = cross * jnp.exp(-lam)
    grad = own + pltpu.roll(own, GROUP - 1, 0) + pltpu.roll(cross, 1, 0)
    grad = grad * (1.0 / (chunks * tokens))
    high = grad.astype(BF16).astype(F32)
    tail = jnp.where(kind == 2, high, pltpu.roll(grad - high, 1, 0))
    quarter = chunks // 4
    sent = []
    for part in range(4):
        for pair in range(quarter // 2):
            d = part * quarter + 2 * pair
            both = [
                jnp.where(
                    kind == 0,
                    ahead[pl.ds(e * GROUP, GROUP), :],
                    jnp.where(kind == 1, behind[pl.ds(e * GROUP, GROUP), :], tail),
                )
                for e in (d, d + 1)
            ]
            stage[pl.ds(d * GROUP, 2 * GROUP), :] = jnp.concatenate(both, axis=0).astype(BF16)
        rows = pl.ds(part * quarter * GROUP, quarter * GROUP)
        copy = pltpu.make_async_copy(stage.at[rows, :], out_hbm.at[rows, :], sems.at[part])
        copy.start()
        sent.append(copy)
    for copy in sent:
        copy.wait()


def residue_kernel(modes, blocks, in_ref, out_ref, tiles, flat):
    tiles[...] = in_ref[...].astype(F32)
    for r in range(modes * blocks // GROUP):
        base = r * GROUP * 4
        flat[pl.ds(r * GROUP, GROUP), :] = (
            tiles[pl.ds(base + 2, GROUP, stride=4), :] + tiles[pl.ds(base + 3, GROUP, stride=4), :]
        )
    for b in range(blocks):
        row = b // GROUP * modes * GROUP + b % GROUP
        out_ref[:, pl.ds(b * LANES, LANES)] = flat[pl.ds(row, modes, stride=GROUP), :]


def final_kernel(
    modes, blocks, tokens, in_ref, fwd_ref, bwd_hbm, dec_ref, gain_ref, upstream_hbm,
    grad_gated_hbm, grad_value_hbm, tiles, zts, gts, bwd_ref, upstream_ref, grad_gated_ref,
    grad_value_ref, in_sems, sems
):
    groups = blocks // GROUP
    half = GROUP * LANES
    own_copies = []
    for g in range(groups):
        rows = pl.ds(g * tokens * GROUP, tokens * GROUP)
        own_copies.append(
            pltpu.make_async_copy(bwd_hbm.at[rows, :], bwd_ref.at[rows, :], in_sems.at[g])
        )
    upstream_copy = pltpu.make_async_copy(upstream_hbm, upstream_ref, in_sems.at[groups])
    for copy in [own_copies[0], upstream_copy] + own_copies[1:]:
        copy.start()
    tiles[...] = in_ref[...].astype(F32)
    copies = []

    def send(src, dst, first, size):
        rows = pl.ds(first * LANES, size * LANES)
        copy = pltpu.make_async_copy(src.at[rows, :], dst.at[rows, :], sems.at[len(copies)])
        copy.start()
        copies.append(copy)

    for g in range(groups):
        decay = [dec_ref[tile(g * modes + m), :] for m in range(modes)]
        scale = [gain_ref[tile(g * modes + m), :] * decay[m] for m in range(modes)]

        def entering(kind, g=g, scale=scale):
            return [
                tiles[pl.ds((g * modes + m) * GROUP * 4 + kind, GROUP, stride=4), :] * scale[m]
                for m in range(modes)
            ]

        def ahead(i, x, g=g, decay=decay):
            for u in range(FINAL_UNROLL):
                t = i * FINAL_UNROLL + u
                zts[g][tile(t), :] = fwd_ref[tile(g * tokens + t), :] + total(list(x))
                x = [a * v for a, v in zip(decay, x)]
            return x

        def behind(i, y, g=g, decay=decay):
            for u in range(FINAL_UNROLL):
                s = tokens - 1 - i * FINAL_UNROLL - u
                gts[g][tile(s), :] = bwd_ref[tile(g * tokens + s), :] + total(list(y))
                y = [a * v for a, v in zip(decay, y)]
            return y

        lax.fori_loop(0, tokens // FINAL_UNROLL, ahead, entering(0))
        if g == 0:
            upstream_copy.wait()
        for j in range(GROUP):
            rows = pl.ds(g * half + j * LANES, LANES)
            z = transposed(zts[g][pl.ds(j, tokens, stride=GROUP), :].astype(BF16))
            grad_value_ref[rows, :] = (upstream_ref[rows, :].astype(F32) * z).astype(BF16)
        send(grad_value_ref, grad_value_hbm, g * GROUP, GROUP)
        own_copies[g].wait()
        lax.fori_loop(0, tokens // FINAL_UNROLL, behind, entering(1))
        for j in range(GROUP):
            rows = pl.ds(g * half + j * LANES, LANES)
            back = transposed(gts[g][pl.ds(j, tokens, stride=GROUP), :].astype(BF16))
            grad_gated_ref[rows, :] = back.astype(BF16)
            if j % 4 == 3:
                send(grad_gated_ref, grad_gated_hbm, g * GROUP + j - 3, 4)
    for copy in copies:
        copy.wait()


def local(gated, value, upstream, residue, rate, skip_weight):
    channels, tokens = gated.shape
    modes = rate.shape[1]
    chunks = lax.axis_size("seq")
    blocks = channels // LANES
    pairs = modes * blocks
    groups = blocks // GROUP
    assert tokens == LANES == UNROLL * GROUP and pairs == 2 * chunks
    assert blocks % GROUP == 0 and modes == 2 * PART and chunks % 8 == 0
    rate_t, residue_t, skip = rate.T, residue.T, skip_weight[None, :]
    vmem = pl.BlockSpec(memory_space=pltpu.VMEM)
    hbm = pl.BlockSpec(memory_space=pltpu.HBM)
    cells = modes * channels * tokens

    def call(kernel, specs, out_specs, shapes, scratch, flops, size, limit=16 * 2**20):
        return pl.pallas_call(
            kernel,
            in_specs=specs,
            out_specs=out_specs,
            out_shape=[jax.ShapeDtypeStruct(*shape) for shape in shapes],
            scratch_shapes=scratch,
            compiler_params=pltpu.CompilerParams(vmem_limit_bytes=limit),
            cost_estimate=pl.CostEstimate(flops=flops, bytes_accessed=size, transcendentals=0),
        )

    native = ((channels, tokens), BF16)
    signal = ((tokens * blocks, LANES), F32)
    per_mode = ((pairs, LANES), F32)
    wire = (chunks * GROUP, LANES)
    one = pltpu.VMEM((tokens * GROUP, LANES), F32)
    raw = pltpu.VMEM(*native)
    unpacked = pltpu.VMEM(wire, F32)
    staged = pltpu.VMEM(wire, BF16)
    flat = pltpu.VMEM(*per_mode)
    sems = lambda count: pltpu.SemaphoreType.DMA((count,))
    states, dz = call(
        functools.partial(state_kernel, modes, blocks, tokens),
        [hbm] * 4,
        [hbm] * 2,
        [(wire, BF16), native],
        [raw, raw, raw, raw, pltpu.VMEM((modes, channels), F32), [one] * groups, [one] * groups]
        + [flat, unpacked, staged, sems(3 * groups + 1), sems(pairs // GROUP // STATE_PART)]
        + [sems(groups)],
        5 * cells,
        8 * channels * tokens,
        LIMIT,
    )(gated, value, upstream, rate_t)

    def exchange(array):
        array = array.reshape(chunks, GROUP, LANES)
        return lax.all_to_all(array, "seq", split_axis=0, concat_axis=0, tiled=True).reshape(wire)

    states, gated_held = lax.optimization_barrier((states, gated))
    fwd, decay, gain, lam = call(
        functools.partial(ahead_kernel, modes, blocks, tokens),
        [vmem] * 4,
        [vmem] * 4,
        [signal, per_mode, per_mode, ((GROUP, LANES), F32)],
        [one],
        4 * cells,
        6 * channels * tokens,
    )(gated_held, rate_t, residue_t, skip)
    (entering,) = call(
        functools.partial(scan_kernel, chunks, tokens),
        [vmem] * 2,
        [hbm],
        [(wire, BF16)],
        [unpacked, unpacked, unpacked, staged, sems(4)],
        8 * chunks * GROUP * LANES,
        4 * chunks * GROUP * LANES,
    )(exchange(states), lam)
    entering, dz_held = lax.optimization_barrier((entering, dz))
    (bwd,) = call(
        functools.partial(behind_kernel, modes, blocks, tokens),
        [vmem] * 4,
        [vmem],
        [signal],
        [one],
        4 * cells,
        6 * channels * tokens,
    )(dz_held, decay, gain, skip)
    returned, bwd = lax.optimization_barrier((exchange(entering), bwd))
    (grad_own,) = call(
        functools.partial(residue_kernel, modes, blocks),
        [vmem],
        [vmem],
        [((modes, channels), F32)],
        [unpacked, flat],
        modes * channels,
        8 * modes * channels,
    )(returned)
    grad_other = lax.ppermute(grad_own, "ch", [(0, 1), (1, 0)])
    grad_gated, grad_value = call(
        functools.partial(final_kernel, modes, blocks, tokens),
        [vmem, vmem, hbm, vmem, vmem, hbm],
        [hbm] * 2,
        [native, native],
        [unpacked, [one] * groups, [one] * groups, pltpu.VMEM(*signal), raw, raw, raw]
        + [sems(groups + 1), sems(3 * groups)],
        4 * cells,
        14 * channels * tokens,
    )(returned, fwd, bwd, decay, gain, upstream)
    low = lax.axis_index("ch") == 0
    grad_res = jnp.concatenate(
        [jnp.where(low, grad_own, grad_other), jnp.where(low, grad_other, grad_own)], axis=1
    )
    return (grad_gated, grad_value, grad_res.T)


def solution(mesh):
    return jax.shard_map(
        local,
        mesh=mesh,
        in_specs=(P("ch", "seq"), P("ch", "seq"), P("ch", "seq"), P(), P(), P()),
        out_specs=(P("ch", "seq"), P("ch", "seq"), P()),
        check_vma=False,
    )
```

time: 68.2 us -> 65.9 us (0.966)
  local copies, waits for them, and re-layouts: 3.21 us -> 1.06 us
  Pallas kernels: 17.2 us -> 16.1 us
  waiting for transfers between devices: 22.8 us -> 23.8 us
    unnamed x20 -> x12, local copies, waits for them, and re-layouts: 3.21 us -> 1.06 us
    pallas_call x1, Pallas kernels: 6.32 us -> 5.39 us  [local(): call(functools.partial(state_kernel, modes, blocks, tokens), [hbm] * 4, [...]
  transfers between devices with their start and end apart: 3 -> 3, of which waited for: 2 -> 3; matrix products, arithmetic and copies ran while one was open for 0% -> 0% of each run, Pallas kernels for 14% -> 14%
where the time goes in v2:
time: 65.9 us; the launch traced here: 65.7 us
  waiting for transfers between devices  23.8 us (36%)
  starting transfers between devices  23.2 us (35%)
  Pallas kernels  16.1 us (24%)
  local copies, waits for them, and re-layouts  1.06 us (2%)
  between operations  0.76 us (1%)
  other arithmetic  0.74 us (1%)
    all_to_all x2, waiting for transfers between devices, exchange(): lax.all_to_all(array, 'seq', split_axis=0, concat_axis=0, tiled=True)  23.4 us
    all_to_all x2, starting transfers between devices, exchange(): lax.all_to_all(array, 'seq', split_axis=0, concat_axis=0, tiled=True)  22.8 us
    pallas_call x1, Pallas kernels, local(): call(functools.partial(state_kernel, modes, blocks, tokens), [hbm] * 4, [...  5.39 us
    pallas_call x1, Pallas kernels, local(): call(functools.partial(final_kernel, modes, blocks, tokens), [vmem, vmem,...  3.94 us
    pallas_call x1, Pallas kernels, local(): call(functools.partial(behind_kernel, modes, blocks, tokens), [vmem] * 4,...  2.82 us
    pallas_call x1, Pallas kernels, local(): call(functools.partial(ahead_kernel, modes, blocks, tokens), [vmem] * 4,...  2.7 us
  transfers between devices with their start and end apart: 3, of which 3 were waited for; matrix products, arithmetic and copies ran while one was open for 0% of the time, Pallas kernels for 14%

profile of v2, /device:TPU:1, one launch (start us, length us, event | category | flops | bytes accessed | tf_op | source)
XLA Modules:
  0.0 65.7 jit_solution(9713160060869533605)
XLA Ops:
  0.6 0.0 copy-start.2
  0.6 0.0 copy-start.4
  0.7 0.0 copy-start.5
  0.7 5.4 %shard_map.85 = (bf16[1024,128]{1,0:T(8,128)(2,1)}, bf16[2048,128]{1,0:T(8,128)(2,1)}) custom-call(bf16[2048,128]{1,0:T(8,128)(2,1)} %gated_ref, bf16[2048,128]{1,0:T(8,128)(2,1)} %value_hbm.1, bf16[2048,128]{1,0:T(8,128)(2,1)} %upstream_hbm.3, f32[16,4096]{1,0:T(8,128)} %bitcast.11), custom_call_target="tpu_custom_call" | custom-call | flops 20971520 | bytes 2097152 | tf_op jit(solution)/shard_map/pallas_call | solution.py:380
  6.1 0.0 copy-start
  6.1 16.5 %all-to-all-start = ((bf16[128,8,128]{2,1,0:T(8,128)(2,1)}), bf16[128,8,128]{2,1,0:T(8,128)(2,1)S(1)}, u32[]{:S(2)}, u32[]{:S(2)}) async-start(bf16[128,8,128]{2,1,0:T(8,128)(2,1)} %bitcast.17), calls=%async_computation | async-start | bytes 524288 | tf_op jit(solution)/shard_map/all_to_all | solution.py:395
  22.6 0.0 copy-done.2
  22.6 0.0 copy-done.4
  22.6 0.0 copy-done.5
  22.6 0.0 copy-done
  22.7 2.7 %shard_map.86 = (f32[2048,128]{1,0:T(8,128)S(1)}, f32[256,128]{1,0:T(8,128)S(1)}, f32[256,128]{1,0:T(8,128)S(1)}, f32[8,128]{1,0:T(8,128)S(1)}) custom-call(bf16[2048,128]{1,0:T(8,128)(2,1)S(1)} %copy-done, f32[16,4096]{1,0:T(8,128)S(1)} %bitcast.12, f32[16,4096]{1,0:T(8,128)S(1)} %bitcast.14, f32[1,4096]{1,0:T(1,128)S(1)} %bitcast.15), custom_call_target="tpu_custom_call" | custom-call | flops 16777216 | bytes 1572864 | tf_op jit(solution)/shard_map/pallas_call | solution.py:398
  25.4 12.3 %all-to-all-done = bf16[128,8,128]{2,1,0:T(8,128)(2,1)S(1)} async-done(((bf16[128,8,128]{2,1,0:T(8,128)(2,1)}), bf16[128,8,128]{2,1,0:T(8,128)(2,1)S(1)}, u32[]{:S(2)}, u32[]{:S(2)}) %all-to-all-start) | async-done | bytes 262176 | tf_op jit(solution)/shard_map/all_to_all | solution.py:395
  37.6 1.2 %shard_map.87 = bf16[1024,128]{1,0:T(8,128)(2,1)} custom-call(bf16[1024,128]{1,0:T(8,128)(2,1)S(1)} %bitcast.13, f32[8,128]{1,0:T(8,128)S(1)} %get-tuple-element.20.lam_ref), custom_call_target="tpu_custom_call" | custom-call | flops 1048576 | bytes 524288 | tf_op jit(solution)/shard_map/pallas_call | solution.py:407
  38.8 6.2 %all-to-all-start.1 = ((bf16[128,8,128]{2,1,0:T(8,128)(2,1)}), bf16[128,8,128]{2,1,0:T(8,128)(2,1)S(1)}, u32[]{:S(2)}, u32[]{:S(2)}) async-start(bf16[128,8,128]{2,1,0:T(8,128)(2,1)} %bitcast.5), calls=%async_computation.1 | async-start | bytes 524288 | tf_op jit(solution)/shard_map/all_to_all | solution.py:395
  45.0 0.0 copy-start.3
  45.0 1.0 %copy-done.3 = bf16[2048,128]{1,0:T(8,128)(2,1)S(1)} copy-done((bf16[2048,128]{1,0:T(8,128)(2,1)S(1)}, bf16[2048,128]{1,0:T(8,128)(2,1)}, u32[]{:S(2)}) %copy-start.3) | copy-done | bytes 524312
  46.0 0.0 copy-start.1
  46.0 2.8 %shard_map.88.bwd_hbm = f32[2048,128]{1,0:T(8,128)S(1)} custom-call(bf16[2048,128]{1,0:T(8,128)(2,1)S(1)} %copy-done.3, f32[256,128]{1,0:T(8,128)S(1)} %get-tuple-element.24.dec_ref, f32[256,128]{1,0:T(8,128)S(1)} %get-tuple-element.25.gain_ref, f32[1,4096]{1,0:T(1,128)S(1)} %bitcast.16), custom_call_target="tpu_custom_call" | custom-call | flops 16777216 | bytes 1572864 | tf_op jit(solution)/shard_map/pallas_call | solution.py:417
  48.9 11.1 %all-to-all-done.1 = bf16[128,8,128]{2,1,0:T(8,128)(2,1)S(1)} async-done(((bf16[128,8,128]{2,1,0:T(8,128)(2,1)}), bf16[128,8,128]{2,1,0:T(8,128)(2,1)S(1)}, u32[]{:S(2)}, u32[]{:S(2)}) %all-to-all-start.1) | async-done | bytes 262176 | tf_op jit(solution)/shard_map/all_to_all | solution.py:395
  60.0 0.1 shard_map.90
  60.1 0.5 collective-permute-start
  60.6 0.0 copy-done.1
  60.6 3.9 %shard_map.89 = (bf16[2048,128]{1,0:T(8,128)(2,1)}, bf16[2048,128]{1,0:T(8,128)(2,1)}) custom-call(bf16[1024,128]{1,0:T(8,128)(2,1)S(1)} %bitcast.10, f32[2048,128]{1,0:T(8,128)S(1)} %get-tuple-element.27.fwd_ref, f32[2048,128]{1,0:T(8,128)S(1)} %shard_map.88.bwd_hbm, f32[256,128]{1,0:T(8,128)S(1)} %get-tuple-element.24.dec_ref, ...), custom_call_target="tpu_custom_call" | custom-call | flops 16777216 | bytes 3670016 | tf_op jit(solution)/shard_map/pallas_call | solution.py:437
  64.5 0.4 collective-permute-done
  64.9 0.7 %maximum_bitcast_fusion = f32[4096,16]{0,1:T(8,128)} fusion(f32[16,2048]{1,0:T(8,128)S(1)} %get-tuple-element.32, f32[16,2048]{1,0:T(8,128)S(1)} %get-tuple-element.31), kind=kLoop, calls=%fused_computation | loop fusion | flops 65536 | bytes 524288 | tf_op jit(solution)/shard_map/transpose | solution.py:451
  (1 shorter events, 0.0 us)
Async XLA Ops:
  0.6 22.0 %copy-start.2 = (f32[4096,16]{0,1:T(8,128)S(1)}, f32[4096,16]{0,1:T(8,128)}, u32[]{:S(2)}) copy-start(f32[4096,16]{0,1:T(8,128)} %param.10) | copy-start | bytes 786436
  0.6 22.0 %copy-start.4 = (f32[4096,16]{0,1:T(8,128)S(1)}, f32[4096,16]{0,1:T(8,128)}, u32[]{:S(2)}) copy-start(f32[4096,16]{0,1:T(8,128)} %param.9) | copy-start | bytes 786436
  0.7 22.0 %copy-start.5 = (f32[4096]{0:T(1024)S(1)}, f32[4096]{0:T(1024)}, u32[]{:S(2)}) copy-start(f32[4096]{0:T(1024)} %param.11) | copy-start | bytes 49156
  6.1 16.6 %copy-start = (bf16[2048,128]{1,0:T(8,128)(2,1)S(1)}, bf16[2048,128]{1,0:T(8,128)(2,1)}, u32[]{:S(2)}) copy-start(bf16[2048,128]{1,0:T(8,128)(2,1)} %gated_ref) | copy-start | bytes 1572868
  6.1 31.5 %all-to-all-start = ((bf16[128,8,128]{2,1,0:T(8,128)(2,1)}), bf16[128,8,128]{2,1,0:T(8,128)(2,1)S(1)}, u32[]{:S(2)}, u32[]{:S(2)}) async-start(bf16[128,8,128]{2,1,0:T(8,128)(2,1)} %bitcast.17), calls=%async_computation | async-start | bytes 524288 | tf_op jit(solution)/shard_map/all_to_all | solution.py:395
  38.8 21.2 %all-to-all-start.1 = ((bf16[128,8,128]{2,1,0:T(8,128)(2,1)}), bf16[128,8,128]{2,1,0:T(8,128)(2,1)S(1)}, u32[]{:S(2)}, u32[]{:S(2)}) async-start(bf16[128,8,128]{2,1,0:T(8,128)(2,1)} %bitcast.5), calls=%async_computation.1 | async-start | bytes 524288 | tf_op jit(solution)/shard_map/all_to_all | solution.py:395
  45.0 1.0 %copy-start.3 = (bf16[2048,128]{1,0:T(8,128)(2,1)S(1)}, bf16[2048,128]{1,0:T(8,128)(2,1)}, u32[]{:S(2)}) copy-start(bf16[2048,128]{1,0:T(8,128)(2,1)} %get-tuple-element.23.dz_ref) | copy-start | bytes 1572868
  46.0 14.5 %copy-start.1 = (bf16[2048,128]{1,0:T(8,128)(2,1)S(1)}, bf16[2048,128]{1,0:T(8,128)(2,1)}, u32[]{:S(2)}) copy-start(bf16[2048,128]{1,0:T(8,128)(2,1)} %upstream_hbm.3) | copy-start | bytes 1572868
  60.1 4.8 %collective-permute-start = (f32[16,2048]{1,0:T(8,128)S(1)}, f32[16,2048]{1,0:T(8,128)S(1)}, u32[]{:S(2)}, u32[]{:S(2)}) collective-permute-start(f32[16,2048]{1,0:T(8,128)S(1)} %shard_map.90), channel_id=1, source_target_pairs={{0,1},{1,0},{2,3},{3,2},{4,5},{5,4},{6,7},{7,6},{8,9},{9,8},{10,11... | collective-permute-start | bytes 393224 | tf_op jit(solution)/shard_map/ppermute | solution.py:436

commit v3 on v2

--- a/solution.py
+++ b/solution.py
@@ -11,8 +11,10 @@
 BF16 = jnp.bfloat16
 LANES = 128
 GROUP = 8
+KINDS = 3
 PART, UNROLL = 8, 16
 FINAL_UNROLL = 16
+SCAN_UNROLL = 4
 STATE_PART, STATE_UNROLL, RUN = 4, 32, 4
 LIMIT = 56 * 2**20
 
@@ -84,7 +86,7 @@
                 for k, (src, dst) in enumerate(pairs)
             ]
         )
-    for copy in copies[0] + [rate_copy] + [copy for part in copies[1:] for copy in part]:
+    for copy in copies[0] + [rate_copy]:
         copy.start()
     copies[0][0].wait()
     for j in range(GROUP):
@@ -93,6 +95,9 @@
     copies[0][2].wait()
     for j in range(GROUP):
         put_dz(value_ref, upstream_ref, dz_ref, dzts[0], j, j, tokens)
+    for part in copies[1:]:
+        for copy in part:
+            copy.start()
     rate_copy.wait()
     spread_modes(rate_ref, lam, 0, modes, blocks)
     zero = jnp.zeros((GROUP, LANES), F32)
@@ -140,12 +145,13 @@
             x, y, own, _, found = lax.fori_loop(0, tokens // STATE_UNROLL, body, carry)
             lags = found if m0 == 0 else lags
             for k in range(STATE_PART):
-                base = (g * modes + m0 + k) * GROUP * 4
+                base = (m0 + k) * GROUP * 2 * KINDS + g * KINDS
                 term = decay[k] * own[k] + horner(decay[k], lags[::-1])
-                high = term.astype(BF16).astype(F32)
-                for kind, rows in enumerate((x[k], y[k], high, term - high)):
-                    pack[pl.ds(base + kind, GROUP, stride=4), :] = rows
-            rows = pl.ds((g * modes + m0) * GROUP * 4, STATE_PART * GROUP * 4)
+                for kind, rows in enumerate((x[k], y[k], term)):
+                    pack[pl.ds(base + kind, GROUP, stride=2 * KINDS), :] = rows
+            if g < groups - 1:
+                continue
+            rows = pl.ds(m0 * GROUP * 2 * KINDS, STATE_PART * GROUP * 2 * KINDS)
             stage[rows, :] = pack[rows, :].astype(BF16)
             copy = pltpu.make_async_copy(
                 stage.at[rows, :], out_hbm.at[rows, :], out_sems.at[len(sent)]
@@ -191,8 +197,10 @@
     spread_modes(rate_ref, dec_ref, first, modes, blocks)
     spread_modes(res_ref, gain_ref, first, modes, blocks)
     for h in range(2):
-        own = dec_ref[pl.ds(lax.axis_index("seq") * 2 + h, 1), :]
-        lam_ref[pl.ds(4 * h, 4), :] = jnp.broadcast_to(own, (4, LANES))
+        for g in range(blocks // GROUP):
+            row = g * modes * GROUP + lax.axis_index("seq") // 2 * 2 + h
+            own = dec_ref[pl.ds(row, 1), :]
+            lam_ref[pl.ds(2 * h + g, 1), :] = own
     dec_ref[...] = jnp.exp(-dec_ref[...])
     for g in range(blocks // GROUP):
         for j in range(GROUP):
@@ -211,49 +219,40 @@
         own_sums(modes, tokens, g, dzt, bwd_ref, dec_ref, gain_ref, skip, order)
 
 
-def scan_kernel(chunks, tokens, in_ref, lam_ref, out_hbm, tiles, ahead, behind, stage, sems):
-    tiles[...] = in_ref[...].astype(F32)
+def scan_kernel(chunks, tokens, own_ref, other_ref, lam_ref, out_hbm, sums, outs, stage, sems):
+    core = lax.axis_index("seq") % 2
+    chips = chunks // 2
+    sums[core] = own_ref[...].astype(F32)
+    sums[1 - core] = other_ref[...].astype(F32)
     lam = lam_ref[...]
     step = jnp.exp(lam * (-1.0 * tokens))
-    kind = lax.broadcasted_iota(jnp.int32, (GROUP, LANES), 0) % 4
-    unroll = 8
-    zero = jnp.zeros((GROUP, LANES), F32)
+    zero = jnp.zeros((4, LANES), F32)
+
+    def at(q, kind):
+        return pl.ds(q * 4 * KINDS + kind, 4, stride=KINDS)
 
     def body(i, carry):
-        fwd, bwd, own, cross = carry
-        for u in range(unroll):
-            d = i * unroll + u
-            e = chunks - 1 - d
-            here, there = tiles[tile(d), :], tiles[tile(e), :]
-            ahead[tile(d), :] = fwd
-            behind[tile(e), :] = bwd
-            own = own + here
-            cross = cross + here * pltpu.roll(fwd, 1, 0)
-            fwd = step * fwd + here
-            bwd = step * bwd + there
-        return fwd, bwd, own, cross
-
-    _, _, own, cross = lax.fori_loop(0, chunks // unroll, body, (zero, zero, zero, zero))
-    cross = cross * jnp.exp(-lam)
-    grad = own + pltpu.roll(own, GROUP - 1, 0) + pltpu.roll(cross, 1, 0)
-    grad = grad * (1.0 / (chunks * tokens))
-    high = grad.astype(BF16).astype(F32)
-    tail = jnp.where(kind == 2, high, pltpu.roll(grad - high, 1, 0))
-    quarter = chunks // 4
+        x, y, own, cross = carry
+        for u in range(SCAN_UNROLL):
+            q, r = i * SCAN_UNROLL + u, chips - 1 - i * SCAN_UNROLL - u
+            for place in range(2):
+                outs[place, at(q, 0), :] = x
+                outs[1 - place, at(r, 1), :] = y
+                own = own + sums[place, at(q, 2), :]
+                cross = cross + sums[place, at(q, 1), :] * x
+                x = step * x + sums[place, at(q, 0), :]
+                y = step * y + sums[1 - place, at(r, 1), :]
+        return x, y, own, cross
+
+    _, _, own, cross = lax.fori_loop(0, chips // SCAN_UNROLL, body, (zero, zero, zero, zero))
+    grad = (own + cross * jnp.exp(-lam)) * (1.0 / (chunks * tokens))
     sent = []
+    quarter = chips // 4
     for part in range(4):
-        for pair in range(quarter // 2):
-            d = part * quarter + 2 * pair
-            both = [
-                jnp.where(
-                    kind == 0,
-                    ahead[pl.ds(e * GROUP, GROUP), :],
-                    jnp.where(kind == 1, behind[pl.ds(e * GROUP, GROUP), :], tail),
-                )
-                for e in (d, d + 1)
-            ]
-            stage[pl.ds(d * GROUP, 2 * GROUP), :] = jnp.concatenate(both, axis=0).astype(BF16)
-        rows = pl.ds(part * quarter * GROUP, quarter * GROUP)
+        for q in range(part * quarter, (part + 1) * quarter):
+            outs[core, at(q, 2), :] = grad
+        rows = pl.ds(part * quarter * 4 * KINDS, quarter * 4 * KINDS)
+        stage[rows, :] = outs[core, rows, :].astype(BF16)
         copy = pltpu.make_async_copy(stage.at[rows, :], out_hbm.at[rows, :], sems.at[part])
         copy.start()
         sent.append(copy)
@@ -261,16 +260,16 @@
         copy.wait()
 
 
-def residue_kernel(modes, blocks, in_ref, out_ref, tiles, flat):
+def residue_kernel(modes, blocks, in_ref, out_ref, wire_ref, tiles, flat):
     tiles[...] = in_ref[...].astype(F32)
     for r in range(modes * blocks // GROUP):
-        base = r * GROUP * 4
-        flat[pl.ds(r * GROUP, GROUP), :] = (
-            tiles[pl.ds(base + 2, GROUP, stride=4), :] + tiles[pl.ds(base + 3, GROUP, stride=4), :]
-        )
+        base = r % modes * GROUP * 2 * KINDS + r // modes * KINDS
+        flat[pl.ds(r * GROUP, GROUP), :] = tiles[pl.ds(base + 2, GROUP, stride=2 * KINDS), :]
     for b in range(blocks):
         row = b // GROUP * modes * GROUP + b % GROUP
-        out_ref[:, pl.ds(b * LANES, LANES)] = flat[pl.ds(row, modes, stride=GROUP), :]
+        found = flat[pl.ds(row, modes, stride=GROUP), :]
+        out_ref[:, pl.ds(b * LANES, LANES)] = found
+        wire_ref[:, pl.ds(b * LANES, LANES)] = found.astype(BF16)
 
 
 def final_kernel(
@@ -303,9 +302,9 @@
         scale = [gain_ref[tile(g * modes + m), :] * decay[m] for m in range(modes)]
 
         def entering(kind, g=g, scale=scale):
+            bases = [m * GROUP * 2 * KINDS + g * KINDS + kind for m in range(modes)]
             return [
-                tiles[pl.ds((g * modes + m) * GROUP * 4 + kind, GROUP, stride=4), :] * scale[m]
-                for m in range(modes)
+                tiles[pl.ds(base, GROUP, stride=2 * KINDS), :] * a for base, a in zip(bases, scale)
             ]
 
         def ahead(i, x, g=g, decay=decay):
@@ -350,7 +349,7 @@
     pairs = modes * blocks
     groups = blocks // GROUP
     assert tokens == LANES == UNROLL * GROUP and pairs == 2 * chunks
-    assert blocks % GROUP == 0 and modes == 2 * PART and chunks % 8 == 0
+    assert blocks == 2 * GROUP and modes == 2 * PART and chunks % (2 * SCAN_UNROLL) == 0
     rate_t, residue_t, skip = rate.T, residue.T, skip_weight[None, :]
     vmem = pl.BlockSpec(memory_space=pltpu.VMEM)
     hbm = pl.BlockSpec(memory_space=pltpu.HBM)
@@ -370,7 +369,7 @@
     native = ((channels, tokens), BF16)
     signal = ((tokens * blocks, LANES), F32)
     per_mode = ((pairs, LANES), F32)
-    wire = (chunks * GROUP, LANES)
+    wire = (chunks * 2 * KINDS, LANES)
     one = pltpu.VMEM((tokens * GROUP, LANES), F32)
     raw = pltpu.VMEM(*native)
     unpacked = pltpu.VMEM(wire, F32)
@@ -383,7 +382,7 @@
         [hbm] * 2,
         [(wire, BF16), native],
         [raw, raw, raw, raw, pltpu.VMEM((modes, channels), F32), [one] * groups, [one] * groups]
-        + [flat, unpacked, staged, sems(3 * groups + 1), sems(pairs // GROUP // STATE_PART)]
+        + [flat, unpacked, staged, sems(3 * groups + 1), sems(modes // STATE_PART)]
         + [sems(groups)],
         5 * cells,
         8 * channels * tokens,
@@ -391,28 +390,34 @@
     )(gated, value, upstream, rate_t)
 
     def exchange(array):
-        array = array.reshape(chunks, GROUP, LANES)
-        return lax.all_to_all(array, "seq", split_axis=0, concat_axis=0, tiled=True).reshape(wire)
+        array = array.reshape(chunks // 2, KINDS, 4, LANES)
+        members = [list(range(core, chunks, 2)) for core in range(2)]
+        return lax.all_to_all(
+            array, "seq", split_axis=0, concat_axis=0, axis_index_groups=members, tiled=True
+        ).reshape(wire)
 
     states, gated_held = lax.optimization_barrier((states, gated))
     fwd, decay, gain, lam = call(
         functools.partial(ahead_kernel, modes, blocks, tokens),
         [vmem] * 4,
         [vmem] * 4,
-        [signal, per_mode, per_mode, ((GROUP, LANES), F32)],
+        [signal, per_mode, per_mode, ((4, LANES), F32)],
         [one],
         4 * cells,
         6 * channels * tokens,
     )(gated_held, rate_t, residue_t, skip)
+    heard, fwd, lam = lax.optimization_barrier((exchange(states), fwd, lam))
+    heard_other = lax.ppermute(heard, "seq", [(d, d ^ 1) for d in range(chunks)])
+    chained = pltpu.VMEM((2,) + wire, F32)
     (entering,) = call(
         functools.partial(scan_kernel, chunks, tokens),
-        [vmem] * 2,
+        [vmem] * 3,
         [hbm],
         [(wire, BF16)],
-        [unpacked, unpacked, unpacked, staged, sems(4)],
+        [chained, chained, staged, sems(4)],
+        16 * chunks * GROUP * LANES,
         8 * chunks * GROUP * LANES,
-        4 * chunks * GROUP * LANES,
-    )(exchange(states), lam)
+    )(heard, heard_other, lam)
     entering, dz_held = lax.optimization_barrier((entering, dz))
     (bwd,) = call(
         functools.partial(behind_kernel, modes, blocks, tokens),
@@ -424,16 +429,16 @@
         6 * channels * tokens,
     )(dz_held, decay, gain, skip)
     returned, bwd = lax.optimization_barrier((exchange(entering), bwd))
-    (grad_own,) = call(
+    grad_own, grad_wire = call(
         functools.partial(residue_kernel, modes, blocks),
         [vmem],
-        [vmem],
-        [((modes, channels), F32)],
+        [vmem] * 2,
+        [((modes, channels), F32), ((modes, channels), BF16)],
         [unpacked, flat],
         modes * channels,
         8 * modes * channels,
     )(returned)
-    grad_other = lax.ppermute(grad_own, "ch", [(0, 1), (1, 0)])
+    grad_other = lax.ppermute(grad_wire, "ch", [(0, 1), (1, 0)]).astype(F32)
     grad_gated, grad_value = call(
         functools.partial(final_kernel, modes, blocks, tokens),
         [vmem, vmem, hbm, vmem, vmem, hbm],

time: 65.9 us -> 61.7 us (0.936)
  waiting for transfers between devices: 23.8 us -> 19.7 us
    all_to_all x2, waiting for transfers between devices: 23.4 us -> 18.6 us  [exchange(): lax.all_to_all(array, 'seq', split_axis=0, concat_axis=0, axis_index_grou...]
    all_to_all x2, starting transfers between devices: 22.8 us -> 19.9 us  [exchange(): lax.all_to_all(array, 'seq', split_axis=0, concat_axis=0, axis_index_grou...]
    ppermute x1 -> x2, starting transfers between devices: 0.48 us -> 2.94 us  [the longest x1 2.46 us: local(): lax.ppermute(heard, 'seq', [(d, d ^ 1) for d in range(chunks)])]
    ppermute x1 -> x2, waiting for transfers between devices: 0.4 us -> 1.07 us  [the longest x1 1.07 us: local(): lax.ppermute(heard, 'seq', [(d, d ^ 1) for d in range(chunks)])]
  transfers between devices with their start and end apart: 3 -> 4, of which waited for: 3 -> 3; matrix products, arithmetic and copies ran while one was open for 0% -> 0% of each run, Pallas kernels for 14% -> 15%
where the time goes in v3:
time: 61.7 us; the launch traced here: 61.1 us
  starting transfers between devices  22.8 us (37%)
  waiting for transfers between devices  19.7 us (32%)
  Pallas kernels  16 us (26%)
  local copies, waits for them, and re-layouts  1.06 us (2%)
  between operations  0.77 us (1%)
  other arithmetic  0.74 us (1%)
    all_to_all x2, starting transfers between devices, exchange(): lax.all_to_all(array, 'seq', split_axis=0, concat_axis=0, axis_index_grou...  19.9 us
    all_to_all x2, waiting for transfers between devices, exchange(): lax.all_to_all(array, 'seq', split_axis=0, concat_axis=0, axis_index_grou...  18.6 us
    pallas_call x1, Pallas kernels, local(): call(functools.partial(state_kernel, modes, blocks, tokens), [hbm] * 4, [...  5.33 us
    pallas_call x1, Pallas kernels, local(): call(functools.partial(final_kernel, modes, blocks, tokens), [vmem, vmem,...  3.93 us
    pallas_call x1, Pallas kernels, local(): call(functools.partial(behind_kernel, modes, blocks, tokens), [vmem] * 4,...  2.82 us
    pallas_call x1, Pallas kernels, local(): call(functools.partial(ahead_kernel, modes, blocks, tokens), [vmem] * 4,...  2.7 us
    ppermute x1, starting transfers between devices, local(): lax.ppermute(heard, 'seq', [(d, d ^ 1) for d in range(chunks)])  2.46 us
  transfers between devices with their start and end apart: 4, of which 3 were waited for; matrix products, arithmetic and copies ran while one was open for 0% of the time, Pallas kernels for 15%

profile of v3, /device:TPU:1, one launch (start us, length us, event | category | flops | bytes accessed | tf_op | source)
XLA Modules:
  0.0 61.1 jit_solution(15658321362628722159)
XLA Ops:
  0.6 0.0 copy-start
  0.6 0.0 copy-start.4
  0.7 5.3 %shard_map.85 = (bf16[768,128]{1,0:T(8,128)(2,1)}, bf16[2048,128]{1,0:T(8,128)(2,1)}) custom-call(bf16[2048,128]{1,0:T(8,128)(2,1)} %gated_ref, bf16[2048,128]{1,0:T(8,128)(2,1)} %value_hbm.1, bf16[2048,128]{1,0:T(8,128)(2,1)} %upstream_hbm.3, f32[16,4096]{1,0:T(8,128)} %bitcast.11), custom_call_target="tpu_custom_call" | custom-call | flops 20971520 | bytes 2097152 | tf_op jit(solution)/shard_map/pallas_call | solution.py:379
  6.0 0.0 copy-start.2
  6.0 0.0 copy-start.5
  6.0 15.3 %all-to-all-start = ((bf16[64,3,4,128]{3,2,1,0:T(4,128)(2,1)}), bf16[64,3,4,128]{3,2,1,0:T(4,128)(2,1)S(1)}, u32[]{:S(2)}, u32[]{:S(2)}) async-start(bf16[64,3,4,128]{3,2,1,0:T(4,128)(2,1)} %bitcast.18), calls=%async_computation | async-start | bytes 393216 | tf_op jit(solution)/shard_map/all_to_all | solution.py:395
  21.3 0.0 copy-done
  21.3 0.0 copy-done.4
  21.3 0.0 copy-done.2
  21.3 0.0 copy-done.5
  21.3 2.7 %shard_map.86 = (f32[2048,128]{1,0:T(8,128)S(1)}, f32[256,128]{1,0:T(8,128)S(1)}, f32[256,128]{1,0:T(8,128)S(1)}, f32[4,128]{1,0:T(4,128)S(1)}) custom-call(bf16[2048,128]{1,0:T(8,128)(2,1)S(1)} %copy-done, f32[16,4096]{1,0:T(8,128)S(1)} %bitcast.12, f32[16,4096]{1,0:T(8,128)S(1)} %bitcast.15, f32[1,4096]{1,0:T(1,128)S(1)} %bitcast.16), custom_call_target="tpu_custom_call" | custom-call | flops 16777216 | bytes 1572864 | tf_op jit(solution)/shard_map/pallas_call | solution.py:400
  24.0 9.5 %all-to-all-done = bf16[64,3,4,128]{3,2,1,0:T(4,128)(2,1)S(1)} async-done(((bf16[64,3,4,128]{3,2,1,0:T(4,128)(2,1)}), bf16[64,3,4,128]{3,2,1,0:T(4,128)(2,1)S(1)}, u32[]{:S(2)}, u32[]{:S(2)}) %all-to-all-start) | async-done | bytes 196640 | tf_op jit(solution)/shard_map/all_to_all | solution.py:395
  33.5 2.5 %collective-permute-start = (bf16[768,128]{1,0:T(8,128)(2,1)S(1)}, bf16[768,128]{1,0:T(8,128)(2,1)S(1)}, u32[]{:S(2)}, u32[]{:S(2)}) collective-permute-start(bf16[768,128]{1,0:T(8,128)(2,1)S(1)} %bitcast.13), channel_id=1, source_target_pairs={{0,2},{2,0},{4,6},{6,4},{8,10},{10,8},{12,14},{14,12},{16,18},{18,... | collective-permute-start | bytes 589832 | tf_op jit(solution)/shard_map/ppermute | solution.py:410
  36.0 1.1 %collective-permute-done.other_ref = bf16[768,128]{1,0:T(8,128)(2,1)S(1)} collective-permute-done((bf16[768,128]{1,0:T(8,128)(2,1)S(1)}, bf16[768,128]{1,0:T(8,128)(2,1)S(1)}, u32[]{:S(2)}, u32[]{:S(2)}) %collective-permute-start) | collective-permute-done | bytes 196640 | tf_op jit(solution)/shard_map/ppermute | solution.py:410
  37.1 1.1 %shard_map.87 = bf16[768,128]{1,0:T(8,128)(2,1)} custom-call(bf16[768,128]{1,0:T(8,128)(2,1)S(1)} %bitcast.14, bf16[768,128]{1,0:T(8,128)(2,1)S(1)} %collective-permute-done.other_ref, f32[4,128]{1,0:T(4,128)S(1)} %get-tuple-element.28.lam_ref), custom_call_target="tpu_custom_call" | custom-call | flops 2097152 | bytes 1048576 | tf_op jit(solution)/shard_map/pallas_call | solution.py:412
  38.2 4.6 %all-to-all-start.1 = ((bf16[64,3,4,128]{3,2,1,0:T(4,128)(2,1)}), bf16[64,3,4,128]{3,2,1,0:T(4,128)(2,1)S(1)}, u32[]{:S(2)}, u32[]{:S(2)}) async-start(bf16[64,3,4,128]{3,2,1,0:T(4,128)(2,1)} %bitcast.5), calls=%async_computation.1 | async-start | bytes 393216 | tf_op jit(solution)/shard_map/all_to_all | solution.py:395
  42.9 0.0 copy-start.3
  42.9 1.0 %copy-done.3 = bf16[2048,128]{1,0:T(8,128)(2,1)S(1)} copy-done((bf16[2048,128]{1,0:T(8,128)(2,1)S(1)}, bf16[2048,128]{1,0:T(8,128)(2,1)}, u32[]{:S(2)}) %copy-start.3) | copy-done | bytes 524312
  43.9 0.0 copy-start.1
  43.9 2.8 %shard_map.88.bwd_hbm = f32[2048,128]{1,0:T(8,128)S(1)} custom-call(bf16[2048,128]{1,0:T(8,128)(2,1)S(1)} %copy-done.3, f32[256,128]{1,0:T(8,128)S(1)} %get-tuple-element.32.dec_ref, f32[256,128]{1,0:T(8,128)S(1)} %get-tuple-element.33.gain_ref, f32[1,4096]{1,0:T(1,128)S(1)} %bitcast.17), custom_call_target="tpu_custom_call" | custom-call | flops 16777216 | bytes 1572864 | tf_op jit(solution)/shard_map/pallas_call | solution.py:422
  46.7 9.1 %all-to-all-done.1 = bf16[64,3,4,128]{3,2,1,0:T(4,128)(2,1)S(1)} async-done(((bf16[64,3,4,128]{3,2,1,0:T(4,128)(2,1)}), bf16[64,3,4,128]{3,2,1,0:T(4,128)(2,1)S(1)}, u32[]{:S(2)}, u32[]{:S(2)}) %all-to-all-start.1) | async-done | bytes 196640 | tf_op jit(solution)/shard_map/all_to_all | solution.py:395
  55.8 0.1 shard_map.90
  55.9 0.5 collective-permute-start.1
  56.4 0.0 copy-done.1
  56.4 3.9 %shard_map.89 = (bf16[2048,128]{1,0:T(8,128)(2,1)}, bf16[2048,128]{1,0:T(8,128)(2,1)}) custom-call(bf16[768,128]{1,0:T(8,128)(2,1)S(1)} %bitcast.10, f32[2048,128]{1,0:T(8,128)S(1)} %get-tuple-element.35.fwd_ref, f32[2048,128]{1,0:T(8,128)S(1)} %shard_map.88.bwd_hbm, f32[256,128]{1,0:T(8,128)S(1)} %get-tuple-element.32.dec_ref, ...), custom_call_target="tpu_custom_call" | custom-call | flops 16777216 | bytes 3670016 | tf_op jit(solution)/shard_map/pallas_call | solution.py:442
  60.3 0.0 collective-permute-done.1
  60.4 0.7 %maximum_bitcast_fusion = f32[4096,16]{0,1:T(8,128)} fusion(f32[16,2048]{1,0:T(8,128)S(1)} %get-tuple-element.42, f32[16,2048]{1,0:T(8,128)S(1)} %get-tuple-element.41), kind=kLoop, calls=%fused_computation | loop fusion | flops 65536 | bytes 524288 | tf_op jit(solution)/shard_map/transpose | solution.py:456
  (1 shorter events, 0.0 us)
Async XLA Ops:
  0.6 20.7 %copy-start = (bf16[2048,128]{1,0:T(8,128)(2,1)S(1)}, bf16[2048,128]{1,0:T(8,128)(2,1)}, u32[]{:S(2)}) copy-start(bf16[2048,128]{1,0:T(8,128)(2,1)} %gated_ref) | copy-start | bytes 1572868
  0.6 20.7 %copy-start.4 = (f32[4096,16]{0,1:T(8,128)S(1)}, f32[4096,16]{0,1:T(8,128)}, u32[]{:S(2)}) copy-start(f32[4096,16]{0,1:T(8,128)} %param.9) | copy-start | bytes 786436
  6.0 15.3 %copy-start.2 = (f32[4096,16]{0,1:T(8,128)S(1)}, f32[4096,16]{0,1:T(8,128)}, u32[]{:S(2)}) copy-start(f32[4096,16]{0,1:T(8,128)} %param.10) | copy-start | bytes 786436
  6.0 15.3 %copy-start.5 = (f32[4096]{0:T(1024)S(1)}, f32[4096]{0:T(1024)}, u32[]{:S(2)}) copy-start(f32[4096]{0:T(1024)} %param.11) | copy-start | bytes 49156
  6.0 27.5 %all-to-all-start = ((bf16[64,3,4,128]{3,2,1,0:T(4,128)(2,1)}), bf16[64,3,4,128]{3,2,1,0:T(4,128)(2,1)S(1)}, u32[]{:S(2)}, u32[]{:S(2)}) async-start(bf16[64,3,4,128]{3,2,1,0:T(4,128)(2,1)} %bitcast.18), calls=%async_computation | async-start | bytes 393216 | tf_op jit(solution)/shard_map/all_to_all | solution.py:395
  33.5 3.5 %collective-permute-start = (bf16[768,128]{1,0:T(8,128)(2,1)S(1)}, bf16[768,128]{1,0:T(8,128)(2,1)S(1)}, u32[]{:S(2)}, u32[]{:S(2)}) collective-permute-start(bf16[768,128]{1,0:T(8,128)(2,1)S(1)} %bitcast.13), channel_id=1, source_target_pairs={{0,2},{2,0},{4,6},{6,4},{8,10},{10,8},{12,14},{14,12},{16,18},{18,... | collective-permute-start | bytes 589832 | tf_op jit(solution)/shard_map/ppermute | solution.py:410
  38.2 17.6 %all-to-all-start.1 = ((bf16[64,3,4,128]{3,2,1,0:T(4,128)(2,1)}), bf16[64,3,4,128]{3,2,1,0:T(4,128)(2,1)S(1)}, u32[]{:S(2)}, u32[]{:S(2)}) async-start(bf16[64,3,4,128]{3,2,1,0:T(4,128)(2,1)} %bitcast.5), calls=%async_computation.1 | async-start | bytes 393216 | tf_op jit(solution)/shard_map/all_to_all | solution.py:395
  42.9 1.0 %copy-start.3 = (bf16[2048,128]{1,0:T(8,128)(2,1)S(1)}, bf16[2048,128]{1,0:T(8,128)(2,1)}, u32[]{:S(2)}) copy-start(bf16[2048,128]{1,0:T(8,128)(2,1)} %get-tuple-element.31.dz_ref) | copy-start | bytes 1572868
  43.9 12.5 %copy-start.1 = (bf16[2048,128]{1,0:T(8,128)(2,1)S(1)}, bf16[2048,128]{1,0:T(8,128)(2,1)}, u32[]{:S(2)}) copy-start(bf16[2048,128]{1,0:T(8,128)(2,1)} %upstream_hbm.3) | copy-start | bytes 1572868
  55.9 4.4 %collective-permute-start.1 = (bf16[16,2048]{1,0:T(8,128)(2,1)S(1)}, bf16[16,2048]{1,0:T(8,128)(2,1)S(1)}, u32[]{:S(2)}, u32[]{:S(2)}) collective-permute-start(bf16[16,2048]{1,0:T(8,128)(2,1)S(1)} %get-tuple-element.40), channel_id=1, source_target_pairs={{0,1},{1,0},{2,3},{3,2},{4,5},{5,4},{6,7},{7,6},{8,9},{9,8},{10,11... | collective-permute-start | bytes 196616 | tf_op jit(solution)/shard_map/ppermute | solution.py:441

commit v4 on v3

--- a/solution.py
+++ b/solution.py
@@ -67,8 +67,8 @@
 
 
 def state_kernel(
-    modes, blocks, tokens, gated_hbm, value_hbm, upstream_hbm, rate_hbm, out_hbm, dz_hbm,
-    gated_ref, value_ref, upstream_ref, dz_ref, rate_ref, gts, dzts, lam, pack, stage, sems, out_sems, dz_sems
+    modes, blocks, tokens, gated_hbm, value_hbm, upstream_hbm, rate_hbm, out_hbm, dz_hbm, edge_hbm,
+    gated_ref, value_ref, upstream_ref, dz_ref, rate_ref, gts, dzts, lam, pack, stage, edge, sems, out_sems, dz_sems
 ):
     half = GROUP * LANES
     groups = blocks // GROUP
@@ -102,6 +102,7 @@
     spread_modes(rate_ref, lam, 0, modes, blocks)
     zero = jnp.zeros((GROUP, LANES), F32)
     sent, late = [], []
+    early = jnp.broadcast_to(lax.axis_index("seq") % 2, (GROUP, LANES)) == 0
     for g in range(groups):
         gt, dzt = gts[g], dzts[g]
         if g:
@@ -147,6 +148,7 @@
             for k in range(STATE_PART):
                 base = (m0 + k) * GROUP * 2 * KINDS + g * KINDS
                 term = decay[k] * own[k] + horner(decay[k], lags[::-1])
+                edge[tile(g * modes + m0 + k), :] = jnp.where(early, x[k], y[k])
                 for kind, rows in enumerate((x[k], y[k], term)):
                     pack[pl.ds(base + kind, GROUP, stride=2 * KINDS), :] = rows
             if g < groups - 1:
@@ -158,7 +160,9 @@
             )
             copy.start()
             sent.append(copy)
-    for copy in sent + late:
+    copy = pltpu.make_async_copy(edge, edge_hbm, dz_sems.at[groups])
+    copy.start()
+    for copy in sent + late + [copy]:
         copy.wait()
 
 
@@ -219,7 +223,7 @@
         own_sums(modes, tokens, g, dzt, bwd_ref, dec_ref, gain_ref, skip, order)
 
 
-def scan_kernel(chunks, tokens, own_ref, other_ref, lam_ref, out_hbm, sums, outs, stage, sems):
+def scan_kernel(chunks, tokens, own_ref, other_ref, lam_ref, out_ref, sums, outs, grads):
     core = lax.axis_index("seq") % 2
     chips = chunks // 2
     sums[core] = own_ref[...].astype(F32)
@@ -235,9 +239,10 @@
         x, y, own, cross = carry
         for u in range(SCAN_UNROLL):
             q, r = i * SCAN_UNROLL + u, chips - 1 - i * SCAN_UNROLL - u
+            for h in range(2):
+                outs[0, pl.ds(q * 6 + 3 * h, 2), :] = x[2 * h : 2 * h + 2]
+                outs[1, pl.ds(r * 6 + 3 * h, 2), :] = y[2 * h : 2 * h + 2]
             for place in range(2):
-                outs[place, at(q, 0), :] = x
-                outs[1 - place, at(r, 1), :] = y
                 own = own + sums[place, at(q, 2), :]
                 cross = cross + sums[place, at(q, 1), :] * x
                 x = step * x + sums[place, at(q, 0), :]
@@ -245,26 +250,19 @@
         return x, y, own, cross
 
     _, _, own, cross = lax.fori_loop(0, chips // SCAN_UNROLL, body, (zero, zero, zero, zero))
-    grad = (own + cross * jnp.exp(-lam)) * (1.0 / (chunks * tokens))
-    sent = []
-    quarter = chips // 4
-    for part in range(4):
-        for q in range(part * quarter, (part + 1) * quarter):
-            outs[core, at(q, 2), :] = grad
-        rows = pl.ds(part * quarter * 4 * KINDS, quarter * 4 * KINDS)
-        stage[rows, :] = outs[core, rows, :].astype(BF16)
-        copy = pltpu.make_async_copy(stage.at[rows, :], out_hbm.at[rows, :], sems.at[part])
-        copy.start()
-        sent.append(copy)
-    for copy in sent:
-        copy.wait()
-
-
-def residue_kernel(modes, blocks, in_ref, out_ref, wire_ref, tiles, flat):
-    tiles[...] = in_ref[...].astype(F32)
-    for r in range(modes * blocks // GROUP):
-        base = r % modes * GROUP * 2 * KINDS + r // modes * KINDS
-        flat[pl.ds(r * GROUP, GROUP), :] = tiles[pl.ds(base + 2, GROUP, stride=2 * KINDS), :]
+    grads[...] = (own + cross * jnp.exp(-lam)) * (1.0 / (chunks * tokens))
+    grad = grads[pl.ds(core, 2, stride=2), :]
+    for q in range(chips):
+        outs[core, pl.ds(q * 6 + 2, 2, stride=3), :] = grad
+    out_ref[...] = outs[core].astype(BF16)
+
+
+def residue_kernel(modes, blocks, own_ref, other_ref, out_ref, wire_ref, tiles, flat):
+    core = lax.axis_index("seq") % 2
+    for k, (ref, g) in enumerate(((own_ref, core), (other_ref, 1 - core))):
+        tiles[k] = ref[...].astype(F32)
+        for m in range(modes):
+            flat[tile(g * modes + m), :] = tiles[k, pl.ds(m * 3 * GROUP + 2, GROUP, stride=3), :]
     for b in range(blocks):
         row = b // GROUP * modes * GROUP + b % GROUP
         found = flat[pl.ds(row, modes, stride=GROUP), :]
@@ -273,7 +271,7 @@
 
 
 def final_kernel(
-    modes, blocks, tokens, in_ref, fwd_ref, bwd_hbm, dec_ref, gain_ref, upstream_hbm,
+    modes, blocks, tokens, own_ref, other_ref, near_ref, fwd_ref, bwd_hbm, dec_ref, gain_ref, upstream_hbm,
     grad_gated_hbm, grad_value_hbm, tiles, zts, gts, bwd_ref, upstream_ref, grad_gated_ref,
     grad_value_ref, in_sems, sems
 ):
@@ -288,7 +286,9 @@
     upstream_copy = pltpu.make_async_copy(upstream_hbm, upstream_ref, in_sems.at[groups])
     for copy in [own_copies[0], upstream_copy] + own_copies[1:]:
         copy.start()
-    tiles[...] = in_ref[...].astype(F32)
+    tiles[0] = own_ref[...].astype(F32)
+    tiles[1] = other_ref[...].astype(F32)
+    odd = jnp.broadcast_to(lax.axis_index("seq") % 2, (GROUP, LANES)) == 1
     copies = []
 
     def send(src, dst, first, size):
@@ -299,13 +299,17 @@
 
     for g in range(groups):
         decay = [dec_ref[tile(g * modes + m), :] for m in range(modes)]
-        scale = [gain_ref[tile(g * modes + m), :] * decay[m] for m in range(modes)]
-
-        def entering(kind, g=g, scale=scale):
-            bases = [m * GROUP * 2 * KINDS + g * KINDS + kind for m in range(modes)]
-            return [
-                tiles[pl.ds(base, GROUP, stride=2 * KINDS), :] * a for base, a in zip(bases, scale)
-            ]
+        left, right = [], []
+        for m in range(modes):
+            rows = pl.ds(m * 3 * GROUP + g, GROUP, stride=3)
+            scale = gain_ref[tile(g * modes + m), :] * decay[m]
+            jump = decay[m]
+            for _ in range(tokens.bit_length() - 1):
+                jump = jump * jump
+            direct = tiles[0, rows, :] * scale
+            across = (tiles[1, rows, :] * jump + near_ref[tile(g * modes + m), :]) * scale
+            left.append(jnp.where(odd, across, direct))
+            right.append(jnp.where(odd, direct, across))
 
         def ahead(i, x, g=g, decay=decay):
             for u in range(FINAL_UNROLL):
@@ -321,7 +325,7 @@
                 y = [a * v for a, v in zip(decay, y)]
             return y
 
-        lax.fori_loop(0, tokens // FINAL_UNROLL, ahead, entering(0))
+        lax.fori_loop(0, tokens // FINAL_UNROLL, ahead, left)
         if g == 0:
             upstream_copy.wait()
         for j in range(GROUP):
@@ -330,7 +334,7 @@
             grad_value_ref[rows, :] = (upstream_ref[rows, :].astype(F32) * z).astype(BF16)
         send(grad_value_ref, grad_value_hbm, g * GROUP, GROUP)
         own_copies[g].wait()
-        lax.fori_loop(0, tokens // FINAL_UNROLL, behind, entering(1))
+        lax.fori_loop(0, tokens // FINAL_UNROLL, behind, right)
         for j in range(GROUP):
             rows = pl.ds(g * half + j * LANES, LANES)
             back = transposed(gts[g][pl.ds(j, tokens, stride=GROUP), :].astype(BF16))
@@ -370,31 +374,36 @@
     signal = ((tokens * blocks, LANES), F32)
     per_mode = ((pairs, LANES), F32)
     wire = (chunks * 2 * KINDS, LANES)
+    answer = (chunks * 3, LANES)
     one = pltpu.VMEM((tokens * GROUP, LANES), F32)
     raw = pltpu.VMEM(*native)
     unpacked = pltpu.VMEM(wire, F32)
     staged = pltpu.VMEM(wire, BF16)
     flat = pltpu.VMEM(*per_mode)
     sems = lambda count: pltpu.SemaphoreType.DMA((count,))
-    states, dz = call(
+    states, dz, edge = call(
         functools.partial(state_kernel, modes, blocks, tokens),
         [hbm] * 4,
-        [hbm] * 2,
-        [(wire, BF16), native],
+        [hbm] * 3,
+        [(wire, BF16), native, per_mode],
         [raw, raw, raw, raw, pltpu.VMEM((modes, channels), F32), [one] * groups, [one] * groups]
-        + [flat, unpacked, staged, sems(3 * groups + 1), sems(modes // STATE_PART)]
-        + [sems(groups)],
+        + [flat, unpacked, staged, flat, sems(3 * groups + 1), sems(modes // STATE_PART)]
+        + [sems(groups + 1)],
         5 * cells,
         8 * channels * tokens,
         LIMIT,
     )(gated, value, upstream, rate_t)
 
     def exchange(array):
-        array = array.reshape(chunks // 2, KINDS, 4, LANES)
+        rows = array.shape[0] // chunks
+        parts = array.reshape(chunks // 2, 3, 2 * rows // 3, LANES)
         members = [list(range(core, chunks, 2)) for core in range(2)]
         return lax.all_to_all(
-            array, "seq", split_axis=0, concat_axis=0, axis_index_groups=members, tiled=True
-        ).reshape(wire)
+            parts, "seq", split_axis=0, concat_axis=0, axis_index_groups=members, tiled=True
+        ).reshape(array.shape)
+
+    def beside(array):
+        return lax.ppermute(array, "seq", [(d, d ^ 1) for d in range(chunks)])
 
     states, gated_held = lax.optimization_barrier((states, gated))
     fwd, decay, gain, lam = call(
@@ -406,19 +415,7 @@
         4 * cells,
         6 * channels * tokens,
     )(gated_held, rate_t, residue_t, skip)
-    heard, fwd, lam = lax.optimization_barrier((exchange(states), fwd, lam))
-    heard_other = lax.ppermute(heard, "seq", [(d, d ^ 1) for d in range(chunks)])
-    chained = pltpu.VMEM((2,) + wire, F32)
-    (entering,) = call(
-        functools.partial(scan_kernel, chunks, tokens),
-        [vmem] * 3,
-        [hbm],
-        [(wire, BF16)],
-        [chained, chained, staged, sems(4)],
-        16 * chunks * GROUP * LANES,
-        8 * chunks * GROUP * LANES,
-    )(heard, heard_other, lam)
-    entering, dz_held = lax.optimization_barrier((entering, dz))
+    fwd, edge, dz = lax.optimization_barrier((fwd, edge, dz))
     (bwd,) = call(
         functools.partial(behind_kernel, modes, blocks, tokens),
         [vmem] * 4,
@@ -427,28 +424,44 @@
         [one],
         4 * cells,
         6 * channels * tokens,
-    )(dz_held, decay, gain, skip)
-    returned, bwd = lax.optimization_barrier((exchange(entering), bwd))
+    )(dz, decay, gain, skip)
+    heard, fwd, bwd, lam, near = lax.optimization_barrier(
+        (exchange(states), fwd, bwd, lam, beside(edge))
+    )
+    heard_other = beside(heard)
+    chained = pltpu.VMEM((2,) + wire, F32)
+    (entering,) = call(
+        functools.partial(scan_kernel, chunks, tokens),
+        [vmem] * 3,
+        [vmem],
+        [(answer, BF16)],
+        [chained, pltpu.VMEM((2,) + answer, F32), pltpu.VMEM((4, LANES), F32)],
+        16 * chunks * GROUP * LANES,
+        8 * chunks * GROUP * LANES,
+    )(heard, heard_other, lam)
+    returned = exchange(entering)
+    returned_other = beside(returned)
     grad_own, grad_wire = call(
         functools.partial(residue_kernel, modes, blocks),
-        [vmem],
+        [vmem] * 2,
         [vmem] * 2,
         [((modes, channels), F32), ((modes, channels), BF16)],
-        [unpacked, flat],
+        [pltpu.VMEM((2,) + answer, F32), flat],
         modes * channels,
         8 * modes * channels,
-    )(returned)
+    )(returned, returned_other)
     grad_other = lax.ppermute(grad_wire, "ch", [(0, 1), (1, 0)]).astype(F32)
     grad_gated, grad_value = call(
         functools.partial(final_kernel, modes, blocks, tokens),
-        [vmem, vmem, hbm, vmem, vmem, hbm],
+        [vmem, vmem, vmem, vmem, hbm, vmem, vmem, hbm],
         [hbm] * 2,
         [native, native],
-        [unpacked, [one] * groups, [one] * groups, pltpu.VMEM(*signal), raw, raw, raw]
+        [pltpu.VMEM((2,) + answer, F32), [one] * groups, [one] * groups]
+        + [pltpu.VMEM(*signal), raw, raw, raw]
         + [sems(groups + 1), sems(3 * groups)],
         4 * cells,
         14 * channels * tokens,
-    )(returned, fwd, bwd, decay, gain, upstream)
+    )(returned, returned_other, near, fwd, bwd, decay, gain, upstream)
     low = lax.axis_index("ch") == 0
     grad_res = jnp.concatenate(
         [jnp.where(low, grad_own, grad_other), jnp.where(low, grad_other, grad_own)], axis=1

time: 61.7 us -> 61.7 us (level)
  blocking collectives: 0 us -> 16.2 us
  waiting for transfers between devices: 19.7 us -> 7.6 us
  starting transfers between devices: 22.8 us -> 20.8 us
  local copies, waits for them, and re-layouts: 1.06 us -> 0.04 us
  Pallas kernels: 16 us -> 15.3 us
    all_to_all x0 -> x1, blocking collectives: none -> 16.2 us  [exchange(): lax.all_to_all(parts, 'seq', split_axis=0, concat_axis=0, axis_index_grou...]
    all_to_all x2 -> x1, waiting for transfers between devices: 18.6 us -> 5.58 us  [exchange(): lax.all_to_all(parts, 'seq', split_axis=0, concat_axis=0, axis_index_grou...]
    all_to_all x2 -> x1, starting transfers between devices: 19.9 us -> 15.3 us  [exchange(): lax.all_to_all(parts, 'seq', split_axis=0, concat_axis=0, axis_index_grou...]
    ppermute x1 -> x3, starting transfers between devices: 2.46 us -> 5.09 us  [beside(): return lax.ppermute(array, 'seq', [(d, d ^ 1) for d in range(chunks)])]
    unnamed x12 -> x14, local copies, waits for them, and re-layouts: 1.06 us -> 0.04 us
    ppermute x1 -> x3, waiting for transfers between devices: 1.07 us -> 2.02 us  [beside(): return lax.ppermute(array, 'seq', [(d, d ^ 1) for d in range(chunks)])]
    pallas_call x2, Pallas kernels: 1.22 us -> 0.52 us  [the longest x1 0.44 us: local(): call(functools.partial(scan_kernel, chunks, tokens), [vmem] * 3, [vmem],...]
  transfers between devices with their start and end apart: 4 -> 5, of which waited for: 3 -> 3; matrix products, arithmetic and copies ran while one was open for 0% -> 0% of each run, Pallas kernels for 15% -> 15%
where the time goes in v4:
time: 61.7 us; the launch traced here: 61.5 us
  starting transfers between devices  20.8 us (34%)
  blocking collectives  16.2 us (26%)
  Pallas kernels  15.3 us (25%)
  waiting for transfers between devices  7.6 us (12%)
  between operations  0.79 us (1%)
  other arithmetic  0.74 us (1%)
    all_to_all x1, blocking collectives, exchange(): lax.all_to_all(parts, 'seq', split_axis=0, concat_axis=0, axis_index_grou...  16.2 us
    all_to_all x1, starting transfers between devices, exchange(): lax.all_to_all(parts, 'seq', split_axis=0, concat_axis=0, axis_index_grou...  15.3 us
    all_to_all x1, waiting for transfers between devices, exchange(): lax.all_to_all(parts, 'seq', split_axis=0, concat_axis=0, axis_index_grou...  5.58 us
    pallas_call x1, Pallas kernels, local(): call(functools.partial(state_kernel, modes, blocks, tokens), [hbm] * 4, [...  5.38 us
    ppermute x3, starting transfers between devices, beside(): return lax.ppermute(array, 'seq', [(d, d ^ 1) for d in range(chunks)])  5.09 us
    pallas_call x1, Pallas kernels, local(): call(functools.partial(final_kernel, modes, blocks, tokens), [vmem, vmem,...  3.94 us
    pallas_call x1, Pallas kernels, local(): call(functools.partial(behind_kernel, modes, blocks, tokens), [vmem] * 4,...  2.82 us
    pallas_call x1, Pallas kernels, local(): call(functools.partial(ahead_kernel, modes, blocks, tokens), [vmem] * 4,...  2.7 us
  transfers between devices with their start and end apart: 5, of which 3 were waited for; matrix products, arithmetic and copies ran while one was open for 0% of the time, Pallas kernels for 15%

profile of v4, /device:TPU:1, one launch (start us, length us, event | category | flops | bytes accessed | tf_op | source)
XLA Modules:
  0.0 61.5 jit_solution(7605821425467055031)
XLA Ops:
  0.6 0.0 copy-start.1
  0.6 0.0 copy-start.4
  0.7 5.4 %shard_map.85 = (bf16[768,128]{1,0:T(8,128)(2,1)}, bf16[2048,128]{1,0:T(8,128)(2,1)}, f32[256,128]{1,0:T(8,128)}) custom-call(bf16[2048,128]{1,0:T(8,128)(2,1)} %gated_ref, bf16[2048,128]{1,0:T(8,128)(2,1)} %value_hbm.1, bf16[2048,128]{1,0:T(8,128)(2,1)} %upstream_hbm.3, f32[16,4096]{1,0:T(8,128)} %bitcast.9), custom_call_target="tpu_custom_call" | custom-call | flops 20971520 | bytes 2097152 | tf_op jit(solution)/shard_map/pallas_call | solution.py:384
  6.0 0.0 copy-start.2
  6.0 0.0 copy-start.5
  6.1 15.3 %all-to-all-start = ((bf16[64,3,4,128]{3,2,1,0:T(4,128)(2,1)}), bf16[64,3,4,128]{3,2,1,0:T(4,128)(2,1)S(1)}, u32[]{:S(2)}, u32[]{:S(2)}) async-start(bf16[64,3,4,128]{3,2,1,0:T(4,128)(2,1)} %bitcast.20), calls=%async_computation | async-start | bytes 393216 | tf_op jit(solution)/shard_map/all_to_all | solution.py:401
  21.3 0.0 copy-done.1
  21.3 0.0 copy-done.4
  21.3 0.0 copy-done.2
  21.4 0.0 copy-done.5
  21.4 0.0 copy-start.6
  21.4 0.0 copy-start.3
  21.4 2.7 %shard_map.86 = (f32[2048,128]{1,0:T(8,128)S(1)}, f32[256,128]{1,0:T(8,128)S(1)}, f32[256,128]{1,0:T(8,128)S(1)}, f32[4,128]{1,0:T(4,128)S(1)}) custom-call(bf16[2048,128]{1,0:T(8,128)(2,1)S(1)} %copy-done.1, f32[16,4096]{1,0:T(8,128)S(1)} %bitcast.10, f32[16,4096]{1,0:T(8,128)S(1)} %bitcast.17, f32[1,4096]{1,0:T(1,128)S(1)} %bitcast.18), custom_call_target="tpu_custom_call" | custom-call | flops 16777216 | bytes 1572864 | tf_op jit(solution)/shard_map/pallas_call | solution.py:409
  24.1 0.0 copy-done.6
  24.1 1.0 %collective-permute-start = (f32[256,128]{1,0:T(8,128)S(1)}, f32[256,128]{1,0:T(8,128)S(1)}, u32[]{:S(2)}, u32[]{:S(2)}) collective-permute-start(f32[256,128]{1,0:T(8,128)S(1)} %copy-done.6), channel_id=1, source_target_pairs={{0,2},{2,0},{4,6},{6,4},{8,10},{10,8},{12,14},{14,12},{16,18},{18,... | collective-permute-start | bytes 393224 | tf_op jit(solution)/shard_map/ppermute | solution.py:406
  25.1 0.0 copy-done.3
  25.1 2.8 %shard_map.87.bwd_hbm = f32[2048,128]{1,0:T(8,128)S(1)} custom-call(bf16[2048,128]{1,0:T(8,128)(2,1)S(1)} %copy-done.3, f32[256,128]{1,0:T(8,128)S(1)} %get-tuple-element.32.dec_ref, f32[256,128]{1,0:T(8,128)S(1)} %get-tuple-element.33.gain_ref, f32[1,4096]{1,0:T(1,128)S(1)} %bitcast.19), custom_call_target="tpu_custom_call" | custom-call | flops 16777216 | bytes 1572864 | tf_op jit(solution)/shard_map/pallas_call | solution.py:419
  28.0 0.0 copy-start
  28.0 0.0 collective-permute-done.near_ref
  28.0 5.6 %all-to-all-done = bf16[64,3,4,128]{3,2,1,0:T(4,128)(2,1)S(1)} async-done(((bf16[64,3,4,128]{3,2,1,0:T(4,128)(2,1)}), bf16[64,3,4,128]{3,2,1,0:T(4,128)(2,1)S(1)}, u32[]{:S(2)}, u32[]{:S(2)}) %all-to-all-start) | async-done | bytes 196640 | tf_op jit(solution)/shard_map/all_to_all | solution.py:401
  33.6 2.5 %collective-permute-start.1 = (bf16[768,128]{1,0:T(8,128)(2,1)S(1)}, bf16[768,128]{1,0:T(8,128)(2,1)S(1)}, u32[]{:S(2)}, u32[]{:S(2)}) collective-permute-start(bf16[768,128]{1,0:T(8,128)(2,1)S(1)} %bitcast.14), channel_id=1, source_target_pairs={{0,2},{2,0},{4,6},{6,4},{8,10},{10,8},{12,14},{14,12},{16,18},{18,... | collective-permute-start | bytes 589832 | tf_op jit(solution)/shard_map/ppermute | solution.py:406
  36.0 1.1 %collective-permute-done.1.other_ref = bf16[768,128]{1,0:T(8,128)(2,1)S(1)} collective-permute-done((bf16[768,128]{1,0:T(8,128)(2,1)S(1)}, bf16[768,128]{1,0:T(8,128)(2,1)S(1)}, u32[]{:S(2)}, u32[]{:S(2)}) %collective-permute-start.1) | collective-permute-done | bytes 196640 | tf_op jit(solution)/shard_map/ppermute | solution.py:406
  37.1 0.4 shard_map.88
  37.5 16.2 %all_to_all.10 = bf16[64,3,2,128]{3,2,1,0:T(2,128)(2,1)S(1)} all-to-all(bf16[64,3,2,128]{3,2,1,0:T(2,128)(2,1)S(1)} %bitcast.16), channel_id=1, replica_groups={{0,4,8,12,16,20,24,28,32,36,40,44,48,52,56,60,64,68,72,76,80,84,88,92,9..., dimensions={0} | all-to-all | bytes 196608 | tf_op jit(solution)/shard_map/all_to_all | solution.py:401
  53.7 1.6 %collective-permute-start.2 = (bf16[384,128]{1,0:T(8,128)(2,1)S(1)}, bf16[384,128]{1,0:T(8,128)(2,1)S(1)}, u32[]{:S(2)}, u32[]{:S(2)}) collective-permute-start(bf16[384,128]{1,0:T(8,128)(2,1)S(1)} %bitcast.11), channel_id=1, source_target_pairs={{0,2},{2,0},{4,6},{6,4},{8,10},{10,8},{12,14},{14,12},{16,18},{18,... | collective-permute-start | bytes 294920 | tf_op jit(solution)/shard_map/ppermute | solution.py:406
  55.3 0.9 %collective-permute-done.2.other_ref = bf16[384,128]{1,0:T(8,128)(2,1)S(1)} collective-permute-done((bf16[384,128]{1,0:T(8,128)(2,1)S(1)}, bf16[384,128]{1,0:T(8,128)(2,1)S(1)}, u32[]{:S(2)}, u32[]{:S(2)}) %collective-permute-start.2) | collective-permute-done | bytes 98336 | tf_op jit(solution)/shard_map/ppermute | solution.py:406
  56.2 0.1 shard_map.90
  56.3 0.5 collective-permute-start.3
  56.8 0.0 copy-done
  56.8 3.9 %shard_map.89 = (bf16[2048,128]{1,0:T(8,128)(2,1)}, bf16[2048,128]{1,0:T(8,128)(2,1)}) custom-call(bf16[384,128]{1,0:T(8,128)(2,1)S(1)} %bitcast.13, bf16[384,128]{1,0:T(8,128)(2,1)S(1)} %collective-permute-done.2.other_ref, f32[256,128]{1,0:T(8,128)S(1)} %collective-permute-done.near_ref, f32[2048,128]{1,0:T(8,128)S(1)} %get-tuple-element.39.fwd_ref, ...), custom_call_target="tpu_custom_call" | custom-call | flops 16777216 | bytes 3670016 | tf_op jit(solution)/shard_map/pallas_call | solution.py:454
  60.8 0.0 collective-permute-done.3
  60.8 0.7 %maximum_bitcast_fusion = f32[4096,16]{0,1:T(8,128)} fusion(f32[16,2048]{1,0:T(8,128)S(1)} %get-tuple-element.46, f32[16,2048]{1,0:T(8,128)S(1)} %get-tuple-element.45), kind=kLoop, calls=%fused_computation | loop fusion | flops 65536 | bytes 524288 | tf_op jit(solution)/shard_map/transpose | solution.py:469
  (1 shorter events, 0.0 us)
Async XLA Ops:
  0.6 20.7 %copy-start.1 = (bf16[2048,128]{1,0:T(8,128)(2,1)S(1)}, bf16[2048,128]{1,0:T(8,128)(2,1)}, u32[]{:S(2)}) copy-start(bf16[2048,128]{1,0:T(8,128)(2,1)} %gated_ref) | copy-start | bytes 1572868
  0.6 20.7 %copy-start.4 = (f32[4096,16]{0,1:T(8,128)S(1)}, f32[4096,16]{0,1:T(8,128)}, u32[]{:S(2)}) copy-start(f32[4096,16]{0,1:T(8,128)} %param.9) | copy-start | bytes 786436
  6.0 15.3 %copy-start.2 = (f32[4096,16]{0,1:T(8,128)S(1)}, f32[4096,16]{0,1:T(8,128)}, u32[]{:S(2)}) copy-start(f32[4096,16]{0,1:T(8,128)} %param.10) | copy-start | bytes 786436
  6.0 15.3 %copy-start.5 = (f32[4096]{0:T(1024)S(1)}, f32[4096]{0:T(1024)}, u32[]{:S(2)}) copy-start(f32[4096]{0:T(1024)} %param.11) | copy-start | bytes 49156
  6.1 27.5 %all-to-all-start = ((bf16[64,3,4,128]{3,2,1,0:T(4,128)(2,1)}), bf16[64,3,4,128]{3,2,1,0:T(4,128)(2,1)S(1)}, u32[]{:S(2)}, u32[]{:S(2)}) async-start(bf16[64,3,4,128]{3,2,1,0:T(4,128)(2,1)} %bitcast.20), calls=%async_computation | async-start | bytes 393216 | tf_op jit(solution)/shard_map/all_to_all | solution.py:401
  21.4 2.7 %copy-start.6 = (f32[256,128]{1,0:T(8,128)S(1)}, f32[256,128]{1,0:T(8,128)}, u32[]{:S(2)}) copy-start(f32[256,128]{1,0:T(8,128)} %get-tuple-element.35) | copy-start | bytes 393220
  21.4 3.8 %copy-start.3 = (bf16[2048,128]{1,0:T(8,128)(2,1)S(1)}, bf16[2048,128]{1,0:T(8,128)(2,1)}, u32[]{:S(2)}) copy-start(bf16[2048,128]{1,0:T(8,128)(2,1)} %get-tuple-element.31.dz_ref) | copy-start | bytes 1572868
  24.1 3.9 %collective-permute-start = (f32[256,128]{1,0:T(8,128)S(1)}, f32[256,128]{1,0:T(8,128)S(1)}, u32[]{:S(2)}, u32[]{:S(2)}) collective-permute-start(f32[256,128]{1,0:T(8,128)S(1)} %copy-done.6), channel_id=1, source_target_pairs={{0,2},{2,0},{4,6},{6,4},{8,10},{10,8},{12,14},{14,12},{16,18},{18,... | collective-permute-start | bytes 393224 | tf_op jit(solution)/shard_map/ppermute | solution.py:406
  28.0 28.8 %copy-start = (bf16[2048,128]{1,0:T(8,128)(2,1)S(1)}, bf16[2048,128]{1,0:T(8,128)(2,1)}, u32[]{:S(2)}) copy-start(bf16[2048,128]{1,0:T(8,128)(2,1)} %upstream_hbm.3) | copy-start | bytes 1572868
  33.6 3.5 %collective-permute-start.1 = (bf16[768,128]{1,0:T(8,128)(2,1)S(1)}, bf16[768,128]{1,0:T(8,128)(2,1)S(1)}, u32[]{:S(2)}, u32[]{:S(2)}) collective-permute-start(bf16[768,128]{1,0:T(8,128)(2,1)S(1)} %bitcast.14), channel_id=1, source_target_pairs={{0,2},{2,0},{4,6},{6,4},{8,10},{10,8},{12,14},{14,12},{16,18},{18,... | collective-permute-start | bytes 589832 | tf_op jit(solution)/shard_map/ppermute | solution.py:406
  53.7 2.5 %collective-permute-start.2 = (bf16[384,128]{1,0:T(8,128)(2,1)S(1)}, bf16[384,128]{1,0:T(8,128)(2,1)S(1)}, u32[]{:S(2)}, u32[]{:S(2)}) collective-permute-start(bf16[384,128]{1,0:T(8,128)(2,1)S(1)} %bitcast.11), channel_id=1, source_target_pairs={{0,2},{2,0},{4,6},{6,4},{8,10},{10,8},{12,14},{14,12},{16,18},{18,... | collective-permute-start | bytes 294920 | tf_op jit(solution)/shard_map/ppermute | solution.py:406
  56.3 4.4 %collective-permute-start.3 = (bf16[16,2048]{1,0:T(8,128)(2,1)S(1)}, bf16[16,2048]{1,0:T(8,128)(2,1)S(1)}, u32[]{:S(2)}, u32[]{:S(2)}) collective-permute-start(bf16[16,2048]{1,0:T(8,128)(2,1)S(1)} %get-tuple-element.44), channel_id=1, source_target_pairs={{0,1},{1,0},{2,3},{3,2},{4,5},{5,4},{6,7},{7,6},{8,9},{9,8},{10,11... | collective-permute-start | bytes 196616 | tf_op jit(solution)/shard_map/ppermute | solution.py:453

commit v5 on v3

--- a/solution.py
+++ b/solution.py
@@ -219,7 +219,7 @@
         own_sums(modes, tokens, g, dzt, bwd_ref, dec_ref, gain_ref, skip, order)
 
 
-def scan_kernel(chunks, tokens, own_ref, other_ref, lam_ref, out_hbm, sums, outs, stage, sems):
+def scan_kernel(chunks, tokens, own_ref, other_ref, lam_ref, out_ref, sums, outs):
     core = lax.axis_index("seq") % 2
     chips = chunks // 2
     sums[core] = own_ref[...].astype(F32)
@@ -246,18 +246,9 @@
 
     _, _, own, cross = lax.fori_loop(0, chips // SCAN_UNROLL, body, (zero, zero, zero, zero))
     grad = (own + cross * jnp.exp(-lam)) * (1.0 / (chunks * tokens))
-    sent = []
-    quarter = chips // 4
-    for part in range(4):
-        for q in range(part * quarter, (part + 1) * quarter):
-            outs[core, at(q, 2), :] = grad
-        rows = pl.ds(part * quarter * 4 * KINDS, quarter * 4 * KINDS)
-        stage[rows, :] = outs[core, rows, :].astype(BF16)
-        copy = pltpu.make_async_copy(stage.at[rows, :], out_hbm.at[rows, :], sems.at[part])
-        copy.start()
-        sent.append(copy)
-    for copy in sent:
-        copy.wait()
+    for q in range(chips):
+        outs[core, at(q, 2), :] = grad
+    out_ref[...] = outs[core].astype(BF16)
 
 
 def residue_kernel(modes, blocks, in_ref, out_ref, wire_ref, tiles, flat):
@@ -273,8 +264,8 @@
 
 
 def final_kernel(
-    modes, blocks, tokens, in_ref, fwd_ref, bwd_hbm, dec_ref, gain_ref, upstream_hbm,
-    grad_gated_hbm, grad_value_hbm, tiles, zts, gts, bwd_ref, upstream_ref, grad_gated_ref,
+    modes, blocks, tokens, in_ref, fwd_ref, bwd_hbm, dec_ref, gain_ref, upstream_hbm, residue_ref,
+    grad_gated_hbm, grad_value_hbm, grad_residue_hbm, tiles, zts, gts, bwd_ref, upstream_ref, grad_gated_ref,
     grad_value_ref, in_sems, sems
 ):
     groups = blocks // GROUP
@@ -286,7 +277,12 @@
             pltpu.make_async_copy(bwd_hbm.at[rows, :], bwd_ref.at[rows, :], in_sems.at[g])
         )
     upstream_copy = pltpu.make_async_copy(upstream_hbm, upstream_ref, in_sems.at[groups])
-    for copy in [own_copies[0], upstream_copy] + own_copies[1:]:
+    channels = blocks * LANES
+    start = pl.multiple_of(lax.axis_index("ch") * channels, LANES)
+    residue_copy = pltpu.make_async_copy(
+        residue_ref, grad_residue_hbm.at[:, pl.ds(start, channels)], in_sems.at[groups + 1]
+    )
+    for copy in [own_copies[0], upstream_copy] + own_copies[1:] + [residue_copy]:
         copy.start()
     tiles[...] = in_ref[...].astype(F32)
     copies = []
@@ -337,7 +333,7 @@
             grad_gated_ref[rows, :] = back.astype(BF16)
             if j % 4 == 3:
                 send(grad_gated_ref, grad_gated_hbm, g * GROUP + j - 3, 4)
-    for copy in copies:
+    for copy in copies + [residue_copy]:
         copy.wait()
 
 
@@ -406,19 +402,7 @@
         4 * cells,
         6 * channels * tokens,
     )(gated_held, rate_t, residue_t, skip)
-    heard, fwd, lam = lax.optimization_barrier((exchange(states), fwd, lam))
-    heard_other = lax.ppermute(heard, "seq", [(d, d ^ 1) for d in range(chunks)])
-    chained = pltpu.VMEM((2,) + wire, F32)
-    (entering,) = call(
-        functools.partial(scan_kernel, chunks, tokens),
-        [vmem] * 3,
-        [hbm],
-        [(wire, BF16)],
-        [chained, chained, staged, sems(4)],
-        16 * chunks * GROUP * LANES,
-        8 * chunks * GROUP * LANES,
-    )(heard, heard_other, lam)
-    entering, dz_held = lax.optimization_barrier((entering, dz))
+    fwd, dz = lax.optimization_barrier((fwd, dz))
     (bwd,) = call(
         functools.partial(behind_kernel, modes, blocks, tokens),
         [vmem] * 4,
@@ -427,8 +411,20 @@
         [one],
         4 * cells,
         6 * channels * tokens,
-    )(dz_held, decay, gain, skip)
-    returned, bwd = lax.optimization_barrier((exchange(entering), bwd))
+    )(dz, decay, gain, skip)
+    heard, fwd, bwd, lam = lax.optimization_barrier((exchange(states), fwd, bwd, lam))
+    heard_other = lax.ppermute(heard, "seq", [(d, d ^ 1) for d in range(chunks)])
+    chained = pltpu.VMEM((2,) + wire, F32)
+    (entering,) = call(
+        functools.partial(scan_kernel, chunks, tokens),
+        [vmem] * 3,
+        [vmem],
+        [(wire, BF16)],
+        [chained, chained],
+        16 * chunks * GROUP * LANES,
+        8 * chunks * GROUP * LANES,
+    )(heard, heard_other, lam)
+    returned = exchange(entering)
     grad_own, grad_wire = call(
         functools.partial(residue_kernel, modes, blocks),
         [vmem],
@@ -439,20 +435,18 @@
         8 * modes * channels,
     )(returned)
     grad_other = lax.ppermute(grad_wire, "ch", [(0, 1), (1, 0)]).astype(F32)
-    grad_gated, grad_value = call(
+    grad_gated, grad_value, grad_res = call(
         functools.partial(final_kernel, modes, blocks, tokens),
-        [vmem, vmem, hbm, vmem, vmem, hbm],
-        [hbm] * 2,
-        [native, native],
+        [vmem, vmem, hbm, vmem, vmem, hbm, vmem],
+        [hbm] * 3,
+        [native, native, ((modes, residue.shape[0]), F32)],
         [unpacked, [one] * groups, [one] * groups, pltpu.VMEM(*signal), raw, raw, raw]
-        + [sems(groups + 1), sems(3 * groups)],
+        + [sems(groups + 2), sems(3 * groups)],
         4 * cells,
         14 * channels * tokens,
-    )(returned, fwd, bwd, decay, gain, upstream)
-    low = lax.axis_index("ch") == 0
-    grad_res = jnp.concatenate(
-        [jnp.where(low, grad_own, grad_other), jnp.where(low, grad_other, grad_own)], axis=1
-    )
+    )(returned, fwd, bwd, decay, gain, upstream, grad_own)
+    place = (1 - lax.axis_index("ch")) * channels
+    grad_res = lax.dynamic_update_slice(grad_res, grad_other, (0, place))
     return (grad_gated, grad_value, grad_res.T)
 
 

time: 61.7 us -> 60.5 us (0.981)
  blocking collectives: 0 us -> 16.6 us
  waiting for transfers between devices: 19.7 us -> 7.73 us
  starting transfers between devices: 22.8 us -> 18.2 us
  local copies, waits for them, and re-layouts: 1.06 us -> 0.03 us
  Pallas kernels: 16 us -> 15.3 us
    all_to_all x0 -> x1, blocking collectives: none -> 16.6 us  [exchange(): lax.all_to_all(array, 'seq', split_axis=0, concat_axis=0, axis_index_grou...]
    all_to_all x2 -> x1, waiting for transfers between devices: 18.6 us -> 6.66 us  [exchange(): lax.all_to_all(array, 'seq', split_axis=0, concat_axis=0, axis_index_grou...]
    all_to_all x2 -> x1, starting transfers between devices: 19.9 us -> 15.3 us  [exchange(): lax.all_to_all(array, 'seq', split_axis=0, concat_axis=0, axis_index_grou...]
    unnamed x12, local copies, waits for them, and re-layouts: 1.06 us -> 0.03 us
    transpose x1 -> x0, other arithmetic: 0.72 us -> none  [local(): return (grad_gated, grad_value, grad_res.T)]
    pallas_call x1, Pallas kernels: 1.14 us -> 0.46 us  [local(): call(functools.partial(scan_kernel, chunks, tokens), [vmem] * 3, [vmem],...]
    dynamic_update_slice x0 -> x1, other arithmetic: none -> 0.67 us  [local(): grad_res = lax.dynamic_update_slice(grad_res, grad_other, (0, place))]
  transfers between devices with their start and end apart: 4 -> 3, of which waited for: 3 -> 2; matrix products, arithmetic and copies ran while one was open for 0% -> 0% of each run, Pallas kernels for 15% -> 16%
where the time goes in v5:
time: 60.5 us; the launch traced here: 59.3 us
  starting transfers between devices  18.2 us (30%)
  blocking collectives  16.6 us (27%)
  Pallas kernels  15.3 us (25%)
  waiting for transfers between devices  7.73 us (13%)
  between operations  0.76 us (1%)
  other arithmetic  0.67 us (1%)
    all_to_all x1, blocking collectives, exchange(): lax.all_to_all(array, 'seq', split_axis=0, concat_axis=0, axis_index_grou...  16.6 us
    all_to_all x1, starting transfers between devices, exchange(): lax.all_to_all(array, 'seq', split_axis=0, concat_axis=0, axis_index_grou...  15.3 us
    all_to_all x1, waiting for transfers between devices, exchange(): lax.all_to_all(array, 'seq', split_axis=0, concat_axis=0, axis_index_grou...  6.66 us
    pallas_call x1, Pallas kernels, local(): call(functools.partial(state_kernel, modes, blocks, tokens), [hbm] * 4, [...  5.33 us
    pallas_call x1, Pallas kernels, local(): call(functools.partial(final_kernel, modes, blocks, tokens), [vmem, vmem,...  3.94 us
    pallas_call x1, Pallas kernels, local(): call(functools.partial(behind_kernel, modes, blocks, tokens), [vmem] * 4,...  2.82 us
    pallas_call x1, Pallas kernels, local(): call(functools.partial(ahead_kernel, modes, blocks, tokens), [vmem] * 4,...  2.7 us
    ppermute x1, starting transfers between devices, local(): lax.ppermute(heard, 'seq', [(d, d ^ 1) for d in range(chunks)])  2.46 us
  transfers between devices with their start and end apart: 3, of which 2 were waited for; matrix products, arithmetic and copies ran while one was open for 0% of the time, Pallas kernels for 16%

profile of v5, /device:TPU:1, one launch (start us, length us, event | category | flops | bytes accessed | tf_op | source)
XLA Modules:
  0.0 59.3 jit_solution(1887272595530526519)
XLA Ops:
  0.6 0.0 copy-start.1
  0.6 0.0 copy-start.4
  0.7 5.3 %shard_map.85 = (bf16[768,128]{1,0:T(8,128)(2,1)}, bf16[2048,128]{1,0:T(8,128)(2,1)}) custom-call(bf16[2048,128]{1,0:T(8,128)(2,1)} %gated_ref, bf16[2048,128]{1,0:T(8,128)(2,1)} %value_hbm.1, bf16[2048,128]{1,0:T(8,128)(2,1)} %upstream_hbm.3, f32[16,4096]{1,0:T(8,128)} %bitcast.10), custom_call_target="tpu_custom_call" | custom-call | flops 20971520 | bytes 2097152 | tf_op jit(solution)/shard_map/pallas_call | solution.py:375
  6.0 0.0 copy-start.2
  6.0 0.0 copy-start.5
  6.0 15.3 %all-to-all-start = ((bf16[64,3,4,128]{3,2,1,0:T(4,128)(2,1)}), bf16[64,3,4,128]{3,2,1,0:T(4,128)(2,1)S(1)}, u32[]{:S(2)}, u32[]{:S(2)}) async-start(bf16[64,3,4,128]{3,2,1,0:T(4,128)(2,1)} %bitcast.18), calls=%async_computation | async-start | bytes 393216 | tf_op jit(solution)/shard_map/all_to_all | solution.py:391
  21.3 0.0 copy-done.1
  21.3 0.0 copy-done.4
  21.3 0.0 copy-done.2
  21.3 0.0 copy-done.5
  21.3 0.0 copy-start.3
  21.3 2.7 %shard_map.86 = (f32[2048,128]{1,0:T(8,128)S(1)}, f32[256,128]{1,0:T(8,128)S(1)}, f32[256,128]{1,0:T(8,128)S(1)}, f32[4,128]{1,0:T(4,128)S(1)}) custom-call(bf16[2048,128]{1,0:T(8,128)(2,1)S(1)} %copy-done.1, f32[16,4096]{1,0:T(8,128)S(1)} %bitcast.11, f32[16,4096]{1,0:T(8,128)S(1)} %bitcast.15, f32[1,4096]{1,0:T(1,128)S(1)} %bitcast.16), custom_call_target="tpu_custom_call" | custom-call | flops 16777216 | bytes 1572864 | tf_op jit(solution)/shard_map/pallas_call | solution.py:396
  24.0 0.0 copy-done.3
  24.0 2.8 %shard_map.87.bwd_hbm = f32[2048,128]{1,0:T(8,128)S(1)} custom-call(bf16[2048,128]{1,0:T(8,128)(2,1)S(1)} %copy-done.3, f32[256,128]{1,0:T(8,128)S(1)} %get-tuple-element.29.dec_ref, f32[256,128]{1,0:T(8,128)S(1)} %get-tuple-element.30.gain_ref, f32[1,4096]{1,0:T(1,128)S(1)} %bitcast.17), custom_call_target="tpu_custom_call" | custom-call | flops 16777216 | bytes 1572864 | tf_op jit(solution)/shard_map/pallas_call | solution.py:406
  26.9 6.7 %all-to-all-done = bf16[64,3,4,128]{3,2,1,0:T(4,128)(2,1)S(1)} async-done(((bf16[64,3,4,128]{3,2,1,0:T(4,128)(2,1)}), bf16[64,3,4,128]{3,2,1,0:T(4,128)(2,1)S(1)}, u32[]{:S(2)}, u32[]{:S(2)}) %all-to-all-start) | async-done | bytes 196640 | tf_op jit(solution)/shard_map/all_to_all | solution.py:391
  33.5 0.0 copy-start
  33.5 2.5 %collective-permute-start = (bf16[768,128]{1,0:T(8,128)(2,1)S(1)}, bf16[768,128]{1,0:T(8,128)(2,1)S(1)}, u32[]{:S(2)}, u32[]{:S(2)}) collective-permute-start(bf16[768,128]{1,0:T(8,128)(2,1)S(1)} %bitcast.12), channel_id=1, source_target_pairs={{0,2},{2,0},{4,6},{6,4},{8,10},{10,8},{12,14},{14,12},{16,18},{18,... | collective-permute-start | bytes 589832 | tf_op jit(solution)/shard_map/ppermute | solution.py:416
  36.0 1.1 %collective-permute-done.other_ref = bf16[768,128]{1,0:T(8,128)(2,1)S(1)} collective-permute-done((bf16[768,128]{1,0:T(8,128)(2,1)S(1)}, bf16[768,128]{1,0:T(8,128)(2,1)S(1)}, u32[]{:S(2)}, u32[]{:S(2)}) %collective-permute-start) | collective-permute-done | bytes 196640 | tf_op jit(solution)/shard_map/ppermute | solution.py:416
  37.1 0.5 shard_map.88
  37.5 16.6 %all_to_all.10 = bf16[64,3,4,128]{3,2,1,0:T(4,128)(2,1)S(1)} all-to-all(bf16[64,3,4,128]{3,2,1,0:T(4,128)(2,1)S(1)} %bitcast.14), channel_id=1, replica_groups={{0,4,8,12,16,20,24,28,32,36,40,44,48,52,56,60,64,68,72,76,80,84,88,92,9..., dimensions={0} | all-to-all | bytes 393216 | tf_op jit(solution)/shard_map/all_to_all | solution.py:391
  54.2 0.1 shard_map.89
  54.2 0.5 collective-permute-start.1
  54.7 0.0 copy-done
  54.7 3.9 %shard_map.90 = (bf16[2048,128]{1,0:T(8,128)(2,1)}, bf16[2048,128]{1,0:T(8,128)(2,1)}, f32[16,4096]{1,0:T(8,128)}) custom-call(bf16[768,128]{1,0:T(8,128)(2,1)S(1)} %bitcast.9, f32[2048,128]{1,0:T(8,128)S(1)} %get-tuple-element.34.fwd_ref, f32[2048,128]{1,0:T(8,128)S(1)} %shard_map.87.bwd_hbm, f32[256,128]{1,0:T(8,128)S(1)} %get-tuple-element.29.dec_ref, ...), custom_call_target="tpu_custom_call" | custom-call | flops 16777216 | bytes 3670016 | tf_op jit(solution)/shard_map/pallas_call | solution.py:438
  58.7 0.0 collective-permute-done.1
  58.7 0.7 %convert_dynamic-update-slice_fusion = f32[16,4096]{1,0:T(8,128)} fusion(f32[16,4096]{1,0:T(8,128)} %get-tuple-element.39, s32[]{:T(128)S(6)} %select_n.3, bf16[16,2048]{1,0:T(8,128)(2,1)S(1)} %collective-permute-done.1), kind=kLoop, calls=%fused_computation | loop fusion | flops 32768 | bytes 196612 | tf_op jit(solution)/shard_map/dynamic_update_slice | solution.py:449
Async XLA Ops:
  0.6 20.7 %copy-start.1 = (bf16[2048,128]{1,0:T(8,128)(2,1)S(1)}, bf16[2048,128]{1,0:T(8,128)(2,1)}, u32[]{:S(2)}) copy-start(bf16[2048,128]{1,0:T(8,128)(2,1)} %gated_ref) | copy-start | bytes 1572868
  0.6 20.7 %copy-start.4 = (f32[4096,16]{0,1:T(8,128)S(1)}, f32[4096,16]{0,1:T(8,128)}, u32[]{:S(2)}) copy-start(f32[4096,16]{0,1:T(8,128)} %param.9) | copy-start | bytes 786436
  6.0 15.3 %copy-start.2 = (f32[4096,16]{0,1:T(8,128)S(1)}, f32[4096,16]{0,1:T(8,128)}, u32[]{:S(2)}) copy-start(f32[4096,16]{0,1:T(8,128)} %param.10) | copy-start | bytes 786436
  6.0 15.3 %copy-start.5 = (f32[4096]{0:T(1024)S(1)}, f32[4096]{0:T(1024)}, u32[]{:S(2)}) copy-start(f32[4096]{0:T(1024)} %param.11) | copy-start | bytes 49156
  6.0 27.5 %all-to-all-start = ((bf16[64,3,4,128]{3,2,1,0:T(4,128)(2,1)}), bf16[64,3,4,128]{3,2,1,0:T(4,128)(2,1)S(1)}, u32[]{:S(2)}, u32[]{:S(2)}) async-start(bf16[64,3,4,128]{3,2,1,0:T(4,128)(2,1)} %bitcast.18), calls=%async_computation | async-start | bytes 393216 | tf_op jit(solution)/shard_map/all_to_all | solution.py:391
  21.3 2.7 %copy-start.3 = (bf16[2048,128]{1,0:T(8,128)(2,1)S(1)}, bf16[2048,128]{1,0:T(8,128)(2,1)}, u32[]{:S(2)}) copy-start(bf16[2048,128]{1,0:T(8,128)(2,1)} %get-tuple-element.28.dz_ref) | copy-start | bytes 1572868
  33.5 21.2 %copy-start = (bf16[2048,128]{1,0:T(8,128)(2,1)S(1)}, bf16[2048,128]{1,0:T(8,128)(2,1)}, u32[]{:S(2)}) copy-start(bf16[2048,128]{1,0:T(8,128)(2,1)} %upstream_hbm.3) | copy-start | bytes 1572868
  33.5 3.5 %collective-permute-start = (bf16[768,128]{1,0:T(8,128)(2,1)S(1)}, bf16[768,128]{1,0:T(8,128)(2,1)S(1)}, u32[]{:S(2)}, u32[]{:S(2)}) collective-permute-start(bf16[768,128]{1,0:T(8,128)(2,1)S(1)} %bitcast.12), channel_id=1, source_target_pairs={{0,2},{2,0},{4,6},{6,4},{8,10},{10,8},{12,14},{14,12},{16,18},{18,... | collective-permute-start | bytes 589832 | tf_op jit(solution)/shard_map/ppermute | solution.py:416
  54.2 4.4 %collective-permute-start.1 = (bf16[16,2048]{1,0:T(8,128)(2,1)S(1)}, bf16[16,2048]{1,0:T(8,128)(2,1)S(1)}, u32[]{:S(2)}, u32[]{:S(2)}) collective-permute-start(bf16[16,2048]{1,0:T(8,128)(2,1)S(1)} %get-tuple-element.40), channel_id=1, source_target_pairs={{0,1},{1,0},{2,3},{3,2},{4,5},{5,4},{6,7},{7,6},{8,9},{9,8},{10,11... | collective-permute-start | bytes 196616 | tf_op jit(solution)/shard_map/ppermute | solution.py:437

commit v6 on v5

--- a/solution.py
+++ b/solution.py
@@ -14,7 +14,7 @@
 KINDS = 3
 PART, UNROLL = 8, 16
 FINAL_UNROLL = 16
-SCAN_UNROLL = 4
+RUN_OF_CHIPS = 8
 STATE_PART, STATE_UNROLL, RUN = 4, 32, 4
 LIMIT = 56 * 2**20
 
@@ -198,7 +198,8 @@
     spread_modes(res_ref, gain_ref, first, modes, blocks)
     for h in range(2):
         for g in range(blocks // GROUP):
-            row = g * modes * GROUP + lax.axis_index("seq") // 2 * 2 + h
+            chip = lax.axis_index("seq") // 2
+            row = g * modes * GROUP + (chip % RUN_OF_CHIPS * RUN_OF_CHIPS + chip // RUN_OF_CHIPS) * 2 + h
             own = dec_ref[pl.ds(row, 1), :]
             lam_ref[pl.ds(2 * h + g, 1), :] = own
     dec_ref[...] = jnp.exp(-dec_ref[...])
@@ -233,8 +234,8 @@
 
     def body(i, carry):
         x, y, own, cross = carry
-        for u in range(SCAN_UNROLL):
-            q, r = i * SCAN_UNROLL + u, chips - 1 - i * SCAN_UNROLL - u
+        for u in range(RUN_OF_CHIPS):
+            q, r = u * RUN_OF_CHIPS + i, chips - 1 - u * RUN_OF_CHIPS - i
             for place in range(2):
                 outs[place, at(q, 0), :] = x
                 outs[1 - place, at(r, 1), :] = y
@@ -244,7 +245,7 @@
                 y = step * y + sums[1 - place, at(r, 1), :]
         return x, y, own, cross
 
-    _, _, own, cross = lax.fori_loop(0, chips // SCAN_UNROLL, body, (zero, zero, zero, zero))
+    _, _, own, cross = lax.fori_loop(0, RUN_OF_CHIPS, body, (zero, zero, zero, zero))
     grad = (own + cross * jnp.exp(-lam)) * (1.0 / (chunks * tokens))
     for q in range(chips):
         outs[core, at(q, 2), :] = grad
@@ -345,7 +346,7 @@
     pairs = modes * blocks
     groups = blocks // GROUP
     assert tokens == LANES == UNROLL * GROUP and pairs == 2 * chunks
-    assert blocks == 2 * GROUP and modes == 2 * PART and chunks % (2 * SCAN_UNROLL) == 0
+    assert blocks == 2 * GROUP and modes == 2 * PART and chunks == 2 * RUN_OF_CHIPS**2
     rate_t, residue_t, skip = rate.T, residue.T, skip_weight[None, :]
     vmem = pl.BlockSpec(memory_space=pltpu.VMEM)
     hbm = pl.BlockSpec(memory_space=pltpu.HBM)
@@ -387,7 +388,11 @@
 
     def exchange(array):
         array = array.reshape(chunks // 2, KINDS, 4, LANES)
-        members = [list(range(core, chunks, 2)) for core in range(2)]
+        run = range(RUN_OF_CHIPS)
+        members = [
+            [2 * (late * RUN_OF_CHIPS + early) + core for early in run for late in run]
+            for core in range(2)
+        ]
         return lax.all_to_all(
             array, "seq", split_axis=0, concat_axis=0, axis_index_groups=members, tiled=True
         ).reshape(wire)

time: 60.5 us -> 59.7 us (0.987)
  the two profiles are of different devices: /device:TPU:1 before, /device:TPU:8 now
where the time goes in v6:
time: 59.7 us; the launch traced here: 59.5 us
  blocking collectives  18.5 us (31%)
  Pallas kernels  15.3 us (26%)
  starting transfers between devices  15.2 us (25%)
  waiting for transfers between devices  8.94 us (15%)
  between operations  0.76 us (1%)
  other arithmetic  0.67 us (1%)
    all_to_all x1, blocking collectives, exchange(): lax.all_to_all(array, 'seq', split_axis=0, concat_axis=0, axis_index_grou...  18.5 us
    all_to_all x1, starting transfers between devices, exchange(): lax.all_to_all(array, 'seq', split_axis=0, concat_axis=0, axis_index_grou...  13.8 us
    all_to_all x1, waiting for transfers between devices, exchange(): lax.all_to_all(array, 'seq', split_axis=0, concat_axis=0, axis_index_grou...  7.5 us
    pallas_call x1, Pallas kernels, local(): call(functools.partial(state_kernel, modes, blocks, tokens), [hbm] * 4, [...  5.33 us
    pallas_call x1, Pallas kernels, local(): call(functools.partial(final_kernel, modes, blocks, tokens), [vmem, vmem,...  3.94 us
    pallas_call x1, Pallas kernels, local(): call(functools.partial(behind_kernel, modes, blocks, tokens), [vmem] * 4,...  2.82 us
    pallas_call x1, Pallas kernels, local(): call(functools.partial(ahead_kernel, modes, blocks, tokens), [vmem] * 4,...  2.7 us
    ppermute x1, waiting for transfers between devices, local(): lax.ppermute(heard, 'seq', [(d, d ^ 1) for d in range(chunks)])  1.44 us
  transfers between devices with their start and end apart: 3, of which 2 were waited for; matrix products, arithmetic and copies ran while one was open for 0% of the time, Pallas kernels for 16%

profile of v6, /device:TPU:8, one launch (start us, length us, event | category | flops | bytes accessed | tf_op | source)
XLA Modules:
  0.0 59.5 jit_solution(3471431047463321554)
XLA Ops:
  0.6 0.0 copy-start.1
  0.6 0.0 copy-start.4
  0.7 5.3 %shard_map.85 = (bf16[768,128]{1,0:T(8,128)(2,1)}, bf16[2048,128]{1,0:T(8,128)(2,1)}) custom-call(bf16[2048,128]{1,0:T(8,128)(2,1)} %gated_ref, bf16[2048,128]{1,0:T(8,128)(2,1)} %value_hbm.1, bf16[2048,128]{1,0:T(8,128)(2,1)} %upstream_hbm.3, f32[16,4096]{1,0:T(8,128)} %bitcast.10), custom_call_target="tpu_custom_call" | custom-call | flops 20971520 | bytes 2097152 | tf_op jit(solution)/shard_map/pallas_call | solution.py:376
  6.0 0.0 copy-start.2
  6.0 0.0 copy-start.5
  6.0 13.8 %all-to-all-start = ((bf16[64,3,4,128]{3,2,1,0:T(4,128)(2,1)}), bf16[64,3,4,128]{3,2,1,0:T(4,128)(2,1)S(1)}, u32[]{:S(2)}, u32[]{:S(2)}) async-start(bf16[64,3,4,128]{3,2,1,0:T(4,128)(2,1)} %bitcast.18), calls=%async_computation | async-start | bytes 393216 | tf_op jit(solution)/shard_map/all_to_all | solution.py:396
  19.8 0.0 copy-done.1
  19.8 0.0 copy-done.4
  19.9 0.0 copy-done.2
  19.9 0.0 copy-done.5
  19.9 0.0 copy-start.3
  19.9 2.7 %shard_map.86 = (f32[2048,128]{1,0:T(8,128)S(1)}, f32[256,128]{1,0:T(8,128)S(1)}, f32[256,128]{1,0:T(8,128)S(1)}, f32[4,128]{1,0:T(4,128)S(1)}) custom-call(bf16[2048,128]{1,0:T(8,128)(2,1)S(1)} %copy-done.1, f32[16,4096]{1,0:T(8,128)S(1)} %bitcast.11, f32[16,4096]{1,0:T(8,128)S(1)} %bitcast.15, f32[1,4096]{1,0:T(1,128)S(1)} %bitcast.16), custom_call_target="tpu_custom_call" | custom-call | flops 16777216 | bytes 1572864 | tf_op jit(solution)/shard_map/pallas_call | solution.py:401
  22.6 0.0 copy-done.3
  22.6 2.8 %shard_map.87.bwd_hbm = f32[2048,128]{1,0:T(8,128)S(1)} custom-call(bf16[2048,128]{1,0:T(8,128)(2,1)S(1)} %copy-done.3, f32[256,128]{1,0:T(8,128)S(1)} %get-tuple-element.29.dec_ref, f32[256,128]{1,0:T(8,128)S(1)} %get-tuple-element.30.gain_ref, f32[1,4096]{1,0:T(1,128)S(1)} %bitcast.17), custom_call_target="tpu_custom_call" | custom-call | flops 16777216 | bytes 1572864 | tf_op jit(solution)/shard_map/pallas_call | solution.py:411
  25.4 7.5 %all-to-all-done = bf16[64,3,4,128]{3,2,1,0:T(4,128)(2,1)S(1)} async-done(((bf16[64,3,4,128]{3,2,1,0:T(4,128)(2,1)}), bf16[64,3,4,128]{3,2,1,0:T(4,128)(2,1)S(1)}, u32[]{:S(2)}, u32[]{:S(2)}) %all-to-all-start) | async-done | bytes 196640 | tf_op jit(solution)/shard_map/all_to_all | solution.py:396
  32.9 0.0 copy-start
  32.9 0.0 collective-permute-start
  32.9 1.4 %collective-permute-done.other_ref = bf16[768,128]{1,0:T(8,128)(2,1)S(1)} collective-permute-done((bf16[768,128]{1,0:T(8,128)(2,1)S(1)}, bf16[768,128]{1,0:T(8,128)(2,1)S(1)}, u32[]{:S(2)}, u32[]{:S(2)}) %collective-permute-start) | collective-permute-done | bytes 196640 | tf_op jit(solution)/shard_map/ppermute | solution.py:421
  34.4 0.4 shard_map.88
  34.8 18.5 %all_to_all.10 = bf16[64,3,4,128]{3,2,1,0:T(4,128)(2,1)S(1)} all-to-all(bf16[64,3,4,128]{3,2,1,0:T(4,128)(2,1)S(1)} %bitcast.14), channel_id=1, replica_groups={{0,32,64,96,128,160,192,224,4,36,68,100,132,164,196,228,8,40,72,104,136..., dimensions={0} | all-to-all | bytes 393216 | tf_op jit(solution)/shard_map/all_to_all | solution.py:396
  53.4 0.1 shard_map.89
  53.4 1.4 %collective-permute-start.1 = (bf16[16,2048]{1,0:T(8,128)(2,1)S(1)}, bf16[16,2048]{1,0:T(8,128)(2,1)S(1)}, u32[]{:S(2)}, u32[]{:S(2)}) collective-permute-start(bf16[16,2048]{1,0:T(8,128)(2,1)S(1)} %get-tuple-element.40), channel_id=1, source_target_pairs={{0,1},{1,0},{2,3},{3,2},{4,5},{5,4},{6,7},{7,6},{8,9},{9,8},{10,11... | collective-permute-start | bytes 196616 | tf_op jit(solution)/shard_map/ppermute | solution.py:442
  54.9 0.0 copy-done
  54.9 3.9 %shard_map.90 = (bf16[2048,128]{1,0:T(8,128)(2,1)}, bf16[2048,128]{1,0:T(8,128)(2,1)}, f32[16,4096]{1,0:T(8,128)}) custom-call(bf16[768,128]{1,0:T(8,128)(2,1)S(1)} %bitcast.9, f32[2048,128]{1,0:T(8,128)S(1)} %get-tuple-element.34.fwd_ref, f32[2048,128]{1,0:T(8,128)S(1)} %shard_map.87.bwd_hbm, f32[256,128]{1,0:T(8,128)S(1)} %get-tuple-element.29.dec_ref, ...), custom_call_target="tpu_custom_call" | custom-call | flops 16777216 | bytes 3670016 | tf_op jit(solution)/shard_map/pallas_call | solution.py:443
  58.8 0.0 collective-permute-done.1
  58.8 0.7 %convert_dynamic-update-slice_fusion = f32[16,4096]{1,0:T(8,128)} fusion(f32[16,4096]{1,0:T(8,128)} %get-tuple-element.39, s32[]{:T(128)S(6)} %select_n.3, bf16[16,2048]{1,0:T(8,128)(2,1)S(1)} %collective-permute-done.1), kind=kLoop, calls=%fused_computation | loop fusion | flops 32768 | bytes 196612 | tf_op jit(solution)/shard_map/dynamic_update_slice | solution.py:454
Async XLA Ops:
  0.6 19.2 %copy-start.1 = (bf16[2048,128]{1,0:T(8,128)(2,1)S(1)}, bf16[2048,128]{1,0:T(8,128)(2,1)}, u32[]{:S(2)}) copy-start(bf16[2048,128]{1,0:T(8,128)(2,1)} %gated_ref) | copy-start | bytes 1572868
  0.6 19.2 %copy-start.4 = (f32[4096,16]{0,1:T(8,128)S(1)}, f32[4096,16]{0,1:T(8,128)}, u32[]{:S(2)}) copy-start(f32[4096,16]{0,1:T(8,128)} %param.9) | copy-start | bytes 786436
  6.0 13.9 %copy-start.2 = (f32[4096,16]{0,1:T(8,128)S(1)}, f32[4096,16]{0,1:T(8,128)}, u32[]{:S(2)}) copy-start(f32[4096,16]{0,1:T(8,128)} %param.10) | copy-start | bytes 786436
  6.0 13.9 %copy-start.5 = (f32[4096]{0:T(1024)S(1)}, f32[4096]{0:T(1024)}, u32[]{:S(2)}) copy-start(f32[4096]{0:T(1024)} %param.11) | copy-start | bytes 49156
  6.0 26.9 %all-to-all-start = ((bf16[64,3,4,128]{3,2,1,0:T(4,128)(2,1)}), bf16[64,3,4,128]{3,2,1,0:T(4,128)(2,1)S(1)}, u32[]{:S(2)}, u32[]{:S(2)}) async-start(bf16[64,3,4,128]{3,2,1,0:T(4,128)(2,1)} %bitcast.18), calls=%async_computation | async-start | bytes 393216 | tf_op jit(solution)/shard_map/all_to_all | solution.py:396
  19.9 2.7 %copy-start.3 = (bf16[2048,128]{1,0:T(8,128)(2,1)S(1)}, bf16[2048,128]{1,0:T(8,128)(2,1)}, u32[]{:S(2)}) copy-start(bf16[2048,128]{1,0:T(8,128)(2,1)} %get-tuple-element.28.dz_ref) | copy-start | bytes 1572868
  32.9 21.9 %copy-start = (bf16[2048,128]{1,0:T(8,128)(2,1)S(1)}, bf16[2048,128]{1,0:T(8,128)(2,1)}, u32[]{:S(2)}) copy-start(bf16[2048,128]{1,0:T(8,128)(2,1)} %upstream_hbm.3) | copy-start | bytes 1572868
  32.9 1.4 %collective-permute-start = (bf16[768,128]{1,0:T(8,128)(2,1)S(1)}, bf16[768,128]{1,0:T(8,128)(2,1)S(1)}, u32[]{:S(2)}, u32[]{:S(2)}) collective-permute-start(bf16[768,128]{1,0:T(8,128)(2,1)S(1)} %bitcast.12), channel_id=1, source_target_pairs={{0,2},{2,0},{4,6},{6,4},{8,10},{10,8},{12,14},{14,12},{16,18},{18,... | collective-permute-start | bytes 589832 | tf_op jit(solution)/shard_map/ppermute | solution.py:421
  53.4 5.4 %collective-permute-start.1 = (bf16[16,2048]{1,0:T(8,128)(2,1)S(1)}, bf16[16,2048]{1,0:T(8,128)(2,1)S(1)}, u32[]{:S(2)}, u32[]{:S(2)}) collective-permute-start(bf16[16,2048]{1,0:T(8,128)(2,1)S(1)} %get-tuple-element.40), channel_id=1, source_target_pairs={{0,1},{1,0},{2,3},{3,2},{4,5},{5,4},{6,7},{7,6},{8,9},{9,8},{10,11... | collective-permute-start | bytes 196616 | tf_op jit(solution)/shard_map/ppermute | solution.py:442

commit v7 on v6

--- a/solution.py
+++ b/solution.py
@@ -189,6 +189,11 @@
     return jnp.concatenate(parts, axis=0)
 
 
+def place_of(chip):
+    z = chip % RUN_OF_CHIPS
+    return (z % 4 * 2 + z // 4) * RUN_OF_CHIPS + chip // RUN_OF_CHIPS
+
+
 def ahead_kernel(
     modes, blocks, tokens, gated_ref, rate_ref, res_ref, skip_ref,
     fwd_ref, dec_ref, gain_ref, lam_ref, gt
@@ -199,7 +204,7 @@
     for h in range(2):
         for g in range(blocks // GROUP):
             chip = lax.axis_index("seq") // 2
-            row = g * modes * GROUP + (chip % RUN_OF_CHIPS * RUN_OF_CHIPS + chip // RUN_OF_CHIPS) * 2 + h
+            row = g * modes * GROUP + place_of(chip) * 2 + h
             own = dec_ref[pl.ds(row, 1), :]
             lam_ref[pl.ds(2 * h + g, 1), :] = own
     dec_ref[...] = jnp.exp(-dec_ref[...])
@@ -235,7 +240,8 @@
     def body(i, carry):
         x, y, own, cross = carry
         for u in range(RUN_OF_CHIPS):
-            q, r = u * RUN_OF_CHIPS + i, chips - 1 - u * RUN_OF_CHIPS - i
+            q = place_of(u) + i
+            r = place_of(RUN_OF_CHIPS - 1 - u) + RUN_OF_CHIPS - 1 - i
             for place in range(2):
                 outs[place, at(q, 0), :] = x
                 outs[1 - place, at(r, 1), :] = y
@@ -388,11 +394,8 @@
 
     def exchange(array):
         array = array.reshape(chunks // 2, KINDS, 4, LANES)
-        run = range(RUN_OF_CHIPS)
-        members = [
-            [2 * (late * RUN_OF_CHIPS + early) + core for early in run for late in run]
-            for core in range(2)
-        ]
+        by_place = sorted(range(chunks // 2), key=place_of)
+        members = [[2 * chip + core for chip in by_place] for core in range(2)]
         return lax.all_to_all(
             array, "seq", split_axis=0, concat_axis=0, axis_index_groups=members, tiled=True
         ).reshape(wire)

time: 59.7 us -> 58.9 us (0.987)
  the two profiles are of different devices: /device:TPU:8 before, /device:TPU:1 now
where the time goes in v7:
time: 58.9 us; the launch traced here: 57.7 us
  starting transfers between devices  18.2 us (31%)
  blocking collectives  16.3 us (28%)
  Pallas kernels  15.3 us (26%)
  waiting for transfers between devices  6.39 us (11%)
  between operations  0.76 us (1%)
  other arithmetic  0.67 us (1%)
    all_to_all x1, blocking collectives, exchange(): lax.all_to_all(array, 'seq', split_axis=0, concat_axis=0, axis_index_grou...  16.3 us
    all_to_all x1, starting transfers between devices, exchange(): lax.all_to_all(array, 'seq', split_axis=0, concat_axis=0, axis_index_grou...  15.3 us
    pallas_call x1, Pallas kernels, local(): call(functools.partial(state_kernel, modes, blocks, tokens), [hbm] * 4, [...  5.33 us
    all_to_all x1, waiting for transfers between devices, exchange(): lax.all_to_all(array, 'seq', split_axis=0, concat_axis=0, axis_index_grou...  5.31 us
    pallas_call x1, Pallas kernels, local(): call(functools.partial(final_kernel, modes, blocks, tokens), [vmem, vmem,...  3.94 us
    pallas_call x1, Pallas kernels, local(): call(functools.partial(behind_kernel, modes, blocks, tokens), [vmem] * 4,...  2.82 us
    pallas_call x1, Pallas kernels, local(): call(functools.partial(ahead_kernel, modes, blocks, tokens), [vmem] * 4,...  2.7 us
    ppermute x1, starting transfers between devices, local(): lax.ppermute(heard, 'seq', [(d, d ^ 1) for d in range(chunks)])  2.47 us
  transfers between devices with their start and end apart: 3, of which 2 were waited for; matrix products, arithmetic and copies ran while one was open for 0% of the time, Pallas kernels for 16%

profile of v7, /device:TPU:1, one launch (start us, length us, event | category | flops | bytes accessed | tf_op | source)
XLA Modules:
  0.0 57.7 jit_solution(8097571858174494911)
XLA Ops:
  0.6 0.0 copy-start.1
  0.6 0.0 copy-start.4
  0.7 5.3 %shard_map.85 = (bf16[768,128]{1,0:T(8,128)(2,1)}, bf16[2048,128]{1,0:T(8,128)(2,1)}) custom-call(bf16[2048,128]{1,0:T(8,128)(2,1)} %gated_ref, bf16[2048,128]{1,0:T(8,128)(2,1)} %value_hbm.1, bf16[2048,128]{1,0:T(8,128)(2,1)} %upstream_hbm.3, f32[16,4096]{1,0:T(8,128)} %bitcast.10), custom_call_target="tpu_custom_call" | custom-call | flops 20971520 | bytes 2097152 | tf_op jit(solution)/shard_map/pallas_call | solution.py:382
  6.0 0.0 copy-start.2
  6.0 0.0 copy-start.5
  6.0 15.3 %all-to-all-start = ((bf16[64,3,4,128]{3,2,1,0:T(4,128)(2,1)}), bf16[64,3,4,128]{3,2,1,0:T(4,128)(2,1)S(1)}, u32[]{:S(2)}, u32[]{:S(2)}) async-start(bf16[64,3,4,128]{3,2,1,0:T(4,128)(2,1)} %bitcast.18), calls=%async_computation | async-start | bytes 393216 | tf_op jit(solution)/shard_map/all_to_all | solution.py:399
  21.3 0.0 copy-done.1
  21.3 0.0 copy-done.4
  21.3 0.0 copy-done.2
  21.3 0.0 copy-done.5
  21.3 0.0 copy-start.3
  21.3 2.7 %shard_map.86 = (f32[2048,128]{1,0:T(8,128)S(1)}, f32[256,128]{1,0:T(8,128)S(1)}, f32[256,128]{1,0:T(8,128)S(1)}, f32[4,128]{1,0:T(4,128)S(1)}) custom-call(bf16[2048,128]{1,0:T(8,128)(2,1)S(1)} %copy-done.1, f32[16,4096]{1,0:T(8,128)S(1)} %bitcast.11, f32[16,4096]{1,0:T(8,128)S(1)} %bitcast.15, f32[1,4096]{1,0:T(1,128)S(1)} %bitcast.16), custom_call_target="tpu_custom_call" | custom-call | flops 16777216 | bytes 1572864 | tf_op jit(solution)/shard_map/pallas_call | solution.py:404
  24.0 0.0 copy-done.3
  24.0 2.8 %shard_map.87.bwd_hbm = f32[2048,128]{1,0:T(8,128)S(1)} custom-call(bf16[2048,128]{1,0:T(8,128)(2,1)S(1)} %copy-done.3, f32[256,128]{1,0:T(8,128)S(1)} %get-tuple-element.29.dec_ref, f32[256,128]{1,0:T(8,128)S(1)} %get-tuple-element.30.gain_ref, f32[1,4096]{1,0:T(1,128)S(1)} %bitcast.17), custom_call_target="tpu_custom_call" | custom-call | flops 16777216 | bytes 1572864 | tf_op jit(solution)/shard_map/pallas_call | solution.py:414
  26.9 5.3 %all-to-all-done = bf16[64,3,4,128]{3,2,1,0:T(4,128)(2,1)S(1)} async-done(((bf16[64,3,4,128]{3,2,1,0:T(4,128)(2,1)}), bf16[64,3,4,128]{3,2,1,0:T(4,128)(2,1)S(1)}, u32[]{:S(2)}, u32[]{:S(2)}) %all-to-all-start) | async-done | bytes 196640 | tf_op jit(solution)/shard_map/all_to_all | solution.py:399
  32.2 0.0 copy-start
  32.2 2.5 %collective-permute-start = (bf16[768,128]{1,0:T(8,128)(2,1)S(1)}, bf16[768,128]{1,0:T(8,128)(2,1)S(1)}, u32[]{:S(2)}, u32[]{:S(2)}) collective-permute-start(bf16[768,128]{1,0:T(8,128)(2,1)S(1)} %bitcast.12), channel_id=1, source_target_pairs={{0,2},{2,0},{4,6},{6,4},{8,10},{10,8},{12,14},{14,12},{16,18},{18,... | collective-permute-start | bytes 589832 | tf_op jit(solution)/shard_map/ppermute | solution.py:424
  34.7 1.1 %collective-permute-done.other_ref = bf16[768,128]{1,0:T(8,128)(2,1)S(1)} collective-permute-done((bf16[768,128]{1,0:T(8,128)(2,1)S(1)}, bf16[768,128]{1,0:T(8,128)(2,1)S(1)}, u32[]{:S(2)}, u32[]{:S(2)}) %collective-permute-start) | collective-permute-done | bytes 196640 | tf_op jit(solution)/shard_map/ppermute | solution.py:424
  35.7 0.4 shard_map.88
  36.2 16.3 %all_to_all.10 = bf16[64,3,4,128]{3,2,1,0:T(4,128)(2,1)S(1)} all-to-all(bf16[64,3,4,128]{3,2,1,0:T(4,128)(2,1)S(1)} %bitcast.14), channel_id=1, replica_groups={{0,32,64,96,128,160,192,224,16,48,80,112,144,176,208,240,4,36,68,100,13..., dimensions={0} | all-to-all | bytes 393216 | tf_op jit(solution)/shard_map/all_to_all | solution.py:399
  52.5 0.1 shard_map.89
  52.6 0.5 collective-permute-start.1
  53.1 0.0 copy-done
  53.1 3.9 %shard_map.90 = (bf16[2048,128]{1,0:T(8,128)(2,1)}, bf16[2048,128]{1,0:T(8,128)(2,1)}, f32[16,4096]{1,0:T(8,128)}) custom-call(bf16[768,128]{1,0:T(8,128)(2,1)S(1)} %bitcast.9, f32[2048,128]{1,0:T(8,128)S(1)} %get-tuple-element.34.fwd_ref, f32[2048,128]{1,0:T(8,128)S(1)} %shard_map.87.bwd_hbm, f32[256,128]{1,0:T(8,128)S(1)} %get-tuple-element.29.dec_ref, ...), custom_call_target="tpu_custom_call" | custom-call | flops 16777216 | bytes 3670016 | tf_op jit(solution)/shard_map/pallas_call | solution.py:446
  57.0 0.0 collective-permute-done.1
  57.1 0.7 %convert_dynamic-update-slice_fusion = f32[16,4096]{1,0:T(8,128)} fusion(f32[16,4096]{1,0:T(8,128)} %get-tuple-element.39, s32[]{:T(128)S(6)} %select_n.3, bf16[16,2048]{1,0:T(8,128)(2,1)S(1)} %collective-permute-done.1), kind=kLoop, calls=%fused_computation | loop fusion | flops 32768 | bytes 196612 | tf_op jit(solution)/shard_map/dynamic_update_slice | solution.py:457
Async XLA Ops:
  0.6 20.7 %copy-start.1 = (bf16[2048,128]{1,0:T(8,128)(2,1)S(1)}, bf16[2048,128]{1,0:T(8,128)(2,1)}, u32[]{:S(2)}) copy-start(bf16[2048,128]{1,0:T(8,128)(2,1)} %gated_ref) | copy-start | bytes 1572868
  0.6 20.7 %copy-start.4 = (f32[4096,16]{0,1:T(8,128)S(1)}, f32[4096,16]{0,1:T(8,128)}, u32[]{:S(2)}) copy-start(f32[4096,16]{0,1:T(8,128)} %param.9) | copy-start | bytes 786436
  6.0 15.3 %copy-start.2 = (f32[4096,16]{0,1:T(8,128)S(1)}, f32[4096,16]{0,1:T(8,128)}, u32[]{:S(2)}) copy-start(f32[4096,16]{0,1:T(8,128)} %param.10) | copy-start | bytes 786436
  6.0 15.3 %copy-start.5 = (f32[4096]{0:T(1024)S(1)}, f32[4096]{0:T(1024)}, u32[]{:S(2)}) copy-start(f32[4096]{0:T(1024)} %param.11) | copy-start | bytes 49156
  6.0 26.2 %all-to-all-start = ((bf16[64,3,4,128]{3,2,1,0:T(4,128)(2,1)}), bf16[64,3,4,128]{3,2,1,0:T(4,128)(2,1)S(1)}, u32[]{:S(2)}, u32[]{:S(2)}) async-start(bf16[64,3,4,128]{3,2,1,0:T(4,128)(2,1)} %bitcast.18), calls=%async_computation | async-start | bytes 393216 | tf_op jit(solution)/shard_map/all_to_all | solution.py:399
  21.3 2.7 %copy-start.3 = (bf16[2048,128]{1,0:T(8,128)(2,1)S(1)}, bf16[2048,128]{1,0:T(8,128)(2,1)}, u32[]{:S(2)}) copy-start(bf16[2048,128]{1,0:T(8,128)(2,1)} %get-tuple-element.28.dz_ref) | copy-start | bytes 1572868
  32.2 20.9 %copy-start = (bf16[2048,128]{1,0:T(8,128)(2,1)S(1)}, bf16[2048,128]{1,0:T(8,128)(2,1)}, u32[]{:S(2)}) copy-start(bf16[2048,128]{1,0:T(8,128)(2,1)} %upstream_hbm.3) | copy-start | bytes 1572868
  32.2 3.5 %collective-permute-start = (bf16[768,128]{1,0:T(8,128)(2,1)S(1)}, bf16[768,128]{1,0:T(8,128)(2,1)S(1)}, u32[]{:S(2)}, u32[]{:S(2)}) collective-permute-start(bf16[768,128]{1,0:T(8,128)(2,1)S(1)} %bitcast.12), channel_id=1, source_target_pairs={{0,2},{2,0},{4,6},{6,4},{8,10},{10,8},{12,14},{14,12},{16,18},{18,... | collective-permute-start | bytes 589832 | tf_op jit(solution)/shard_map/ppermute | solution.py:424
  52.6 4.4 %collective-permute-start.1 = (bf16[16,2048]{1,0:T(8,128)(2,1)S(1)}, bf16[16,2048]{1,0:T(8,128)(2,1)S(1)}, u32[]{:S(2)}, u32[]{:S(2)}) collective-permute-start(bf16[16,2048]{1,0:T(8,128)(2,1)S(1)} %get-tuple-element.40), channel_id=1, source_target_pairs={{0,1},{1,0},{2,3},{3,2},{4,5},{5,4},{6,7},{7,6},{8,9},{9,8},{10,11... | collective-permute-start | bytes 196616 | tf_op jit(solution)/shard_map/ppermute | solution.py:445

commit v8 on v7

--- a/solution.py
+++ b/solution.py
@@ -15,7 +15,7 @@
 PART, UNROLL = 8, 16
 FINAL_UNROLL = 16
 RUN_OF_CHIPS = 8
-STATE_PART, STATE_UNROLL, RUN = 4, 32, 4
+STATE_PART, STATE_UNROLL, RUN = 4, 64, 4
 LIMIT = 56 * 2**20
 
 
@@ -338,8 +338,10 @@
             rows = pl.ds(g * half + j * LANES, LANES)
             back = transposed(gts[g][pl.ds(j, tokens, stride=GROUP), :].astype(BF16))
             grad_gated_ref[rows, :] = back.astype(BF16)
-            if j % 4 == 3:
-                send(grad_gated_ref, grad_gated_hbm, g * GROUP + j - 3, 4)
+            if j == 3:
+                send(grad_gated_ref, grad_gated_hbm, g * GROUP, 4)
+            elif j in (5, 7):
+                send(grad_gated_ref, grad_gated_hbm, g * GROUP + j - 1, 2)
     for copy in copies + [residue_copy]:
         copy.wait()
 
@@ -449,7 +451,7 @@
         [hbm] * 3,
         [native, native, ((modes, residue.shape[0]), F32)],
         [unpacked, [one] * groups, [one] * groups, pltpu.VMEM(*signal), raw, raw, raw]
-        + [sems(groups + 2), sems(3 * groups)],
+        + [sems(groups + 2), sems(4 * groups)],
         4 * cells,
         14 * channels * tokens,
     )(returned, fwd, bwd, decay, gain, upstream, grad_own)

time: 58.9 us -> 58.8 us (level)
  no operation moved by 1% of the time
where the time goes in v8:
time: 58.8 us; the launch traced here: 57.7 us
  starting transfers between devices  18.2 us (31%)
  blocking collectives  16.3 us (28%)
  Pallas kernels  15.3 us (26%)
  waiting for transfers between devices  6.39 us (11%)
  between operations  0.76 us (1%)
  other arithmetic  0.67 us (1%)
    all_to_all x1, blocking collectives, exchange(): lax.all_to_all(array, 'seq', split_axis=0, concat_axis=0, axis_index_grou...  16.3 us
    all_to_all x1, starting transfers between devices, exchange(): lax.all_to_all(array, 'seq', split_axis=0, concat_axis=0, axis_index_grou...  15.3 us
    all_to_all x1, waiting for transfers between devices, exchange(): lax.all_to_all(array, 'seq', split_axis=0, concat_axis=0, axis_index_grou...  5.31 us
    pallas_call x1, Pallas kernels, local(): call(functools.partial(state_kernel, modes, blocks, tokens), [hbm] * 4, [...  5.26 us
    pallas_call x1, Pallas kernels, local(): call(functools.partial(final_kernel, modes, blocks, tokens), [vmem, vmem,...  3.96 us
    pallas_call x1, Pallas kernels, local(): call(functools.partial(behind_kernel, modes, blocks, tokens), [vmem] * 4,...  2.82 us
    pallas_call x1, Pallas kernels, local(): call(functools.partial(ahead_kernel, modes, blocks, tokens), [vmem] * 4,...  2.7 us
    ppermute x1, starting transfers between devices, local(): lax.ppermute(heard, 'seq', [(d, d ^ 1) for d in range(chunks)])  2.47 us
  transfers between devices with their start and end apart: 3, of which 2 were waited for; matrix products, arithmetic and copies ran while one was open for 0% of the time, Pallas kernels for 16%

profile of v8, /device:TPU:1, one launch (start us, length us, event | category | flops | bytes accessed | tf_op | source)
XLA Modules:
  0.0 57.7 jit_solution(4543773265710442166)
XLA Ops:
  0.6 0.0 copy-start.1
  0.6 0.0 copy-start.4
  0.7 5.3 %shard_map.85 = (bf16[768,128]{1,0:T(8,128)(2,1)}, bf16[2048,128]{1,0:T(8,128)(2,1)}) custom-call(bf16[2048,128]{1,0:T(8,128)(2,1)} %gated_ref, bf16[2048,128]{1,0:T(8,128)(2,1)} %value_hbm.1, bf16[2048,128]{1,0:T(8,128)(2,1)} %upstream_hbm.3, f32[16,4096]{1,0:T(8,128)} %bitcast.10), custom_call_target="tpu_custom_call" | custom-call | flops 20971520 | bytes 2097152 | tf_op jit(solution)/shard_map/pallas_call | solution.py:384
  5.9 0.0 copy-start.2
  5.9 0.0 copy-start.5
  5.9 15.3 %all-to-all-start = ((bf16[64,3,4,128]{3,2,1,0:T(4,128)(2,1)}), bf16[64,3,4,128]{3,2,1,0:T(4,128)(2,1)S(1)}, u32[]{:S(2)}, u32[]{:S(2)}) async-start(bf16[64,3,4,128]{3,2,1,0:T(4,128)(2,1)} %bitcast.18), calls=%async_computation | async-start | bytes 393216 | tf_op jit(solution)/shard_map/all_to_all | solution.py:401
  21.2 0.0 copy-done.1
  21.2 0.0 copy-done.4
  21.2 0.0 copy-done.2
  21.2 0.0 copy-done.5
  21.3 0.0 copy-start.3
  21.3 2.7 %shard_map.86 = (f32[2048,128]{1,0:T(8,128)S(1)}, f32[256,128]{1,0:T(8,128)S(1)}, f32[256,128]{1,0:T(8,128)S(1)}, f32[4,128]{1,0:T(4,128)S(1)}) custom-call(bf16[2048,128]{1,0:T(8,128)(2,1)S(1)} %copy-done.1, f32[16,4096]{1,0:T(8,128)S(1)} %bitcast.11, f32[16,4096]{1,0:T(8,128)S(1)} %bitcast.15, f32[1,4096]{1,0:T(1,128)S(1)} %bitcast.16), custom_call_target="tpu_custom_call" | custom-call | flops 16777216 | bytes 1572864 | tf_op jit(solution)/shard_map/pallas_call | solution.py:406
  24.0 0.0 copy-done.3
  24.0 2.8 %shard_map.87.bwd_hbm = f32[2048,128]{1,0:T(8,128)S(1)} custom-call(bf16[2048,128]{1,0:T(8,128)(2,1)S(1)} %copy-done.3, f32[256,128]{1,0:T(8,128)S(1)} %get-tuple-element.29.dec_ref, f32[256,128]{1,0:T(8,128)S(1)} %get-tuple-element.30.gain_ref, f32[1,4096]{1,0:T(1,128)S(1)} %bitcast.17), custom_call_target="tpu_custom_call" | custom-call | flops 16777216 | bytes 1572864 | tf_op jit(solution)/shard_map/pallas_call | solution.py:416
  26.8 5.3 %all-to-all-done = bf16[64,3,4,128]{3,2,1,0:T(4,128)(2,1)S(1)} async-done(((bf16[64,3,4,128]{3,2,1,0:T(4,128)(2,1)}), bf16[64,3,4,128]{3,2,1,0:T(4,128)(2,1)S(1)}, u32[]{:S(2)}, u32[]{:S(2)}) %all-to-all-start) | async-done | bytes 196640 | tf_op jit(solution)/shard_map/all_to_all | solution.py:401
  32.1 0.0 copy-start
  32.1 2.5 %collective-permute-start = (bf16[768,128]{1,0:T(8,128)(2,1)S(1)}, bf16[768,128]{1,0:T(8,128)(2,1)S(1)}, u32[]{:S(2)}, u32[]{:S(2)}) collective-permute-start(bf16[768,128]{1,0:T(8,128)(2,1)S(1)} %bitcast.12), channel_id=1, source_target_pairs={{0,2},{2,0},{4,6},{6,4},{8,10},{10,8},{12,14},{14,12},{16,18},{18,... | collective-permute-start | bytes 589832 | tf_op jit(solution)/shard_map/ppermute | solution.py:426
  34.6 1.1 %collective-permute-done.other_ref = bf16[768,128]{1,0:T(8,128)(2,1)S(1)} collective-permute-done((bf16[768,128]{1,0:T(8,128)(2,1)S(1)}, bf16[768,128]{1,0:T(8,128)(2,1)S(1)}, u32[]{:S(2)}, u32[]{:S(2)}) %collective-permute-start) | collective-permute-done | bytes 196640 | tf_op jit(solution)/shard_map/ppermute | solution.py:426
  35.7 0.4 shard_map.88
  36.1 16.3 %all_to_all.10 = bf16[64,3,4,128]{3,2,1,0:T(4,128)(2,1)S(1)} all-to-all(bf16[64,3,4,128]{3,2,1,0:T(4,128)(2,1)S(1)} %bitcast.14), channel_id=1, replica_groups={{0,32,64,96,128,160,192,224,16,48,80,112,144,176,208,240,4,36,68,100,13..., dimensions={0} | all-to-all | bytes 393216 | tf_op jit(solution)/shard_map/all_to_all | solution.py:401
  52.5 0.1 shard_map.89
  52.5 0.5 collective-permute-start.1
  53.0 0.0 copy-done
  53.0 4.0 %shard_map.90 = (bf16[2048,128]{1,0:T(8,128)(2,1)}, bf16[2048,128]{1,0:T(8,128)(2,1)}, f32[16,4096]{1,0:T(8,128)}) custom-call(bf16[768,128]{1,0:T(8,128)(2,1)S(1)} %bitcast.9, f32[2048,128]{1,0:T(8,128)S(1)} %get-tuple-element.34.fwd_ref, f32[2048,128]{1,0:T(8,128)S(1)} %shard_map.87.bwd_hbm, f32[256,128]{1,0:T(8,128)S(1)} %get-tuple-element.29.dec_ref, ...), custom_call_target="tpu_custom_call" | custom-call | flops 16777216 | bytes 3670016 | tf_op jit(solution)/shard_map/pallas_call | solution.py:448
  57.0 0.0 collective-permute-done.1
  57.0 0.7 %convert_dynamic-update-slice_fusion = f32[16,4096]{1,0:T(8,128)} fusion(f32[16,4096]{1,0:T(8,128)} %get-tuple-element.39, s32[]{:T(128)S(6)} %select_n.3, bf16[16,2048]{1,0:T(8,128)(2,1)S(1)} %collective-permute-done.1), kind=kLoop, calls=%fused_computation | loop fusion | flops 32768 | bytes 196612 | tf_op jit(solution)/shard_map/dynamic_update_slice | solution.py:459
Async XLA Ops:
  0.6 20.6 %copy-start.1 = (bf16[2048,128]{1,0:T(8,128)(2,1)S(1)}, bf16[2048,128]{1,0:T(8,128)(2,1)}, u32[]{:S(2)}) copy-start(bf16[2048,128]{1,0:T(8,128)(2,1)} %gated_ref) | copy-start | bytes 1572868
  0.6 20.6 %copy-start.4 = (f32[4096,16]{0,1:T(8,128)S(1)}, f32[4096,16]{0,1:T(8,128)}, u32[]{:S(2)}) copy-start(f32[4096,16]{0,1:T(8,128)} %param.9) | copy-start | bytes 786436
  5.9 15.3 %copy-start.2 = (f32[4096,16]{0,1:T(8,128)S(1)}, f32[4096,16]{0,1:T(8,128)}, u32[]{:S(2)}) copy-start(f32[4096,16]{0,1:T(8,128)} %param.10) | copy-start | bytes 786436
  5.9 15.3 %copy-start.5 = (f32[4096]{0:T(1024)S(1)}, f32[4096]{0:T(1024)}, u32[]{:S(2)}) copy-start(f32[4096]{0:T(1024)} %param.11) | copy-start | bytes 49156
  5.9 26.2 %all-to-all-start = ((bf16[64,3,4,128]{3,2,1,0:T(4,128)(2,1)}), bf16[64,3,4,128]{3,2,1,0:T(4,128)(2,1)S(1)}, u32[]{:S(2)}, u32[]{:S(2)}) async-start(bf16[64,3,4,128]{3,2,1,0:T(4,128)(2,1)} %bitcast.18), calls=%async_computation | async-start | bytes 393216 | tf_op jit(solution)/shard_map/all_to_all | solution.py:401
  21.3 2.7 %copy-start.3 = (bf16[2048,128]{1,0:T(8,128)(2,1)S(1)}, bf16[2048,128]{1,0:T(8,128)(2,1)}, u32[]{:S(2)}) copy-start(bf16[2048,128]{1,0:T(8,128)(2,1)} %get-tuple-element.28.dz_ref) | copy-start | bytes 1572868
  32.1 20.9 %copy-start = (bf16[2048,128]{1,0:T(8,128)(2,1)S(1)}, bf16[2048,128]{1,0:T(8,128)(2,1)}, u32[]{:S(2)}) copy-start(bf16[2048,128]{1,0:T(8,128)(2,1)} %upstream_hbm.3) | copy-start | bytes 1572868
  32.1 3.5 %collective-permute-start = (bf16[768,128]{1,0:T(8,128)(2,1)S(1)}, bf16[768,128]{1,0:T(8,128)(2,1)S(1)}, u32[]{:S(2)}, u32[]{:S(2)}) collective-permute-start(bf16[768,128]{1,0:T(8,128)(2,1)S(1)} %bitcast.12), channel_id=1, source_target_pairs={{0,2},{2,0},{4,6},{6,4},{8,10},{10,8},{12,14},{14,12},{16,18},{18,... | collective-permute-start | bytes 589832 | tf_op jit(solution)/shard_map/ppermute | solution.py:426
  52.5 4.5 %collective-permute-start.1 = (bf16[16,2048]{1,0:T(8,128)(2,1)S(1)}, bf16[16,2048]{1,0:T(8,128)(2,1)S(1)}, u32[]{:S(2)}, u32[]{:S(2)}) collective-permute-start(bf16[16,2048]{1,0:T(8,128)(2,1)S(1)} %get-tuple-element.40), channel_id=1, source_target_pairs={{0,1},{1,0},{2,3},{3,2},{4,5},{5,4},{6,7},{7,6},{8,9},{9,8},{10,11... | collective-permute-start | bytes 196616 | tf_op jit(solution)/shard_map/ppermute | solution.py:447

commit v9 on v8

--- a/solution.py
+++ b/solution.py
@@ -191,7 +191,7 @@
 
 def place_of(chip):
     z = chip % RUN_OF_CHIPS
-    return (z % 4 * 2 + z // 4) * RUN_OF_CHIPS + chip // RUN_OF_CHIPS
+    return ((8 - z) % 4 * 2 + z // 4) * RUN_OF_CHIPS + chip // RUN_OF_CHIPS
 
 
 def ahead_kernel(

time: 58.8 us -> 59 us (level)
  no operation moved by 1% of the time
where the time goes in v9:
time: 59 us; the launch traced here: 58 us
  starting transfers between devices  18.3 us (31%)
  blocking collectives  16.2 us (27%)
  Pallas kernels  15.2 us (26%)
  waiting for transfers between devices  6.84 us (12%)
  between operations  0.76 us (1%)
  other arithmetic  0.67 us (1%)
    all_to_all x1, blocking collectives, exchange(): lax.all_to_all(array, 'seq', split_axis=0, concat_axis=0, axis_index_grou...  16.2 us
    all_to_all x1, starting transfers between devices, exchange(): lax.all_to_all(array, 'seq', split_axis=0, concat_axis=0, axis_index_grou...  15.3 us
    all_to_all x1, waiting for transfers between devices, exchange(): lax.all_to_all(array, 'seq', split_axis=0, concat_axis=0, axis_index_grou...  5.77 us
    pallas_call x1, Pallas kernels, local(): call(functools.partial(state_kernel, modes, blocks, tokens), [hbm] * 4, [...  5.26 us
    pallas_call x1, Pallas kernels, local(): call(functools.partial(final_kernel, modes, blocks, tokens), [vmem, vmem,...  3.96 us
    pallas_call x1, Pallas kernels, local(): call(functools.partial(behind_kernel, modes, blocks, tokens), [vmem] * 4,...  2.82 us
    pallas_call x1, Pallas kernels, local(): call(functools.partial(ahead_kernel, modes, blocks, tokens), [vmem] * 4,...  2.7 us
    ppermute x1, starting transfers between devices, local(): lax.ppermute(heard, 'seq', [(d, d ^ 1) for d in range(chunks)])  2.56 us
  transfers between devices with their start and end apart: 3, of which 2 were waited for; matrix products, arithmetic and copies ran while one was open for 0% of the time, Pallas kernels for 16%

profile of v9, /device:TPU:1, one launch (start us, length us, event | category | flops | bytes accessed | tf_op | source)
XLA Modules:
  0.0 58.0 jit_solution(6064201634420416647)
XLA Ops:
  0.6 0.0 copy-start.1
  0.6 0.0 copy-start.4
  0.7 5.3 %shard_map.85 = (bf16[768,128]{1,0:T(8,128)(2,1)}, bf16[2048,128]{1,0:T(8,128)(2,1)}) custom-call(bf16[2048,128]{1,0:T(8,128)(2,1)} %gated_ref, bf16[2048,128]{1,0:T(8,128)(2,1)} %value_hbm.1, bf16[2048,128]{1,0:T(8,128)(2,1)} %upstream_hbm.3, f32[16,4096]{1,0:T(8,128)} %bitcast.10), custom_call_target="tpu_custom_call" | custom-call | flops 20971520 | bytes 2097152 | tf_op jit(solution)/shard_map/pallas_call | solution.py:384
  5.9 0.0 copy-start.2
  5.9 0.0 copy-start.5
  5.9 15.3 %all-to-all-start = ((bf16[64,3,4,128]{3,2,1,0:T(4,128)(2,1)}), bf16[64,3,4,128]{3,2,1,0:T(4,128)(2,1)S(1)}, u32[]{:S(2)}, u32[]{:S(2)}) async-start(bf16[64,3,4,128]{3,2,1,0:T(4,128)(2,1)} %bitcast.18), calls=%async_computation | async-start | bytes 393216 | tf_op jit(solution)/shard_map/all_to_all | solution.py:401
  21.2 0.0 copy-done.1
  21.2 0.0 copy-done.4
  21.2 0.0 copy-done.2
  21.2 0.0 copy-done.5
  21.3 0.0 copy-start.3
  21.3 2.7 %shard_map.86 = (f32[2048,128]{1,0:T(8,128)S(1)}, f32[256,128]{1,0:T(8,128)S(1)}, f32[256,128]{1,0:T(8,128)S(1)}, f32[4,128]{1,0:T(4,128)S(1)}) custom-call(bf16[2048,128]{1,0:T(8,128)(2,1)S(1)} %copy-done.1, f32[16,4096]{1,0:T(8,128)S(1)} %bitcast.11, f32[16,4096]{1,0:T(8,128)S(1)} %bitcast.15, f32[1,4096]{1,0:T(1,128)S(1)} %bitcast.16), custom_call_target="tpu_custom_call" | custom-call | flops 16777216 | bytes 1572864 | tf_op jit(solution)/shard_map/pallas_call | solution.py:406
  24.0 0.0 copy-done.3
  24.0 2.8 %shard_map.87.bwd_hbm = f32[2048,128]{1,0:T(8,128)S(1)} custom-call(bf16[2048,128]{1,0:T(8,128)(2,1)S(1)} %copy-done.3, f32[256,128]{1,0:T(8,128)S(1)} %get-tuple-element.29.dec_ref, f32[256,128]{1,0:T(8,128)S(1)} %get-tuple-element.30.gain_ref, f32[1,4096]{1,0:T(1,128)S(1)} %bitcast.17), custom_call_target="tpu_custom_call" | custom-call | flops 16777216 | bytes 1572864 | tf_op jit(solution)/shard_map/pallas_call | solution.py:416
  26.8 5.8 %all-to-all-done = bf16[64,3,4,128]{3,2,1,0:T(4,128)(2,1)S(1)} async-done(((bf16[64,3,4,128]{3,2,1,0:T(4,128)(2,1)}), bf16[64,3,4,128]{3,2,1,0:T(4,128)(2,1)S(1)}, u32[]{:S(2)}, u32[]{:S(2)}) %all-to-all-start) | async-done | bytes 196640 | tf_op jit(solution)/shard_map/all_to_all | solution.py:401
  32.6 0.0 copy-start
  32.6 2.6 %collective-permute-start = (bf16[768,128]{1,0:T(8,128)(2,1)S(1)}, bf16[768,128]{1,0:T(8,128)(2,1)S(1)}, u32[]{:S(2)}, u32[]{:S(2)}) collective-permute-start(bf16[768,128]{1,0:T(8,128)(2,1)S(1)} %bitcast.12), channel_id=1, source_target_pairs={{0,2},{2,0},{4,6},{6,4},{8,10},{10,8},{12,14},{14,12},{16,18},{18,... | collective-permute-start | bytes 589832 | tf_op jit(solution)/shard_map/ppermute | solution.py:426
  35.1 1.1 %collective-permute-done.other_ref = bf16[768,128]{1,0:T(8,128)(2,1)S(1)} collective-permute-done((bf16[768,128]{1,0:T(8,128)(2,1)S(1)}, bf16[768,128]{1,0:T(8,128)(2,1)S(1)}, u32[]{:S(2)}, u32[]{:S(2)}) %collective-permute-start) | collective-permute-done | bytes 196640 | tf_op jit(solution)/shard_map/ppermute | solution.py:426
  36.2 0.4 shard_map.88
  36.6 16.2 %all_to_all.10 = bf16[64,3,4,128]{3,2,1,0:T(4,128)(2,1)S(1)} all-to-all(bf16[64,3,4,128]{3,2,1,0:T(4,128)(2,1)S(1)} %bitcast.14), channel_id=1, replica_groups={{0,32,64,96,128,160,192,224,16,48,80,112,144,176,208,240,12,44,76,108,1..., dimensions={0} | all-to-all | bytes 393216 | tf_op jit(solution)/shard_map/all_to_all | solution.py:401
  52.8 0.1 shard_map.89
  52.9 0.5 collective-permute-start.1
  53.4 0.0 copy-done
  53.4 4.0 %shard_map.90 = (bf16[2048,128]{1,0:T(8,128)(2,1)}, bf16[2048,128]{1,0:T(8,128)(2,1)}, f32[16,4096]{1,0:T(8,128)}) custom-call(bf16[768,128]{1,0:T(8,128)(2,1)S(1)} %bitcast.9, f32[2048,128]{1,0:T(8,128)S(1)} %get-tuple-element.34.fwd_ref, f32[2048,128]{1,0:T(8,128)S(1)} %shard_map.87.bwd_hbm, f32[256,128]{1,0:T(8,128)S(1)} %get-tuple-element.29.dec_ref, ...), custom_call_target="tpu_custom_call" | custom-call | flops 16777216 | bytes 3670016 | tf_op jit(solution)/shard_map/pallas_call | solution.py:448
  57.4 0.0 collective-permute-done.1
  57.4 0.7 %convert_dynamic-update-slice_fusion = f32[16,4096]{1,0:T(8,128)} fusion(f32[16,4096]{1,0:T(8,128)} %get-tuple-element.39, s32[]{:T(128)S(6)} %select_n.3, bf16[16,2048]{1,0:T(8,128)(2,1)S(1)} %collective-permute-done.1), kind=kLoop, calls=%fused_computation | loop fusion | flops 32768 | bytes 196612 | tf_op jit(solution)/shard_map/dynamic_update_slice | solution.py:459
Async XLA Ops:
  0.6 20.6 %copy-start.1 = (bf16[2048,128]{1,0:T(8,128)(2,1)S(1)}, bf16[2048,128]{1,0:T(8,128)(2,1)}, u32[]{:S(2)}) copy-start(bf16[2048,128]{1,0:T(8,128)(2,1)} %gated_ref) | copy-start | bytes 1572868
  0.6 20.6 %copy-start.4 = (f32[4096,16]{0,1:T(8,128)S(1)}, f32[4096,16]{0,1:T(8,128)}, u32[]{:S(2)}) copy-start(f32[4096,16]{0,1:T(8,128)} %param.9) | copy-start | bytes 786436
  5.9 15.3 %copy-start.2 = (f32[4096,16]{0,1:T(8,128)S(1)}, f32[4096,16]{0,1:T(8,128)}, u32[]{:S(2)}) copy-start(f32[4096,16]{0,1:T(8,128)} %param.10) | copy-start | bytes 786436
  5.9 15.3 %copy-start.5 = (f32[4096]{0:T(1024)S(1)}, f32[4096]{0:T(1024)}, u32[]{:S(2)}) copy-start(f32[4096]{0:T(1024)} %param.11) | copy-start | bytes 49156
  5.9 26.6 %all-to-all-start = ((bf16[64,3,4,128]{3,2,1,0:T(4,128)(2,1)}), bf16[64,3,4,128]{3,2,1,0:T(4,128)(2,1)S(1)}, u32[]{:S(2)}, u32[]{:S(2)}) async-start(bf16[64,3,4,128]{3,2,1,0:T(4,128)(2,1)} %bitcast.18), calls=%async_computation | async-start | bytes 393216 | tf_op jit(solution)/shard_map/all_to_all | solution.py:401
  21.3 2.7 %copy-start.3 = (bf16[2048,128]{1,0:T(8,128)(2,1)S(1)}, bf16[2048,128]{1,0:T(8,128)(2,1)}, u32[]{:S(2)}) copy-start(bf16[2048,128]{1,0:T(8,128)(2,1)} %get-tuple-element.28.dz_ref) | copy-start | bytes 1572868
  32.6 20.8 %copy-start = (bf16[2048,128]{1,0:T(8,128)(2,1)S(1)}, bf16[2048,128]{1,0:T(8,128)(2,1)}, u32[]{:S(2)}) copy-start(bf16[2048,128]{1,0:T(8,128)(2,1)} %upstream_hbm.3) | copy-start | bytes 1572868
  32.6 3.6 %collective-permute-start = (bf16[768,128]{1,0:T(8,128)(2,1)S(1)}, bf16[768,128]{1,0:T(8,128)(2,1)S(1)}, u32[]{:S(2)}, u32[]{:S(2)}) collective-permute-start(bf16[768,128]{1,0:T(8,128)(2,1)S(1)} %bitcast.12), channel_id=1, source_target_pairs={{0,2},{2,0},{4,6},{6,4},{8,10},{10,8},{12,14},{14,12},{16,18},{18,... | collective-permute-start | bytes 589832 | tf_op jit(solution)/shard_map/ppermute | solution.py:426
  52.9 4.5 %collective-permute-start.1 = (bf16[16,2048]{1,0:T(8,128)(2,1)S(1)}, bf16[16,2048]{1,0:T(8,128)(2,1)S(1)}, u32[]{:S(2)}, u32[]{:S(2)}) collective-permute-start(bf16[16,2048]{1,0:T(8,128)(2,1)S(1)} %get-tuple-element.40), channel_id=1, source_target_pairs={{0,1},{1,0},{2,3},{3,2},{4,5},{5,4},{6,7},{7,6},{8,9},{9,8},{10,11... | collective-permute-start | bytes 196616 | tf_op jit(solution)/shard_map/ppermute | solution.py:447
